TPU v7x, 256 devices: a whole 4x4x8 slice. The times are simulated.
256 devices in a mesh: patch: 32 (over y_hi, z, core), tp: 8 (over y_lo, x).
Axes of the slice: x: 4, y: 4 (y_hi: 2, y_lo: 2; y = y_hi * 2 + y_lo), z: 8, core: 2. Of those that a mesh axis runs over, the one named last changes fastest.
Arguments:
- image: bfloat16 [6144, 3072], P('patch'), may hold values from -1.5 to 1.5
- mod_shift: float32 [3072], replicated, may hold values from -3 to 3
- mod_scale: float32 [3072], replicated, may hold values from -3 to 3
- mod_gate: float32 [3072], replicated, may hold values from -6 to 6
- qkv_weight: bfloat16 [3072, 3, 2048], P(None, None, 'tp'), may hold values from -0.109375 to 0.109375
- qkv_bias: float32 [3, 2048], P(None, 'tp'), may hold values from -3 to 3
- q_gain: float32 [128], replicated, may hold values from 1 to 2.5
- k_gain: float32 [128], replicated, may hold values from 1 to 2.5
- stale_kv: bfloat16 [2, 6144, 2048], P(None, 'patch', 'tp'), may hold values from -2.5 to 2.5
- text_kv: bfloat16 [2, 512, 2048], P(None, None, 'tp'), may hold values from -2.5 to 2.5
- out_weight: bfloat16 [2048, 3072], P('tp'), may hold values from -1 to 1
- out_bias: float32 [3072], replicated, may hold values from -3 to 3
Outputs:
- mixed: bfloat16 [6144, 3072], P('patch')
- fresh_kv: bfloat16 [2, 6144, 2048], P(None, 'patch', 'tp')
All inputs are finite; a program needn't handle non-finite values.
Results may differ from a plain program's by a relative error of at most 0.0098.
Values may be sent and summed in bfloat16 or wider, within the bound.
No kernel may reach another device: no remote copies, remote signals or barrier semaphores. Data moves between devices by JAX's collectives and lax.ppermute only.
A program may use at most 128 MiB of HBM per device.

v0:
```python
import math

import jax
import jax.numpy as jnp
from jax import lax
from jax.sharding import PartitionSpec as P


def modulate(image, mod_shift, mod_scale):
    wide = image.astype(jnp.float32)
    average = jnp.mean(wide, -1, keepdims=True)
    centred = wide - average
    spread = jnp.mean(centred * centred, -1, keepdims=True)
    normed = centred * lax.rsqrt(spread + 1e-06)
    return (normed * (1.0 + mod_scale) + mod_shift).astype(jnp.bfloat16)


def head_norm(part, gain):
    tok_rows = part.shape[0]
    per_head = part.reshape(tok_rows, -1, gain.shape[0])
    scaled = per_head * lax.rsqrt(jnp.mean(per_head * per_head, -1, keepdims=True) + 1e-06) * gain
    return scaled.reshape(tok_rows, -1).astype(jnp.bfloat16)


def project(modulated, qkv_weight, qkv_bias, q_gain, k_gain):
    width = qkv_weight.shape[2]
    projected = jnp.dot(
        modulated,
        qkv_weight.reshape(qkv_weight.shape[0], 3 * width),
        preferred_element_type=jnp.float32,
    )
    projected = projected.reshape(-1, 3, width) + qkv_bias
    queries = head_norm(projected[:, 0], q_gain)
    keys = head_norm(projected[:, 1], k_gain)
    values = projected[:, 2].astype(jnp.bfloat16)
    return (queries, keys, values)


def attend(queries, keys, values, keep_mask, head_size):
    query_heads = queries.reshape(queries.shape[0], -1, head_size)
    key_heads = keys.reshape(keys.shape[0], -1, head_size)
    value_heads = values.reshape(values.shape[0], -1, head_size)
    scores = jnp.einsum(
        "thd,rhd->thr", query_heads, key_heads, preferred_element_type=jnp.float32
    ) * (1.0 / math.sqrt(head_size))
    weights = jnp.exp(scores)
    if keep_mask is not None:
        weights = weights * keep_mask
    totals = jnp.sum(weights, -1)
    summed = jnp.einsum(
        "thr,rhd->thd",
        weights.astype(jnp.bfloat16),
        value_heads,
        preferred_element_type=jnp.float32,
    )
    return (summed, totals)


def shards(
    image,
    mod_shift,
    mod_scale,
    mod_gate,
    qkv_weight,
    qkv_bias,
    q_gain,
    k_gain,
    stale_kv,
    text_kv,
    out_weight,
    out_bias,
):
    head_size = q_gain.shape[0]
    tok_rows = image.shape[0]
    modulated = modulate(image, mod_shift, mod_scale)
    queries, keys, values = project(modulated, qkv_weight, qkv_bias, q_gain, k_gain)
    fresh_kv = jnp.stack([keys, values])
    own_start = lax.axis_index("patch") * tok_rows
    text_sum, text_total = attend(queries, text_kv[0], text_kv[1], None, head_size)
    own_sum, own_total = attend(queries, keys, values, None, head_size)
    kv_piece = lax.all_gather(stale_kv, "patch", axis=1, tiled=True)
    positions = jnp.arange(kv_piece.shape[1], dtype=jnp.int32)
    keep_mask = ((positions < own_start) | (positions >= own_start + tok_rows)).astype(jnp.float32)
    part_sum, part_total = attend(queries, kv_piece[0], kv_piece[1], keep_mask, head_size)
    summed = text_sum + own_sum + part_sum
    totals = text_total + own_total + part_total
    attended = (summed / totals[..., None]).reshape(tok_rows, -1).astype(jnp.bfloat16)
    residual = image.astype(jnp.float32)
    partial_terms = jnp.dot(attended, out_weight, preferred_element_type=jnp.float32)
    projection = lax.psum(partial_terms, "tp") + out_bias
    mixed = (residual + mod_gate * projection).astype(jnp.bfloat16)
    return (mixed, fresh_kv)


def solution(mesh):
    placed = (
        P("patch", None),
        P(),
        P(),
        P(),
        P(None, None, "tp"),
        P(None, "tp"),
        P(),
        P(),
        P(None, "patch", "tp"),
        P(None, None, "tp"),
        P("tp", None),
        P(),
    )
    return jax.shard_map(
        shards,
        mesh=mesh,
        in_specs=placed,
        out_specs=(P("patch", None), P(None, "patch", "tp")),
        check_vma=False,
    )
```

profile of v0, /device:TPU:32, one launch (start us, length us, event | category | flops | bytes accessed | tf_op | source)
XLA Modules:
  0.0 253.5 jit_solution(17877434125411675517)
XLA Ops:
  7.2 1.9 copy.80
  9.2 6.8 %copy.68 = bf16[3072,3,256]{0,2,1:T(8,128)(2,1)} copy(bf16[3072,3,256]{2,0,1:T(8,128)(2,1)} %param.16) | data formatting | bytes 9437184 | tf_op args[4]
  16.1 0.2 convert_reduce_fusion
  16.3 0.5 fusion.5
  16.8 4.1 %fusion.12 = f32[192,3,256]{2,0,1:T(8,128)S(1)} fusion(bf16[3072,3,256]{0,2,1:T(8,128)(2,1)} %copy.68, bf16[192,3072]{1,0:T(8,128)(2,1)S(1)} %copy-done.2, f32[3072]{0:T(1024)S(1)} %copy-done.11, f32[3072]{0:T(1024)S(1)} %broadcast_add_fusion, f32[192]{0:T(256)S(1)} %add_rsqrt_fusion.2, f32[192]{0:T(256)S(1)} %broadcast_multiply_fusion, ...), kind=kOutput, calls=%fused_computation.19 | convolution fusion | flops 909656064 | bytes 6517248 | tf_op jit(solution)/shard_map/dot_general | solution.py:27
  21.0 0.7 copy-done.3
  21.8 0.1 reshape_squeeze.20
  21.9 0.3 multiply_reduce_fusion.1
  22.2 0.1 reshape_squeeze.23
  22.4 1.8 fusion.45
  24.2 1.8 copy.92
  26.0 0.9 copy.91
  26.8 0.6 fusion.41
  27.4 0.3 multiply_reduce_fusion
  27.8 0.1 fusion.33
  27.9 0.3 multiply_convert_fusion
  28.2 0.3 fusion.47
  28.4 0.2 convolution_bitcast_fusion.1
  28.7 2.0 fusion.46
  30.7 77.5 %all-gather.2.cloned.1.call-done = bf16[2,6144,256]{2,0,1:T(2,128)(2,1)} async-done(((bf16[2,192,256]{2,0,1:T(2,128)(2,1)}), bf16[2,6144,256]{2,0,1:T(2,128)(2,1)}) %all-gather.2.cloned.1.call-update) | async-done | bytes 6291472 | tf_op jit(solution)/shard_map/all_gather | solution.py:81
  108.1 13.8 %fusion.43 = (bf16[1,6144,256]{2,0,1:T(2,128)(2,1)}, bf16[1,6144,256]{2,0,1:T(2,128)(2,1)}) fusion(bf16[2,6144,256]{2,0,1:T(2,128)(2,1)} %all-gather.2.cloned.1.call-done), kind=kLoop, calls=%fused_computation.65 | loop fusion | bytes 12582912 | tf_op jit(solution)/shard_map/slice | solution.py:84
  121.9 13.5 %copy.94 = bf16[1,6144,256]{1,2,0:T(8,128)(2,1)} copy(bf16[1,6144,256]{2,0,1:T(2,128)(2,1)} %get-tuple-element.3) | data formatting | bytes 6291456
  135.4 13.5 %copy.93 = bf16[1,6144,256]{1,2,0:T(8,128)(2,1)} copy(bf16[1,6144,256]{2,0,1:T(2,128)(2,1)} %get-tuple-element.2) | data formatting | bytes 6291456
  148.9 4.6 %bitcast_reduce_fusion = (f32[192,2]{0,1:T(2,128)S(1)}, bf16[2,192,6144]{2,1,0:T(8,128)(2,1)S(1)}) fusion(f32[6144]{0:T(1024)S(1)} %copy-done.6, bf16[192,2,128]{2,0,1:T(8,128)(2,1)S(1)} %fusion.33, bf16[6144,2,128]{0,2,1:T(8,128)(2,1)} %bitcast.77), kind=kOutput, calls=%fused_computation | convolution fusion | flops 613416576 | bytes 7988736 | tf_op jit(solution)/shard_map/thd,rhd->thr/dot_general | solution.py:43
  153.5 1.4 fusion.26
  154.9 0.3 fusion.28
  155.2 1.9 fusion.35
  157.2 0.9 mul.156
  158.1 1.1 mul.169
  159.3 0.7 pad_maximum_fusion
  160.0 83.6 %all-reduce.2.cloned.1.call-done = f32[192,3072]{1,0:T(8,128)} async-done(((f32[192,3072]{1,0:T(8,128)}), f32[192,3072]{1,0:T(8,128)}) %all-reduce.2.cloned.1.call-update) | async-done | bytes 2359312 | tf_op jit(solution)/shard_map/psum | solution.py:90
  243.6 3.1 %fusion.9 = bf16[192,3072]{1,0:T(8,128)(2,1)} fusion(bf16[192,3072]{1,0:T(8,128)(2,1)S(1)} %copy-done.2, f32[192,3072]{1,0:T(8,128)} %all-reduce.2.cloned.1.call-done, f32[3072]{0:T(1024)S(1)} %copy-done.7, f32[3072]{0:T(1024)} %param.15), kind=kLoop, calls=%fused_computation.15 | loop fusion | flops 2949120 | bytes 4743168 | tf_op jit(solution)/shard_map/convert_element_type | solution.py:91
  (44 shorter events, 0.4 us)
Async XLA Ops:
  7.2 148.1 %copy-start = (bf16[256,3072]{1,0:T(8,128)(2,1)S(1)}, bf16[256,3072]{1,0:T(8,128)(2,1)}, u32[]{:S(2)}) copy-start(bf16[256,3072]{1,0:T(8,128)(2,1)} %param.22) | copy-start | bytes 4718596
  7.2 101.0 %all-gather.2.cloned.1.call-start = ((), (), s32[]{:S(2)}) async-start(), calls=%async_computation | async-start | bytes 6488064 | tf_op jit(solution)/shard_map/all_gather | solution.py:81
  9.2 234.4 %all-reduce.2.cloned.1.call-start = ((), (), s32[]{:S(2)}) async-start(), calls=%async_computation.1 | async-start | bytes 4718592 | tf_op jit(solution)/shard_map/psum | solution.py:90
  9.2 6.8 %copy-start.2 = (bf16[192,3072]{1,0:T(8,128)(2,1)S(1)}, bf16[192,3072]{1,0:T(8,128)(2,1)}, u32[]{:S(2)}) copy-start(bf16[192,3072]{1,0:T(8,128)(2,1)} %param.12) | copy-start | bytes 3538948
  16.0 0.7 copy-start.8
  16.0 0.8 copy-start.11
  16.1 0.8 copy-start.12
  20.9 0.8 copy-start.3
  21.0 6.8 %copy-start.9 = (f32[128]{0:T(128)S(1)}, f32[128]{0:T(128)}, u32[]{:S(2)}) copy-start(f32[128]{0:T(128)} %param.18) | copy-start | bytes 1540
  21.0 6.9 %copy-start.10 = (f32[128]{0:T(128)S(1)}, f32[128]{0:T(128)}, u32[]{:S(2)}) copy-start(f32[128]{0:T(128)} %param.19) | copy-start | bytes 1540
  135.4 13.5 %copy-start.6 = (f32[6144]{0:T(1024)S(1)}, f32[6144]{0:T(1024)}, u32[]{:S(2)}) copy-start(f32[6144]{0:T(1024)} %fusion.41) | copy-start | bytes 73732
  148.9 4.6 %copy-start.1 = (bf16[1,6144,256]{1,2,0:T(8,128)(2,1)S(1)}, bf16[1,6144,256]{1,2,0:T(8,128)(2,1)}, u32[]{:S(2)}) copy-start(bf16[1,6144,256]{1,2,0:T(8,128)(2,1)} %copy.94) | copy-start | bytes 9437188
  153.5 1.4 copy-start.5
  153.5 1.4 copy-start.13
  157.1 2.1 copy-start.4
  157.1 86.5 %copy-start.7 = (f32[3072]{0:T(1024)S(1)}, f32[3072]{0:T(1024)}, u32[]{:S(2)}) copy-start(f32[3072]{0:T(1024)} %param.23) | copy-start | bytes 36868
Sparse Core Ops, SparseCore 0:
  11.4 96.7 all-gather.1
  157.3 86.2 all-reduce.1
where the time goes:
time: 255 us; the launch traced here: 253 us
  waiting for transfers between devices  161 us (63%)
  local copies, waits for them, and re-layouts  57.1 us (22%)
  matrix products  14.7 us (6%)
  between operations  14.3 us (6%)
  other arithmetic  6.07 us (2%)
    psum x1, waiting for transfers between devices, shards(): projection = lax.psum(partial_terms, 'tp') + out_bias  83.6 us
    all_gather x1, waiting for transfers between devices, shards(): kv_piece = lax.all_gather(stale_kv, 'patch', axis=1, tiled=True)  77.5 us
    unnamed x34, local copies, waits for them, and re-layouts  39.2 us
    slice x1, local copies, waits for them, and re-layouts, shards(): kv_piece[0]  13.8 us
    dot_general x3, matrix products, attend(): jnp.einsum('thd,rhd->thr', query_heads, key_heads, preferred_element_type...  6.83 us
  transfers between devices with their start and end apart: 2, of which 2 were waited for; matrix products, arithmetic and copies ran while one was open for 9% of the time, Pallas kernels for 0%

commit v1 on v0

v1 whole, which is shorter than its diff:
```python
import math

import jax
import jax.numpy as jnp
from jax import lax
from jax.experimental import pallas as pl
from jax.experimental.pallas import tpu as pltpu
from jax.sharding import PartitionSpec as P

BF = jnp.bfloat16
F32 = jnp.float32
VMEM = pl.BlockSpec(memory_space=pltpu.VMEM)
LIMIT = 48 * 1024 * 1024


def params(**kw):
    return pltpu.CompilerParams(vmem_limit_bytes=LIMIT, **kw)


def modulate_into(image_ref, shift_ref, scale_ref, out_ref):
    rows = image_ref.shape[0]
    step = 16

    def body(i, carry):
        at = pl.ds(pl.multiple_of(i * step, step), step)
        wide = image_ref[at, :].astype(F32)
        average = jnp.mean(wide, -1, keepdims=True)
        centred = wide - average
        spread = jnp.mean(centred * centred, -1, keepdims=True)
        normed = centred * lax.rsqrt(spread + 1e-06)
        out_ref[at, :] = (normed * (1.0 + scale_ref[...]) + shift_ref[...]).astype(BF)
        return carry

    lax.fori_loop(0, rows // step, body, 0)


def finish_heads(acc, bias_ref, q_gain_ref, k_gain_ref, out_ref):
    hd = q_gain_ref.shape[1]

    def norm(part, gain):
        return part * lax.rsqrt(jnp.mean(part * part, -1, keepdims=True) + 1e-06) * gain

    q = acc[:, :hd] + bias_ref[0:1, :]
    k = acc[:, hd : 2 * hd] + bias_ref[1:2, :]
    v = acc[:, 2 * hd :] + bias_ref[2:3, :]
    out_ref[0] = norm(q, q_gain_ref[...]).astype(BF)
    out_ref[1] = norm(k, k_gain_ref[...]).astype(BF)
    out_ref[2] = v.astype(BF)


def own_kernel(c_ref, image_ref, shift_ref, scale_ref, w_ref, bias_ref, q_gain_ref, k_gain_ref, out_ref, wide_ref, mod_ref, acc_ref):
    k = pl.program_id(0)

    @pl.when(k == 0)
    def _():
        modulate_into(image_ref, shift_ref, scale_ref, mod_ref)
        acc_ref[...] = jnp.zeros_like(acc_ref)

    depth = w_ref.shape[0]
    flat = jnp.concatenate([w_ref[:, j, :] for j in range(3)], axis=1)
    wide_ref[...] = flat
    at = pl.ds(pl.multiple_of(k * depth, depth), depth)
    acc_ref[...] += jnp.dot(mod_ref[:, at], flat, preferred_element_type=F32)

    @pl.when(k == pl.num_programs(0) - 1)
    def _():
        finish_heads(acc_ref[...], bias_ref, q_gain_ref, k_gain_ref, out_ref)


def project_own(core, image, shift, scale, weight, bias, q_gain, k_gain):
    rows, features = image.shape
    hd = q_gain.shape[1]
    depth = features // 8
    whole = lambda shape: pl.BlockSpec(shape, lambda k, c: (0,) * len(shape))
    return pl.pallas_call(
        own_kernel,
        grid_spec=pltpu.PrefetchScalarGridSpec(
            num_scalar_prefetch=1,
            grid=(features // depth,),
            in_specs=[
                whole((rows, features)),
                whole((1, features)),
                whole((1, features)),
                pl.BlockSpec((depth, 3, hd), lambda k, c: (k, 0, c[0])),
                pl.BlockSpec((3, hd), lambda k, c: (0, c[0])),
                whole((1, hd)),
                whole((1, hd)),
            ],
            out_specs=[
                whole((3, rows, hd)),
                pl.BlockSpec((depth, 3 * hd), lambda k, c: (k, 0)),
            ],
            scratch_shapes=[
                pltpu.VMEM((rows, features), BF),
                pltpu.VMEM((rows, 3 * hd), F32),
            ],
        ),
        out_shape=[
            jax.ShapeDtypeStruct((3, rows, hd), BF),
            jax.ShapeDtypeStruct((features, 3 * hd), BF),
        ],
        compiler_params=params(),
        name="project_own",
    )(core, image, shift, scale, weight, bias, q_gain, k_gain)


def other_kernel(c_ref, image_ref, shift_ref, scale_ref, wide_ref, bias_ref, q_gain_ref, k_gain_ref, out_ref, mod_ref):
    modulate_into(image_ref, shift_ref, scale_ref, mod_ref)
    acc = jnp.dot(mod_ref[...], wide_ref[...], preferred_element_type=F32)
    finish_heads(acc, bias_ref, q_gain_ref, k_gain_ref, out_ref)


def project_other(core, image, shift, scale, wide, bias, q_gain, k_gain):
    rows, features = image.shape
    hd = q_gain.shape[1]
    whole = lambda shape: pl.BlockSpec(shape, lambda k, c: (0,) * len(shape))
    return pl.pallas_call(
        other_kernel,
        grid_spec=pltpu.PrefetchScalarGridSpec(
            num_scalar_prefetch=1,
            grid=(1,),
            in_specs=[
                whole((rows, features)),
                whole((1, features)),
                whole((1, features)),
                whole((features, 3 * hd)),
                pl.BlockSpec((3, hd), lambda k, c: (0, c[0])),
                whole((1, hd)),
                whole((1, hd)),
            ],
            out_specs=whole((3, rows, hd)),
            scratch_shapes=[pltpu.VMEM((rows, features), BF)],
        ),
        out_shape=jax.ShapeDtypeStruct((3, rows, hd), BF),
        compiler_params=params(),
        name="project_other",
    )(core, image, shift, scale, wide, bias, q_gain, k_gain)


def block_sums(q, k, v_ref_value):
    hd = q.shape[1]
    scores = lax.dot_general(q, k, (((1,), (1,)), ((), ())), preferred_element_type=F32)
    weights = jnp.exp2(scores * (math.log2(math.e) / math.sqrt(hd))).astype(BF)
    ones = jnp.ones_like(v_ref_value)
    return jnp.dot(weights, jnp.concatenate([v_ref_value, ones], 1), preferred_element_type=F32)


def eye(n):
    return (lax.broadcasted_iota(jnp.int32, (n, n), 0) == lax.broadcasted_iota(jnp.int32, (n, n), 1)).astype(F32)


def remote_kernel(q_ref, kv0_ref, kv1_ref, kv2_ref, kv3_ref, out_ref):
    rows, hd = q_ref.shape
    same = eye(hd)
    for i in range(rows // hd):
        at = slice(i * hd, (i + 1) * hd)
        q = q_ref[at, :]
        total = None
        for kv in (kv0_ref, kv1_ref, kv2_ref, kv3_ref):
            part = block_sums(q, kv[0], kv[1])
            total = part if total is None else total + part
        out_ref[at, :] = total[:, :hd].astype(BF)
        line = jnp.sum(total[:, hd:] * same, 0, keepdims=True)
        high = line.astype(BF).astype(F32)
        out_ref[pl.ds(rows + 16 * i, 16), :] = jnp.concatenate(
            [jnp.broadcast_to(high, (8, hd)), jnp.broadcast_to(line - high, (8, hd))], 0
        ).astype(BF)


def attend_remote(q, kvs):
    rows, hd = q.shape
    return pl.pallas_call(
        remote_kernel,
        in_specs=[VMEM] * 5,
        out_specs=VMEM,
        out_shape=jax.ShapeDtypeStruct((rows + 16 * (rows // hd), hd), BF),
        compiler_params=params(),
        name="attend_remote",
    )(q, *kvs)


def local_kernel(own_ref, other_ref, kv0_ref, kv1_ref, kv2_ref, kv3_ref, text_ref, out_ref):
    rows = own_ref.shape[1]
    for mine, (half, fresh) in enumerate(((0, own_ref), (1, other_ref))):
        q = fresh[0]
        stale = pl.ds((1 - half) * rows, rows)
        total = block_sums(q, fresh[1], fresh[2])
        total += block_sums(q, kv0_ref[0, stale, :], kv0_ref[1, stale, :])
        for kv in (kv1_ref, kv2_ref, kv3_ref, text_ref):
            total += block_sums(q, kv[0], kv[1])
        out_ref[pl.ds(mine * rows, rows), :] = total


def attend_local(core, own, other, kvs, text):
    _, rows, hd = own.shape
    whole = lambda a: pl.BlockSpec(a.shape, lambda k, c: (0,) * a.ndim)
    return pl.pallas_call(
        lambda c_ref, *refs: local_kernel(*refs),
        grid_spec=pltpu.PrefetchScalarGridSpec(
            num_scalar_prefetch=1,
            grid=(1,),
            in_specs=[whole(own), whole(other)]
            + [whole(kv) for kv in kvs]
            + [pl.BlockSpec((2, text.shape[1], hd), lambda k, c: (0, 0, c[0]))],
            out_specs=pl.BlockSpec((2 * rows, 2 * hd), lambda k, c: (0, 0)),
        ),
        out_shape=jax.ShapeDtypeStruct((2 * rows, 2 * hd), F32),
        compiler_params=params(),
        name="attend_local",
    )(core, own, other, *kvs, text)


def combine_kernel(local_ref, p1_ref, p2_ref, p3_ref, out_ref):
    rows, hd = out_ref.shape
    same = eye(hd)
    for i in range(rows // hd):
        at = slice(i * hd, (i + 1) * hd)
        summed = local_ref[at, :hd]
        totals = local_ref[at, hd:]
        line = None
        for p in (p1_ref, p2_ref, p3_ref):
            summed += p[at, :].astype(F32)
            pair = p[pl.ds(rows + 16 * i, 16), :].astype(F32)
            both = pair[0:1] + pair[8:9]
            line = both if line is None else line + both
        column = jnp.sum(jnp.broadcast_to(line, (hd, hd)) * same, 1, keepdims=True)
        out_ref[at, :] = (summed / (totals + column)).astype(BF)


def combine(local, parts):
    rows, hd = local.shape[0], local.shape[1] // 2
    return pl.pallas_call(
        combine_kernel,
        in_specs=[VMEM] * 4,
        out_specs=VMEM,
        out_shape=jax.ShapeDtypeStruct((rows, hd), BF),
        compiler_params=params(),
        name="combine",
    )(local, *parts)


def out_kernel(t_ref, a_ref, w_ref, image_ref, gate_ref, bias_ref, out_ref):
    n = a_ref.shape[0]
    acc = None
    for i in range(n):
        part = jnp.dot(a_ref[i], w_ref[i], preferred_element_type=F32)
        acc = part if acc is None else acc + part
    projection = acc + bias_ref[...]
    out_ref[...] = (image_ref[...].astype(F32) + gate_ref[...] * projection).astype(BF)


def project_out(tp, gathered, weight, image, gate, bias):
    n, rows, width = gathered.shape
    columns = weight.shape[2]
    return pl.pallas_call(
        out_kernel,
        grid_spec=pltpu.PrefetchScalarGridSpec(
            num_scalar_prefetch=1,
            grid=(1,),
            in_specs=[
                pl.BlockSpec((n, rows, width), lambda k, t: (0, 0, 0)),
                pl.BlockSpec((n, width, columns), lambda k, t: (0, 0, 0)),
                pl.BlockSpec((rows, columns), lambda k, t: (0, t[0])),
                pl.BlockSpec((1, columns), lambda k, t: (0, t[0])),
                pl.BlockSpec((1, columns), lambda k, t: (0, t[0])),
            ],
            out_specs=pl.BlockSpec((rows, columns), lambda k, t: (0, 0)),
        ),
        out_shape=jax.ShapeDtypeStruct((rows, columns), BF),
        compiler_params=params(),
        name="project_out",
    )(tp, gathered, weight, image, gate, bias)


def shards(image, mod_shift, mod_scale, mod_gate, qkv_weight, qkv_bias, q_gain, k_gain, stale_kv, text_kv, out_weight, out_bias):
    hd = q_gain.shape[0]
    rows, features = image.shape
    n_patch = lax.axis_size("patch")
    n_tp = lax.axis_size("tp")
    patch = lax.axis_index("patch")
    tp = lax.axis_index("tp")
    core = patch % 2
    core_at = core.astype(jnp.int32).reshape(1)
    tp_at = tp.astype(jnp.int32).reshape(1)

    def flip(bits):
        return [(i, i ^ bits) for i in range(n_patch)]

    def turn(k):
        return [(i, (i & ~12) | ((i + 4 * k) & 12)) for i in range(n_patch)]

    def send(x, perm):
        return lax.ppermute(x, "patch", perm)

    mine = lax.dynamic_slice_in_dim(stale_kv, core * hd, hd, 2)
    theirs = lax.dynamic_slice_in_dim(stale_kv, (1 - core) * hd, hd, 2)
    kv0 = jnp.concatenate([mine, send(theirs, flip(1))], 1)
    kvs = [kv0] + [send(kv0, turn(k)) for k in (1, 2, 3)]

    other_image = send(image, flip(1))
    shift = mod_shift.reshape(1, -1)
    scale = mod_scale.reshape(1, -1)
    gains = (q_gain.reshape(1, -1), k_gain.reshape(1, -1))
    own, wide = project_own(core_at, image, shift, scale, qkv_weight, qkv_bias, *gains)
    other = project_other(core_at, other_image, shift, scale, wide, qkv_bias, *gains)

    q = jnp.concatenate([own[0], other[0]], 0)
    hops = (2, 16, 18)
    partial = []
    for bits in hops:
        there = send(q, flip(bits))
        partial.append(send(attend_remote(there, kvs), flip(bits)))
    local = attend_local(core_at, own, other, kvs, text_kv)
    attended = combine(local, partial)

    back = send(other[1:], flip(1))
    first = core == 0
    fresh_kv = jnp.where(first, jnp.concatenate([own[1:], back], 2), jnp.concatenate([back, own[1:]], 2))

    swapped = send(attended[rows:], flip(1))
    kept = attended[:rows]
    heads = jnp.where(first, jnp.concatenate([kept, swapped], 1), jnp.concatenate([swapped, kept], 1))
    gathered = lax.all_to_all(jnp.broadcast_to(heads[None], (n_tp,) + heads.shape), "tp", 0, 0)

    columns = features // n_tp
    parts = out_weight.reshape(-1, n_tp, columns).swapaxes(0, 1)
    weight = lax.all_to_all(parts, "tp", 0, 0)
    piece = project_out(tp_at, gathered, weight, image, mod_gate.reshape(1, -1), out_bias.reshape(1, -1))
    pieces = lax.all_to_all(jnp.broadcast_to(piece[None], (n_tp,) + piece.shape), "tp", 0, 0)
    mixed = pieces.swapaxes(0, 1).reshape(rows, features)
    return (mixed, fresh_kv)


def solution(mesh):
    placed = (
        P("patch", None),
        P(),
        P(),
        P(),
        P(None, None, "tp"),
        P(None, "tp"),
        P(),
        P(),
        P(None, "patch", "tp"),
        P(None, None, "tp"),
        P("tp", None),
        P(),
    )
    return jax.shard_map(
        shards,
        mesh=mesh,
        in_specs=placed,
        out_specs=(P("patch", None), P(None, "patch", "tp")),
        check_vma=False,
    )
```

time: 255 us -> 120 us (0.47)
  waiting for transfers between devices: 161 us -> 41.1 us
  local copies, waits for them, and re-layouts: 57.1 us -> 16.9 us
  starting transfers between devices: 0.08 us -> 37.6 us
  Pallas kernels: 0 us -> 21.5 us
  matrix products: 14.7 us -> 0 us
  between operations: 14.3 us -> 0.99 us
  other arithmetic: 6.07 us -> 0.79 us
    psum x1 -> x0, waiting for transfers between devices: 83.6 us -> none  [shards(): projection = lax.psum(partial_terms, 'tp') + out_bias]
    all_gather x1 -> x0, waiting for transfers between devices: 77.5 us -> none  [shards(): kv_piece = lax.all_gather(stale_kv, 'patch', axis=1, tiled=True)]
    all_to_all x0 -> x3, waiting for transfers between devices: none -> 28.3 us  [the longest x1 15 us: shards(): lax.all_to_all(jnp.broadcast_to(piece[None], (n_tp,) + piece.shape), 'tp'...]
    unnamed x34 -> x30, local copies, waits for them, and re-layouts: 39.2 us -> 11.9 us
    ppermute x0 -> x13, starting transfers between devices: none -> 23.4 us  [send(): return lax.ppermute(x, 'patch', perm)]
    pallas_call x0 -> x8, Pallas kernels: none -> 21.5 us  [the longest x1 10.7 us: project_own(): pl.pallas_call(own_kernel, grid_spec=pltpu.PrefetchScalarGridSpec(num_sca...]
    slice x4 -> x3, local copies, waits for them, and re-layouts: 15.6 us -> 0.03 us  [the longest x1 0.01 us: shards(): kept = attended[:rows]]
    dot_general x8 -> x0, matrix products: 14.7 us -> none  [the longest x3 6.83 us: attend(): jnp.einsum('thd,rhd->thr', query_heads, key_heads, preferred_element_type...]
  transfers between devices with their start and end apart: 2 -> 16, of which waited for: 2 -> 9; matrix products, arithmetic and copies ran while one was open for 9% -> 11% of each run, Pallas kernels for 0% -> 18%
where the time goes in v1:
time: 120 us; the launch traced here: 119 us
  waiting for transfers between devices  41.1 us (34%)
  starting transfers between devices  37.6 us (31%)
  Pallas kernels  21.5 us (18%)
  local copies, waits for them, and re-layouts  16.9 us (14%)
    ppermute x13, starting transfers between devices, send(): return lax.ppermute(x, 'patch', perm)  23.4 us
    all_to_all x1, waiting for transfers between devices, shards(): lax.all_to_all(jnp.broadcast_to(piece[None], (n_tp,) + piece.shape), 'tp'...  15 us
    all_to_all x1, waiting for transfers between devices, shards(): lax.all_to_all(jnp.broadcast_to(heads[None], (n_tp,) + heads.shape), 'tp'...  13.2 us
    ppermute x13, waiting for transfers between devices, send(): return lax.ppermute(x, 'patch', perm)  12.8 us
    unnamed x30, local copies, waits for them, and re-layouts  11.9 us
    pallas_call x1, Pallas kernels, project_own(): pl.pallas_call(own_kernel, grid_spec=pltpu.PrefetchScalarGridSpec(num_sca...  10.7 us
    all_to_all x1, starting transfers between devices, shards(): weight = lax.all_to_all(parts, 'tp', 0, 0)  5.44 us
    all_to_all x1, starting transfers between devices, shards(): lax.all_to_all(jnp.broadcast_to(heads[None], (n_tp,) + heads.shape), 'tp'...  5.07 us
  transfers between devices with their start and end apart: 16, of which 9 were waited for; matrix products, arithmetic and copies ran while one was open for 11% of the time, Pallas kernels for 18%

profile of v1, /device:TPU:32, one launch (start us, length us, event | category | flops | bytes accessed | tf_op | source)
XLA Modules:
  0.0 118.8 jit_solution(10769614601080777891)
XLA Ops:
  0.7 1.7 %copy.22 = bf16[256,3072]{0,1:T(8,128)(2,1)S(1)} copy(bf16[256,3072]{1,0:T(8,128)(2,1)} %param.22) | data formatting | bytes 3145728 | tf_op args[10]
  2.4 1.6 %copy.23 = bf16[256,8,384]{2,0,1:T(8,128)(2,1)} copy(bf16[256,8,384]{0,2,1:T(8,128)(2,1)S(1)} %bitcast.27) | data formatting | bytes 3145728 | tf_op jit(solution)/shard_map/reshape | solution.py:326
  4.1 5.4 %all-to-all-start.1 = ((bf16[8,256,384]{2,1,0:T(8,128)(2,1)}), bf16[8,256,384]{2,1,0:T(8,128)(2,1)S(1)}, u32[]{:S(2)}, u32[]{:S(2)}) async-start(bf16[8,256,384]{2,1,0:T(8,128)(2,1)} %bitcast.9), calls=%async_computation.1 | async-start | bytes 3145728 | tf_op jit(solution)/shard_map/all_to_all | solution.py:327
  9.9 9.4 %copy.21.w_ref = bf16[3072,3,256]{2,1,0:T(4,128)(2,1)} copy(bf16[3072,3,256]{2,0,1:T(8,128)(2,1)} %param.16) | data formatting | bytes 9437184 | tf_op args[4]
  19.4 10.7 %project_own.1 = (bf16[3,192,128]{2,1,0:T(8,128)(2,1)S(1)}, bf16[3072,384]{1,0:T(8,128)(2,1)S(1)}) custom-call(s32[1]{0:T(128)} %bitcast.1.c_ref, bf16[192,3072]{1,0:T(8,128)(2,1)S(1)} %copy-done, f32[1,3072]{1,0:T(1,128)S(1)} %bitcast.17, f32[1,3072]{1,0:T(1,128)S(1)} %bitcast.19, bf16[3072,3,256]{2,1,0:T(4,128)(2,1)} %copy.21.w_ref, ...), custom_call_target="tpu_custom_call" | custom-call | tf_op jit(solution)/shard_map/project_own/pallas_call | solution.py:75
  30.1 3.4 %collective-permute-start.2 = (bf16[2,384,128]{2,1,0:T(8,128)(2,1)S(1)}, bf16[2,384,128]{2,1,0:T(8,128)(2,1)S(1)}, u32[]{:S(2)}, u32[]{:S(2)}) collective-permute-start(bf16[2,384,128]{2,1,0:T(8,128)(2,1)S(1)} %pad_maximum_fusion.refs_2_.kv0_ref), channel_id=1, source_target_pairs={{0,32},{8,40},{16,48},{24,56},{32,64},{40,72},{48,80},{56,88},{64,... | collective-permute-start | bytes 589832 | tf_op jit(solution)/shard_map/ppermute | solution.py:293
  33.5 4.5 %collective-permute-start.3 = (bf16[2,384,128]{2,1,0:T(8,128)(2,1)S(1)}, bf16[2,384,128]{2,1,0:T(8,128)(2,1)S(1)}, u32[]{:S(2)}, u32[]{:S(2)}) collective-permute-start(bf16[2,384,128]{2,1,0:T(8,128)(2,1)S(1)} %pad_maximum_fusion.refs_2_.kv0_ref), channel_id=1, source_target_pairs={{0,64},{8,72},{16,80},{24,88},{32,96},{40,104},{48,112},{56,120},{... | collective-permute-start | bytes 589832 | tf_op jit(solution)/shard_map/ppermute | solution.py:293
  38.0 2.7 %collective-permute-start.4 = (bf16[2,384,128]{2,1,0:T(8,128)(2,1)S(1)}, bf16[2,384,128]{2,1,0:T(8,128)(2,1)S(1)}, u32[]{:S(2)}, u32[]{:S(2)}) collective-permute-start(bf16[2,384,128]{2,1,0:T(8,128)(2,1)S(1)} %pad_maximum_fusion.refs_2_.kv0_ref), channel_id=1, source_target_pairs={{0,96},{8,104},{16,112},{24,120},{32,0},{40,8},{48,16},{56,24},{64... | collective-permute-start | bytes 589832 | tf_op jit(solution)/shard_map/ppermute | solution.py:293
  40.7 5.0 %project_other.1.refs_1_ = bf16[3,192,128]{2,1,0:T(8,128)(2,1)S(1)} custom-call(s32[1]{0:T(128)} %bitcast.1.c_ref, bf16[192,3072]{1,0:T(8,128)(2,1)} %collective-permute-done.image_ref, f32[1,3072]{1,0:T(1,128)S(1)} %bitcast.18, f32[1,3072]{1,0:T(1,128)S(1)} %bitcast.20, bf16[3072,384]{1,0:T(8,128)(2,1)S(1)} %get-tuple-element.5.wide_ref, ...), custom_call_target="tpu_custom_call" | custom-call | tf_op jit(solution)/shard_map/project_other/pallas_call | solution.py:117
  45.8 3.4 %collective-permute-start.9 = (bf16[384,128]{1,0:T(8,128)(2,1)S(1)}, bf16[384,128]{1,0:T(8,128)(2,1)S(1)}, u32[]{:S(2)}, u32[]{:S(2)}) collective-permute-start(bf16[384,128]{1,0:T(8,128)(2,1)S(1)} %pad_maximum_fusion.1), channel_id=1, source_target_pairs={{0,144},{8,152},{16,128},{24,136},{32,176},{40,184},{48,160},{56,1... | collective-permute-start | bytes 294920 | tf_op jit(solution)/shard_map/ppermute | solution.py:293
  49.2 0.6 collective-permute-start.7
  49.8 1.2 %collective-permute-done.2.refs_3_.kv1_ref = bf16[2,384,128]{2,1,0:T(8,128)(2,1)S(1)} collective-permute-done((bf16[2,384,128]{2,1,0:T(8,128)(2,1)S(1)}, bf16[2,384,128]{2,1,0:T(8,128)(2,1)S(1)}, u32[]{:S(2)}, u32[]{:S(2)}) %collective-permute-start.2) | collective-permute-done | bytes 196640 | tf_op jit(solution)/shard_map/ppermute | solution.py:293
  51.0 3.5 %collective-permute-done.4.refs_5_.kv3_ref = bf16[2,384,128]{2,1,0:T(8,128)(2,1)S(1)} collective-permute-done((bf16[2,384,128]{2,1,0:T(8,128)(2,1)S(1)}, bf16[2,384,128]{2,1,0:T(8,128)(2,1)S(1)}, u32[]{:S(2)}, u32[]{:S(2)}) %collective-permute-start.4) | collective-permute-done | bytes 196640 | tf_op jit(solution)/shard_map/ppermute | solution.py:293
  54.6 2.4 %collective-permute-done.9.q_ref = bf16[384,128]{1,0:T(8,128)(2,1)S(1)} collective-permute-done((bf16[384,128]{1,0:T(8,128)(2,1)S(1)}, bf16[384,128]{1,0:T(8,128)(2,1)S(1)}, u32[]{:S(2)}, u32[]{:S(2)}) %collective-permute-start.9) | collective-permute-done | bytes 98336 | tf_op jit(solution)/shard_map/ppermute | solution.py:293
  56.9 1.2 %attend_remote.5 = bf16[432,128]{1,0:T(8,128)(2,1)S(1)} custom-call(bf16[384,128]{1,0:T(8,128)(2,1)S(1)} %collective-permute-done.9.q_ref, bf16[2,384,128]{2,1,0:T(8,128)(2,1)S(1)} %pad_maximum_fusion.refs_2_.kv0_ref, bf16[2,384,128]{2,1,0:T(8,128)(2,1)S(1)} %collective-permute-done.2.refs_3_.kv1_ref, ...), custom_call_target="tpu_custom_call" | custom-call | tf_op jit(solution)/shard_map/attend_remote/pallas_call | solution.py:172
  58.1 5.0 %collective-permute-start.10 = (bf16[432,128]{1,0:T(8,128)(2,1)S(1)}, bf16[432,128]{1,0:T(8,128)(2,1)S(1)}, u32[]{:S(2)}, u32[]{:S(2)}) collective-permute-start(bf16[432,128]{1,0:T(8,128)(2,1)S(1)} %attend_remote.5), channel_id=1, source_target_pairs={{0,144},{8,152},{16,128},{24,136},{32,176},{40,184},{48,160},{56,1... | collective-permute-start | bytes 331784 | tf_op jit(solution)/shard_map/ppermute | solution.py:293
  63.1 1.2 %attend_remote.4 = bf16[432,128]{1,0:T(8,128)(2,1)S(1)} custom-call(bf16[384,128]{1,0:T(8,128)(2,1)S(1)} %collective-permute-done.7.q_ref, bf16[2,384,128]{2,1,0:T(8,128)(2,1)S(1)} %pad_maximum_fusion.refs_2_.kv0_ref, bf16[2,384,128]{2,1,0:T(8,128)(2,1)S(1)} %collective-permute-done.2.refs_3_.kv1_ref, ...), custom_call_target="tpu_custom_call" | custom-call | tf_op jit(solution)/shard_map/attend_remote/pallas_call | solution.py:172
  64.3 3.2 %collective-permute-start.8 = (bf16[432,128]{1,0:T(8,128)(2,1)S(1)}, bf16[432,128]{1,0:T(8,128)(2,1)S(1)}, u32[]{:S(2)}, u32[]{:S(2)}) collective-permute-start(bf16[432,128]{1,0:T(8,128)(2,1)S(1)} %attend_remote.4), channel_id=1, source_target_pairs={{0,128},{8,136},{16,144},{24,152},{32,160},{40,168},{48,176},{56,1... | collective-permute-start | bytes 331784 | tf_op jit(solution)/shard_map/ppermute | solution.py:293
  67.5 1.2 %attend_remote.3 = bf16[432,128]{1,0:T(8,128)(2,1)S(1)} custom-call(bf16[384,128]{1,0:T(8,128)(2,1)S(1)} %collective-permute-done.5.q_ref, bf16[2,384,128]{2,1,0:T(8,128)(2,1)S(1)} %pad_maximum_fusion.refs_2_.kv0_ref, bf16[2,384,128]{2,1,0:T(8,128)(2,1)S(1)} %collective-permute-done.2.refs_3_.kv1_ref, ...), custom_call_target="tpu_custom_call" | custom-call | tf_op jit(solution)/shard_map/attend_remote/pallas_call | solution.py:172
  68.8 1.4 %attend_local.1.local_ref = f32[384,256]{1,0:T(8,128)S(1)} custom-call(s32[1]{0:T(128)} %bitcast.1.c_ref, bf16[3,192,128]{2,1,0:T(8,128)(2,1)S(1)} %get-tuple-element.4.refs_0_, bf16[3,192,128]{2,1,0:T(8,128)(2,1)S(1)} %project_other.1.refs_1_, bf16[2,384,128]{2,1,0:T(8,128)(2,1)S(1)} %pad_maximum_fusion.refs_2_.kv0_ref, ...), custom_call_target="tpu_custom_call" | custom-call | tf_op jit(solution)/shard_map/attend_local/pallas_call | solution.py:197
  70.8 2.7 %collective-permute-done.6.p1_ref = bf16[432,128]{1,0:T(8,128)(2,1)S(1)} collective-permute-done((bf16[432,128]{1,0:T(8,128)(2,1)S(1)}, bf16[432,128]{1,0:T(8,128)(2,1)S(1)}, u32[]{:S(2)}, u32[]{:S(2)}) %collective-permute-start.6) | collective-permute-done | bytes 110624 | tf_op jit(solution)/shard_map/ppermute | solution.py:293
  73.8 1.2 %collective-permute-done.11 = bf16[192,128]{1,0:T(8,128)(2,1)S(1)} collective-permute-done((bf16[192,128]{1,0:T(8,128)(2,1)S(1)}, bf16[192,128]{1,0:T(8,128)(2,1)S(1)}, u32[]{:S(2)}, u32[]{:S(2)}) %collective-permute-start.11) | collective-permute-done | bytes 49184 | tf_op jit(solution)/shard_map/ppermute | solution.py:293
  75.0 0.9 broadcast_in_dim.4
  76.0 5.1 %all-to-all-start = ((bf16[8,192,256]{2,1,0:T(8,128)(2,1)}), bf16[8,192,256]{2,1,0:T(8,128)(2,1)S(1)}, u32[]{:S(2)}, u32[]{:S(2)}) async-start(bf16[8,192,256]{2,1,0:T(8,128)(2,1)} %broadcast_in_dim.4), calls=%async_computation | async-start | bytes 1572864 | tf_op jit(solution)/shard_map/all_to_all | solution.py:323
  81.0 13.2 %all-to-all-done.a_ref = bf16[8,192,256]{2,1,0:T(8,128)(2,1)S(1)} async-done(((bf16[8,192,256]{2,1,0:T(8,128)(2,1)}), bf16[8,192,256]{2,1,0:T(8,128)(2,1)S(1)}, u32[]{:S(2)}, u32[]{:S(2)}) %all-to-all-start) | async-done | bytes 786464 | tf_op jit(solution)/shard_map/all_to_all | solution.py:323
  94.3 0.7 copy-done.10
  95.6 1.1 broadcast_in_dim.5
  96.7 3.7 %all-to-all-start.2 = ((bf16[8,192,384]{2,1,0:T(8,128)(2,1)}), bf16[8,192,384]{2,1,0:T(8,128)(2,1)S(1)}, u32[]{:S(2)}, u32[]{:S(2)}) async-start(bf16[8,192,384]{2,1,0:T(8,128)(2,1)} %broadcast_in_dim.5), calls=%async_computation.2 | async-start | bytes 2359296 | tf_op jit(solution)/shard_map/all_to_all | solution.py:329
  100.5 1.3 %collective-permute-done.12 = bf16[2,192,128]{2,1,0:T(8,128)(2,1)S(1)} collective-permute-done((bf16[2,192,128]{2,1,0:T(8,128)(2,1)S(1)}, bf16[2,192,128]{2,1,0:T(8,128)(2,1)S(1)}, u32[]{:S(2)}, u32[]{:S(2)}) %collective-permute-start.12) | collective-permute-done | bytes 98336 | tf_op jit(solution)/shard_map/ppermute | solution.py:293
  101.8 0.7 maximum_select_fusion
  102.6 15.0 %all-to-all-done.2 = bf16[8,192,384]{2,1,0:T(8,128)(2,1)S(1)} async-done(((bf16[8,192,384]{2,1,0:T(8,128)(2,1)}), bf16[8,192,384]{2,1,0:T(8,128)(2,1)S(1)}, u32[]{:S(2)}, u32[]{:S(2)}) %all-to-all-start.2) | async-done | bytes 1179680 | tf_op jit(solution)/shard_map/all_to_all | solution.py:329
  117.6 1.2 %copy.25 = bf16[8,24,8,384]{3,2,0,1:T(8,128)(2,1)} copy(bf16[8,24,8,384]{3,2,1,0:T(8,128)(2,1)S(1)} %bitcast.28) | data formatting | bytes 2359296 | tf_op jit(solution)/shard_map/reshape | solution.py:330
  (52 shorter events, 2.2 us)
Async XLA Ops:
  0.6 40.0 %collective-permute-start = (bf16[192,3072]{1,0:T(8,128)(2,1)}, bf16[192,3072]{1,0:T(8,128)(2,1)}, u32[]{:S(2)}, u32[]{:S(2)}) collective-permute-start(bf16[192,3072]{1,0:T(8,128)(2,1)} %image_ref.3), channel_id=1, source_target_pairs={{0,8},{8,0},{16,24},{24,16},{32,40},{40,32},{48,56},{56,48},{64,72... | collective-permute-start | bytes 3538952 | tf_op jit(solution)/shard_map/ppermute | solution.py:293
  4.1 5.4 %copy-start.13 = (bf16[2,192,256]{2,1,0:T(8,128)(2,1)S(1)}, bf16[2,192,256]{2,1,0:T(8,128)(2,1)}, u32[]{:S(2)}) copy-start(bf16[2,192,256]{2,1,0:T(8,128)(2,1)} %param.20) | copy-start | bytes 589828
  4.1 71.0 %all-to-all-start.1 = ((bf16[8,256,384]{2,1,0:T(8,128)(2,1)}), bf16[8,256,384]{2,1,0:T(8,128)(2,1)S(1)}, u32[]{:S(2)}, u32[]{:S(2)}) async-start(bf16[8,256,384]{2,1,0:T(8,128)(2,1)} %bitcast.9), calls=%async_computation.1 | async-start | bytes 3145728 | tf_op jit(solution)/shard_map/all_to_all | solution.py:327
  9.6 9.8 %copy-start = (bf16[192,3072]{1,0:T(8,128)(2,1)S(1)}, bf16[192,3072]{1,0:T(8,128)(2,1)}, u32[]{:S(2)}) copy-start(bf16[192,3072]{1,0:T(8,128)(2,1)} %image_ref.3) | copy-start | bytes 3538948
  9.6 9.8 %copy-start.6 = (f32[3072]{0:T(1024)S(1)}, f32[3072]{0:T(1024)}, u32[]{:S(2)}) copy-start(f32[3072]{0:T(1024)} %param.13) | copy-start | bytes 36868
  9.6 9.8 %copy-start.7 = (f32[3072]{0:T(1024)S(1)}, f32[3072]{0:T(1024)}, u32[]{:S(2)}) copy-start(f32[3072]{0:T(1024)} %param.14) | copy-start | bytes 36868
  9.6 9.8 %copy-start.8 = (f32[3,256]{1,0:T(4,128)S(1)}, f32[3,256]{1,0:T(4,128)}, u32[]{:S(2)}) copy-start(f32[3,256]{1,0:T(4,128)} %bias_ref.3) | copy-start | bytes 9220
  9.6 9.8 %copy-start.11 = (f32[128]{0:T(128)S(1)}, f32[128]{0:T(128)}, u32[]{:S(2)}) copy-start(f32[128]{0:T(128)} %param.18) | copy-start | bytes 1540
  9.6 9.8 %copy-start.12 = (f32[128]{0:T(128)S(1)}, f32[128]{0:T(128)}, u32[]{:S(2)}) copy-start(f32[128]{0:T(128)} %param.19) | copy-start | bytes 1540
  9.6 20.5 %collective-permute-start.1 = (bf16[2,192,128]{2,1,0:T(8,128)(2,1)S(1)}, bf16[2,192,128]{2,1,0:T(8,128)(2,1)S(1)}, u32[]{:S(2)}, u32[]{:S(2)}) collective-permute-start(bf16[2,192,128]{2,1,0:T(8,128)(2,1)S(1)} %get-tuple-element.7), channel_id=1, source_target_pairs={{0,8},{8,0},{16,24},{24,16},{32,40},{40,32},{48,56},{56,48},{64,72... | collective-permute-start | bytes 294920 | tf_op jit(solution)/shard_map/ppermute | solution.py:293
  30.1 38.7 %copy-start.3 = (bf16[3,192,128]{2,1,0:T(8,128)(2,1)}, bf16[3,192,128]{2,1,0:T(8,128)(2,1)S(1)}, u32[]{:S(2)}) copy-start(bf16[3,192,128]{2,1,0:T(8,128)(2,1)S(1)} %get-tuple-element.4.refs_0_) | copy-start | bytes 442372
  30.1 20.9 %collective-permute-start.2 = (bf16[2,384,128]{2,1,0:T(8,128)(2,1)S(1)}, bf16[2,384,128]{2,1,0:T(8,128)(2,1)S(1)}, u32[]{:S(2)}, u32[]{:S(2)}) collective-permute-start(bf16[2,384,128]{2,1,0:T(8,128)(2,1)S(1)} %pad_maximum_fusion.refs_2_.kv0_ref), channel_id=1, source_target_pairs={{0,32},{8,40},{16,48},{24,56},{32,64},{40,72},{48,80},{56,88},{64,... | collective-permute-start | bytes 589832 | tf_op jit(solution)/shard_map/ppermute | solution.py:293
  33.5 17.6 %collective-permute-start.3 = (bf16[2,384,128]{2,1,0:T(8,128)(2,1)S(1)}, bf16[2,384,128]{2,1,0:T(8,128)(2,1)S(1)}, u32[]{:S(2)}, u32[]{:S(2)}) collective-permute-start(bf16[2,384,128]{2,1,0:T(8,128)(2,1)S(1)} %pad_maximum_fusion.refs_2_.kv0_ref), channel_id=1, source_target_pairs={{0,64},{8,72},{16,80},{24,88},{32,96},{40,104},{48,112},{56,120},{... | collective-permute-start | bytes 589832 | tf_op jit(solution)/shard_map/ppermute | solution.py:293
  38.0 16.6 %collective-permute-start.4 = (bf16[2,384,128]{2,1,0:T(8,128)(2,1)S(1)}, bf16[2,384,128]{2,1,0:T(8,128)(2,1)S(1)}, u32[]{:S(2)}, u32[]{:S(2)}) collective-permute-start(bf16[2,384,128]{2,1,0:T(8,128)(2,1)S(1)} %pad_maximum_fusion.refs_2_.kv0_ref), channel_id=1, source_target_pairs={{0,96},{8,104},{16,112},{24,120},{32,0},{40,8},{48,16},{56,24},{64... | collective-permute-start | bytes 589832 | tf_op jit(solution)/shard_map/ppermute | solution.py:293
  45.7 23.1 %copy-start.1 = (bf16[3,192,128]{2,1,0:T(8,128)(2,1)}, bf16[3,192,128]{2,1,0:T(8,128)(2,1)S(1)}, u32[]{:S(2)}) copy-start(bf16[3,192,128]{2,1,0:T(8,128)(2,1)S(1)} %project_other.1.refs_1_) | copy-start | bytes 442372
  45.7 23.1 %copy-start.5 = (bf16[2,512,256]{2,1,0:T(8,128)(2,1)S(1)}, bf16[2,512,256]{2,1,0:T(8,128)(2,1)}, u32[]{:S(2)}) copy-start(bf16[2,512,256]{2,1,0:T(8,128)(2,1)} %refs_6_.1) | copy-start | bytes 1572868
  45.8 11.2 %collective-permute-start.9 = (bf16[384,128]{1,0:T(8,128)(2,1)S(1)}, bf16[384,128]{1,0:T(8,128)(2,1)S(1)}, u32[]{:S(2)}, u32[]{:S(2)}) collective-permute-start(bf16[384,128]{1,0:T(8,128)(2,1)S(1)} %pad_maximum_fusion.1), channel_id=1, source_target_pairs={{0,144},{8,152},{16,128},{24,136},{32,176},{40,184},{48,160},{56,1... | collective-permute-start | bytes 294920 | tf_op jit(solution)/shard_map/ppermute | solution.py:293
  49.2 13.9 %collective-permute-start.7 = (bf16[384,128]{1,0:T(8,128)(2,1)S(1)}, bf16[384,128]{1,0:T(8,128)(2,1)S(1)}, u32[]{:S(2)}, u32[]{:S(2)}) collective-permute-start(bf16[384,128]{1,0:T(8,128)(2,1)S(1)} %pad_maximum_fusion.1), channel_id=1, source_target_pairs={{0,128},{8,136},{16,144},{24,152},{32,160},{40,168},{48,176},{56,1... | collective-permute-start | bytes 294920 | tf_op jit(solution)/shard_map/ppermute | solution.py:293
  51.0 16.4 %collective-permute-start.5 = (bf16[384,128]{1,0:T(8,128)(2,1)S(1)}, bf16[384,128]{1,0:T(8,128)(2,1)S(1)}, u32[]{:S(2)}, u32[]{:S(2)}) collective-permute-start(bf16[384,128]{1,0:T(8,128)(2,1)S(1)} %pad_maximum_fusion.1), channel_id=1, source_target_pairs={{0,16},{8,24},{16,0},{24,8},{32,48},{40,56},{48,32},{56,40},{64,80... | collective-permute-start | bytes 294920 | tf_op jit(solution)/shard_map/ppermute | solution.py:293
  58.1 12.1 %collective-permute-start.10 = (bf16[432,128]{1,0:T(8,128)(2,1)S(1)}, bf16[432,128]{1,0:T(8,128)(2,1)S(1)}, u32[]{:S(2)}, u32[]{:S(2)}) collective-permute-start(bf16[432,128]{1,0:T(8,128)(2,1)S(1)} %attend_remote.5), channel_id=1, source_target_pairs={{0,144},{8,152},{16,128},{24,136},{32,176},{40,184},{48,160},{56,1... | collective-permute-start | bytes 331784 | tf_op jit(solution)/shard_map/ppermute | solution.py:293
  64.3 6.5 %collective-permute-start.8 = (bf16[432,128]{1,0:T(8,128)(2,1)S(1)}, bf16[432,128]{1,0:T(8,128)(2,1)S(1)}, u32[]{:S(2)}, u32[]{:S(2)}) collective-permute-start(bf16[432,128]{1,0:T(8,128)(2,1)S(1)} %attend_remote.4), channel_id=1, source_target_pairs={{0,128},{8,136},{16,144},{24,152},{32,160},{40,168},{48,176},{56,1... | collective-permute-start | bytes 331784 | tf_op jit(solution)/shard_map/ppermute | solution.py:293
  68.7 4.8 %collective-permute-start.6 = (bf16[432,128]{1,0:T(8,128)(2,1)S(1)}, bf16[432,128]{1,0:T(8,128)(2,1)S(1)}, u32[]{:S(2)}, u32[]{:S(2)}) collective-permute-start(bf16[432,128]{1,0:T(8,128)(2,1)S(1)} %attend_remote.3), channel_id=1, source_target_pairs={{0,16},{8,24},{16,0},{24,8},{32,48},{40,56},{48,32},{56,40},{64,80... | collective-permute-start | bytes 331784 | tf_op jit(solution)/shard_map/ppermute | solution.py:293
  73.6 20.6 %copy-start.9 = (f32[3072]{0:T(1024)S(1)}, f32[3072]{0:T(1024)}, u32[]{:S(2)}) copy-start(f32[3072]{0:T(1024)} %param.15) | copy-start | bytes 36868
  73.7 1.3 %collective-permute-start.11 = (bf16[192,128]{1,0:T(8,128)(2,1)S(1)}, bf16[192,128]{1,0:T(8,128)(2,1)S(1)}, u32[]{:S(2)}, u32[]{:S(2)}) collective-permute-start(bf16[192,128]{1,0:T(8,128)(2,1)S(1)} %get-tuple-element.9), channel_id=1, source_target_pairs={{0,8},{8,0},{16,24},{24,16},{32,40},{40,32},{48,56},{56,48},{64,72... | collective-permute-start | bytes 147464 | tf_op jit(solution)/shard_map/ppermute | solution.py:293
  76.0 18.3 %all-to-all-start = ((bf16[8,192,256]{2,1,0:T(8,128)(2,1)}), bf16[8,192,256]{2,1,0:T(8,128)(2,1)S(1)}, u32[]{:S(2)}, u32[]{:S(2)}) async-start(bf16[8,192,256]{2,1,0:T(8,128)(2,1)} %broadcast_in_dim.4), calls=%async_computation | async-start | bytes 1572864 | tf_op jit(solution)/shard_map/all_to_all | solution.py:323
  94.3 0.7 copy-start.10
  95.6 4.8 %copy-start.2 = (bf16[3,192,128]{2,1,0:T(8,128)(2,1)S(1)}, bf16[3,192,128]{2,1,0:T(8,128)(2,1)}, u32[]{:S(2)}) copy-start(bf16[3,192,128]{2,1,0:T(8,128)(2,1)} %copy-done.1) | copy-start | bytes 442372
  96.7 3.8 %copy-start.4 = (bf16[3,192,128]{2,1,0:T(8,128)(2,1)S(1)}, bf16[3,192,128]{2,1,0:T(8,128)(2,1)}, u32[]{:S(2)}) copy-start(bf16[3,192,128]{2,1,0:T(8,128)(2,1)} %copy-done.3) | copy-start | bytes 442372
  96.7 20.9 %all-to-all-start.2 = ((bf16[8,192,384]{2,1,0:T(8,128)(2,1)}), bf16[8,192,384]{2,1,0:T(8,128)(2,1)S(1)}, u32[]{:S(2)}, u32[]{:S(2)}) async-start(bf16[8,192,384]{2,1,0:T(8,128)(2,1)} %broadcast_in_dim.5), calls=%async_computation.2 | async-start | bytes 2359296 | tf_op jit(solution)/shard_map/all_to_all | solution.py:329
  100.4 1.4 %collective-permute-start.12 = (bf16[2,192,128]{2,1,0:T(8,128)(2,1)S(1)}, bf16[2,192,128]{2,1,0:T(8,128)(2,1)S(1)}, u32[]{:S(2)}, u32[]{:S(2)}) collective-permute-start(bf16[2,192,128]{2,1,0:T(8,128)(2,1)S(1)} %slice.28), channel_id=1, source_target_pairs={{0,8},{8,0},{16,24},{24,16},{32,40},{40,32},{48,56},{56,48},{64,72... | collective-permute-start | bytes 294920 | tf_op jit(solution)/shard_map/ppermute | solution.py:293

commit v2 on v1

v2 whole, which is shorter than its diff:
```python
import math

import jax
import jax.numpy as jnp
from jax import lax
from jax.experimental import pallas as pl
from jax.experimental.pallas import tpu as pltpu
from jax.sharding import PartitionSpec as P

BF = jnp.bfloat16
F32 = jnp.float32
VMEM = pl.BlockSpec(memory_space=pltpu.VMEM)
SMEM = pl.BlockSpec(memory_space=pltpu.SMEM)
LIMIT = 48 * 1024 * 1024


def params(**kw):
    return pltpu.CompilerParams(vmem_limit_bytes=LIMIT, **kw)


def prepare_kernel(c_ref, image_ref, shift_ref, scale_ref, stale_ref, mod_ref, mine_ref, theirs_ref):
    hd = mine_ref.shape[2]
    core = c_ref[0]
    mine_ref[...] = stale_ref[:, :, pl.ds(pl.multiple_of(core * hd, hd), hd)]
    theirs_ref[...] = stale_ref[:, :, pl.ds(pl.multiple_of((1 - core) * hd, hd), hd)]
    step = 32
    for i in range(image_ref.shape[0] // step):
        at = slice(i * step, (i + 1) * step)
        wide = image_ref[at, :].astype(F32)
        average = jnp.mean(wide, -1, keepdims=True)
        centred = wide - average
        spread = jnp.mean(centred * centred, -1, keepdims=True)
        normed = centred * lax.rsqrt(spread + 1e-06)
        mod_ref[at, :] = (normed * (1.0 + scale_ref[...]) + shift_ref[...]).astype(BF)


def prepare(core, image, shift, scale, stale, hd):
    return pl.pallas_call(
        prepare_kernel,
        in_specs=[SMEM] + [VMEM] * 4,
        out_specs=[VMEM] * 3,
        out_shape=[
            jax.ShapeDtypeStruct(image.shape, BF),
            jax.ShapeDtypeStruct(stale.shape[:2] + (hd,), BF),
            jax.ShapeDtypeStruct(stale.shape[:2] + (hd,), BF),
        ],
        compiler_params=params(),
        name="prepare",
    )(core, image, shift, scale, stale)


def project_kernel(c_ref, own_ref, other_ref, w_ref, bias_ref, q_gain_ref, k_gain_ref, q_ref, kv_own_ref, kv_other_ref, acc_ref):
    k = pl.program_id(0)
    rows = own_ref.shape[0]
    hd = q_gain_ref.shape[1]
    w = w_ref[...].reshape(3 * hd, w_ref.shape[2])

    @pl.when(k == 0)
    def _():
        acc_ref[...] = jnp.zeros_like(acc_ref)

    for i, m_ref in enumerate((own_ref, other_ref)):
        acc_ref[pl.ds(i * rows, rows), :] += lax.dot_general(
            m_ref[...], w, (((1,), (1,)), ((), ())), preferred_element_type=F32
        )

    def norm(part, gain):
        return part * lax.rsqrt(jnp.mean(part * part, -1, keepdims=True) + 1e-06) * gain

    @pl.when(k == pl.num_programs(0) - 1)
    def _():
        q = acc_ref[:, :hd] + bias_ref[0:1, :]
        q_ref[...] = norm(q, q_gain_ref[...]).astype(BF)
        for i, out_ref in enumerate((kv_own_ref, kv_other_ref)):
            at = pl.ds(i * rows, rows)
            out_ref[0] = norm(acc_ref[at, hd : 2 * hd] + bias_ref[1:2, :], k_gain_ref[...]).astype(BF)
            out_ref[1] = (acc_ref[at, 2 * hd :] + bias_ref[2:3, :]).astype(BF)


def project(core, own, other, weight, bias, q_gain, k_gain):
    rows, features = own.shape
    hd = q_gain.shape[1]
    depth = features // 4
    whole = lambda shape: pl.BlockSpec(shape, lambda k, c: (0,) * len(shape))
    return pl.pallas_call(
        project_kernel,
        grid_spec=pltpu.PrefetchScalarGridSpec(
            num_scalar_prefetch=1,
            grid=(features // depth,),
            in_specs=[
                pl.BlockSpec((rows, depth), lambda k, c: (0, k)),
                pl.BlockSpec((rows, depth), lambda k, c: (0, k)),
                pl.BlockSpec((3, hd, depth), lambda k, c: (0, c[0], k)),
                pl.BlockSpec((3, hd), lambda k, c: (0, c[0])),
                whole((1, hd)),
                whole((1, hd)),
            ],
            out_specs=[whole((2 * rows, hd)), whole((2, rows, hd)), whole((2, rows, hd))],
            scratch_shapes=[pltpu.VMEM((2 * rows, 3 * hd), F32)],
        ),
        out_shape=[
            jax.ShapeDtypeStruct((2 * rows, hd), BF),
            jax.ShapeDtypeStruct((2, rows, hd), BF),
            jax.ShapeDtypeStruct((2, rows, hd), BF),
        ],
        compiler_params=params(),
        name="project",
    )(core, own, other, weight, bias, q_gain, k_gain)


def block_sums(q, k, v_ref_value):
    hd = q.shape[1]
    scores = lax.dot_general(q, k, (((1,), (1,)), ((), ())), preferred_element_type=F32)
    weights = jnp.exp2(scores * (math.log2(math.e) / math.sqrt(hd))).astype(BF)
    ones = jnp.ones_like(v_ref_value)
    return jnp.dot(weights, jnp.concatenate([v_ref_value, ones], 1), preferred_element_type=F32)


def eye(n):
    return (lax.broadcasted_iota(jnp.int32, (n, n), 0) == lax.broadcasted_iota(jnp.int32, (n, n), 1)).astype(F32)


def remote_kernel(q_ref, kv_ref, out_ref):
    rows, hd = q_ref.shape
    same = eye(hd)
    for i in range(rows // hd):
        at = slice(i * hd, (i + 1) * hd)
        q = q_ref[at, :]
        total = None
        for j in range(kv_ref.shape[0]):
            part = block_sums(q, kv_ref[j, 0], kv_ref[j, 1])
            total = part if total is None else total + part
        out_ref[at, :] = total[:, :hd].astype(BF)
        line = jnp.sum(total[:, hd:] * same, 0, keepdims=True)
        high = line.astype(BF).astype(F32)
        out_ref[pl.ds(rows + 16 * i, 16), :] = jnp.concatenate(
            [jnp.broadcast_to(high, (8, hd)), jnp.broadcast_to(line - high, (8, hd))], 0
        ).astype(BF)


def attend_remote(q, kv):
    rows, hd = q.shape
    return pl.pallas_call(
        remote_kernel,
        in_specs=[VMEM] * 2,
        out_specs=VMEM,
        out_shape=jax.ShapeDtypeStruct((rows + 16 * (rows // hd), hd), BF),
        compiler_params=params(),
        name="attend_remote",
    )(q, kv)


def local_kernel(c_ref, q_ref, own_ref, other_ref, kv_ref, text_ref, out_ref):
    rows = own_ref.shape[1]
    hd = q_ref.shape[1]
    n = kv_ref.shape[0]
    slot = c_ref[1]
    head = pl.ds(pl.multiple_of(c_ref[0] * hd, hd), hd)
    for i, fresh in enumerate((own_ref, other_ref)):
        at = pl.ds(i * rows, rows)
        q = q_ref[at, :]
        stale = pl.ds((1 - i) * rows, rows)
        total = block_sums(q, fresh[0], fresh[1])
        total += block_sums(q, kv_ref[slot, 0, stale, :], kv_ref[slot, 1, stale, :])
        total += block_sums(q, text_ref[0, :, head], text_ref[1, :, head])
        for j in range(1, n):
            there = lax.rem(slot + j, n)
            total += block_sums(q, kv_ref[there, 0], kv_ref[there, 1])
        out_ref[at, :] = total


def attend_local(core_slot, q, own, other, kv, text):
    rows, hd = q.shape
    return pl.pallas_call(
        local_kernel,
        in_specs=[SMEM] + [VMEM] * 5,
        out_specs=VMEM,
        out_shape=jax.ShapeDtypeStruct((rows, 2 * hd), F32),
        compiler_params=params(),
        name="attend_local",
    )(core_slot, q, own, other, kv, text)


def combine_kernel(local_ref, p1_ref, p2_ref, p3_ref, own_ref, other_ref):
    rows, hd = local_ref.shape[0], own_ref.shape[1]
    same = eye(hd)
    for i in range(rows // hd):
        at = slice(i * hd, (i + 1) * hd)
        summed = local_ref[at, :hd]
        totals = local_ref[at, hd:]
        line = None
        for p in (p1_ref, p2_ref, p3_ref):
            summed += p[at, :].astype(F32)
            pair = p[pl.ds(rows + 16 * i, 16), :].astype(F32)
            both = pair[0:1] + pair[8:9]
            line = both if line is None else line + both
        column = jnp.sum(jnp.broadcast_to(line, (hd, hd)) * same, 1, keepdims=True)
        done = (summed / (totals + column)).astype(BF)
        half = rows // 2
        for out_ref, start in ((own_ref, 0), (other_ref, half)):
            low, high = max(i * hd, start), min((i + 1) * hd, start + half)
            if low < high:
                out_ref[low - start : high - start, :] = done[low - i * hd : high - i * hd]


def combine(local, parts):
    rows, hd = local.shape[0], local.shape[1] // 2
    return pl.pallas_call(
        combine_kernel,
        in_specs=[VMEM] * 4,
        out_specs=[VMEM] * 2,
        out_shape=[jax.ShapeDtypeStruct((rows // 2, hd), BF)] * 2,
        compiler_params=params(),
        name="combine",
    )(local, *parts)


def spread_kernel(c_ref, kept_ref, swapped_ref, out_ref):
    n, rows, width = out_ref.shape
    hd = width // 2
    core = c_ref[0]
    mine = pl.ds(pl.multiple_of(core * hd, hd), hd)
    theirs = pl.ds(pl.multiple_of((1 - core) * hd, hd), hd)
    for i in range(n):
        out_ref[i, :, mine] = kept_ref[...]
        out_ref[i, :, theirs] = swapped_ref[...]


def spread(core, kept, swapped, n):
    rows, hd = kept.shape
    return pl.pallas_call(
        spread_kernel,
        in_specs=[SMEM, VMEM, VMEM],
        out_specs=VMEM,
        out_shape=jax.ShapeDtypeStruct((n, rows, 2 * hd), BF),
        compiler_params=params(),
        name="spread",
    )(core, kept, swapped)


def cut_kernel(x_ref, out_ref):
    out_ref[0] = x_ref[...]


def cut(x, n):
    rows, features = x.shape
    columns = features // n
    return pl.pallas_call(
        cut_kernel,
        grid=(n,),
        in_specs=[pl.BlockSpec((rows, columns), lambda i: (0, i))],
        out_specs=pl.BlockSpec((1, rows, columns), lambda i: (i, 0, 0)),
        out_shape=jax.ShapeDtypeStruct((n, rows, columns), BF),
        compiler_params=params(),
        name="cut",
    )(x)


def out_kernel(t_ref, a_ref, w_ref, image_ref, gate_ref, bias_ref, out_ref):
    n = a_ref.shape[0]
    acc = None
    for i in range(n):
        part = jnp.dot(a_ref[i], w_ref[i], preferred_element_type=F32)
        acc = part if acc is None else acc + part
    projection = acc + bias_ref[...]
    piece = (image_ref[...].astype(F32) + gate_ref[...] * projection).astype(BF)
    for i in range(n):
        out_ref[i] = piece


def project_out(tp, gathered, weight, image, gate, bias):
    n, rows, width = gathered.shape
    columns = weight.shape[2]
    return pl.pallas_call(
        out_kernel,
        grid_spec=pltpu.PrefetchScalarGridSpec(
            num_scalar_prefetch=1,
            grid=(1,),
            in_specs=[
                pl.BlockSpec((n, rows, width), lambda k, t: (0, 0, 0)),
                pl.BlockSpec((n, width, columns), lambda k, t: (0, 0, 0)),
                pl.BlockSpec((rows, columns), lambda k, t: (0, t[0])),
                pl.BlockSpec((1, columns), lambda k, t: (0, t[0])),
                pl.BlockSpec((1, columns), lambda k, t: (0, t[0])),
            ],
            out_specs=pl.BlockSpec((n, rows, columns), lambda k, t: (0, 0, 0)),
        ),
        out_shape=jax.ShapeDtypeStruct((n, rows, columns), BF),
        compiler_params=params(),
        name="project_out",
    )(tp, gathered, weight, image, gate, bias)


def shards(image, mod_shift, mod_scale, mod_gate, qkv_weight, qkv_bias, q_gain, k_gain, stale_kv, text_kv, out_weight, out_bias):
    hd = q_gain.shape[0]
    rows, features = image.shape
    n_patch = lax.axis_size("patch")
    n_tp = lax.axis_size("tp")
    patch = lax.axis_index("patch")
    tp = lax.axis_index("tp")
    core = patch % 2
    slot = (patch // 4) % 4
    core_at = jnp.stack([core, slot]).astype(jnp.int32)
    tp_at = tp.astype(jnp.int32).reshape(1)

    def flip(bits):
        return [(i, i ^ bits) for i in range(n_patch)]

    def send(x, perm):
        return lax.ppermute(x, "patch", perm)

    groups = [[(i & ~12) | (4 * j) for j in range(4)] for i in range(n_patch) if not i & 12]

    shift = mod_shift.reshape(1, -1)
    scale = mod_scale.reshape(1, -1)
    modulated, mine, theirs = prepare(core_at, image, shift, scale, stale_kv, hd)
    kv_chip = jnp.concatenate([mine, send(theirs, flip(1))], 1)
    kv = lax.all_gather(kv_chip, "patch", axis_index_groups=groups)

    other = send(modulated, flip(1))
    gains = (q_gain.reshape(1, -1), k_gain.reshape(1, -1))
    wide = jnp.transpose(qkv_weight, (1, 2, 0))
    q, kv_own, kv_other = project(core_at, modulated, other, wide, qkv_bias, *gains)

    hops = (2, 16, 18)
    partial = []
    for bits in hops:
        there = send(q, flip(bits))
        partial.append(send(attend_remote(there, kv), flip(bits)))
    local = attend_local(core_at, q, kv_own, kv_other, kv, text_kv)
    kept, leaving = combine(local, partial)

    back = send(kv_other, flip(1))
    first = core == 0
    fresh_kv = jnp.where(first, jnp.concatenate([kv_own, back], 2), jnp.concatenate([back, kv_own], 2))

    heads = spread(core_at, kept, send(leaving, flip(1)), n_tp)
    gathered = lax.all_to_all(heads, "tp", 0, 0)

    late_weight, _ = lax.optimization_barrier((out_weight, q))
    weight = lax.all_to_all(cut(late_weight, n_tp), "tp", 0, 0)
    pieces = project_out(tp_at, gathered, weight, image, mod_gate.reshape(1, -1), out_bias.reshape(1, -1))
    pieces = lax.all_to_all(pieces, "tp", 0, 0)
    mixed = pieces.swapaxes(0, 1).reshape(rows, features)
    return (mixed, fresh_kv)


def solution(mesh):
    placed = (
        P("patch", None),
        P(),
        P(),
        P(),
        P(None, None, "tp"),
        P(None, "tp"),
        P(),
        P(),
        P(None, "patch", "tp"),
        P(None, None, "tp"),
        P("tp", None),
        P(),
    )
    return jax.shard_map(
        shards,
        mesh=mesh,
        in_specs=placed,
        out_specs=(P("patch", None), P(None, "patch", "tp")),
        check_vma=False,
    )
```

time: 120 us -> 132 us (1.10)
  blocking collectives: 0 us -> 22.5 us
  starting transfers between devices: 37.6 us -> 23.2 us
  waiting for transfers between devices: 41.1 us -> 51.9 us
  Pallas kernels: 21.5 us -> 17.4 us
  local copies, waits for them, and re-layouts: 16.9 us -> 13.2 us
    all_gather x0 -> x1, blocking collectives: none -> 22.5 us  [shards(): kv = lax.all_gather(kv_chip, 'patch', axis_index_groups=groups)]
    all_to_all x3, waiting for transfers between devices: 28.3 us -> 46.7 us  [the longest x1 21.4 us: shards(): weight = lax.all_to_all(cut(late_weight, n_tp), 'tp', 0, 0)]
    ppermute x13 -> x10, starting transfers between devices: 23.4 us -> 11.5 us  [send(): return lax.ppermute(x, 'patch', perm)]
    ppermute x13 -> x10, waiting for transfers between devices: 12.8 us -> 5.26 us  [send(): return lax.ppermute(x, 'patch', perm)]
    pallas_call x7 -> x9, Pallas kernels: 20.9 us -> 16.7 us  [the longest x1 4.93 us: project(): pl.pallas_call(project_kernel, grid_spec=pltpu.PrefetchScalarGridSpec(num...]
    all_to_all x3, starting transfers between devices: 14.2 us -> 11.6 us  [the longest x1 4.33 us: shards(): gathered = lax.all_to_all(heads, 'tp', 0, 0)]
    broadcast_in_dim x2 -> x0, local copies, waits for them, and re-layouts: 2.05 us -> none  [the longest x1 1.12 us: shards(): jnp.broadcast_to(piece[None], (n_tp,) + piece.shape)]
    reshape x1 -> x0, local copies, waits for them, and re-layouts: 1.61 us -> none  [shards(): parts = out_weight.reshape(-1, n_tp, columns).swapaxes(0, 1)]
  transfers between devices with their start and end apart: 16 -> 13, of which waited for: 9 -> 7; matrix products, arithmetic and copies ran while one was open for 11% -> 6% of each run, Pallas kernels for 18% -> 7%
where the time goes in v2:
time: 132 us; the launch traced here: 130 us
  waiting for transfers between devices  51.9 us (39%)
  starting transfers between devices  23.2 us (18%)
  blocking collectives  22.5 us (17%)
  Pallas kernels  17.4 us (13%)
  local copies, waits for them, and re-layouts  13.2 us (10%)
    all_gather x1, blocking collectives, shards(): kv = lax.all_gather(kv_chip, 'patch', axis_index_groups=groups)  22.5 us
    all_to_all x1, waiting for transfers between devices, shards(): weight = lax.all_to_all(cut(late_weight, n_tp), 'tp', 0, 0)  21.4 us
    all_to_all x1, waiting for transfers between devices, shards(): pieces = lax.all_to_all(pieces, 'tp', 0, 0)  15 us
    unnamed x35, local copies, waits for them, and re-layouts  12 us
    ppermute x10, starting transfers between devices, send(): return lax.ppermute(x, 'patch', perm)  11.5 us
    all_to_all x1, waiting for transfers between devices, shards(): gathered = lax.all_to_all(heads, 'tp', 0, 0)  10.2 us
    ppermute x10, waiting for transfers between devices, send(): return lax.ppermute(x, 'patch', perm)  5.26 us
    pallas_call x1, Pallas kernels, project(): pl.pallas_call(project_kernel, grid_spec=pltpu.PrefetchScalarGridSpec(num...  4.93 us
  transfers between devices with their start and end apart: 13, of which 7 were waited for; matrix products, arithmetic and copies ran while one was open for 6% of the time, Pallas kernels for 7%

profile of v2, /device:TPU:32, one launch (start us, length us, event | category | flops | bytes accessed | tf_op | source)
XLA Modules:
  0.0 130.0 jit_solution(1377951514474249655)
XLA Ops:
  0.7 1.3 copy-done
  2.0 0.9 copy-done.7
  2.9 0.7 copy-done.10
  3.7 0.7 copy-done.11
  4.4 1.6 %prepare.1 = (bf16[192,3072]{1,0:T(8,128)(2,1)S(1)}, bf16[2,192,128]{2,1,0:T(8,128)(2,1)S(1)}, bf16[2,192,128]{2,1,0:T(8,128)(2,1)S(1)}) custom-call(s32[2]{0:T(128)S(1)} %pad_add_fusion.c_ref, bf16[192,3072]{1,0:T(8,128)(2,1)S(1)} %copy-done, f32[1,3072]{1,0:T(1,128)S(1)} %bitcast.18, f32[1,3072]{1,0:T(1,128)S(1)} %bitcast.19, ...), custom_call_target="tpu_custom_call" | custom-call | tf_op jit(solution)/shard_map/prepare/pallas_call | solution.py:38
  6.6 6.6 %copy.17 = bf16[3072,3,256]{0,2,1:T(8,128)(2,1)} copy(bf16[3072,3,256]{2,0,1:T(8,128)(2,1)} %param.16) | data formatting | bytes 9437184 | tf_op args[4]
  13.3 4.9 %project.1 = (bf16[384,128]{1,0:T(8,128)(2,1)S(1)}, bf16[2,192,128]{2,1,0:T(8,128)(2,1)S(1)}, bf16[2,192,128]{2,1,0:T(8,128)(2,1)S(1)}) custom-call(s32[2]{0:T(128)S(1)} %pad_add_fusion.c_ref, bf16[192,3072]{1,0:T(8,128)(2,1)S(1)} %get-tuple-element.11.own_ref, bf16[192,3072]{1,0:T(8,128)(2,1)S(1)} %collective-permute-done.other_ref, ...), custom_call_target="tpu_custom_call" | custom-call | tf_op jit(solution)/shard_map/project/pallas_call | solution.py:85
  18.3 2.8 %collective-permute-start.6 = (bf16[384,128]{1,0:T(8,128)(2,1)S(1)}, bf16[384,128]{1,0:T(8,128)(2,1)S(1)}, u32[]{:S(2)}, u32[]{:S(2)}) collective-permute-start(bf16[384,128]{1,0:T(8,128)(2,1)S(1)} %get-tuple-element.12.q_ref), channel_id=1, source_target_pairs={{0,144},{8,152},{16,128},{24,136},{32,176},{40,184},{48,160},{56,1... | collective-permute-start | bytes 294920 | tf_op jit(solution)/shard_map/ppermute | solution.py:310
  21.1 2.1 %collective-permute-start.4 = (bf16[384,128]{1,0:T(8,128)(2,1)S(1)}, bf16[384,128]{1,0:T(8,128)(2,1)S(1)}, u32[]{:S(2)}, u32[]{:S(2)}) collective-permute-start(bf16[384,128]{1,0:T(8,128)(2,1)S(1)} %get-tuple-element.12.q_ref), channel_id=1, source_target_pairs={{0,128},{8,136},{16,144},{24,152},{32,160},{40,168},{48,176},{56,1... | collective-permute-start | bytes 294920 | tf_op jit(solution)/shard_map/ppermute | solution.py:310
  23.3 22.5 %all-gather = bf16[8,384,128]{2,1,0:T(8,128)(2,1)S(1)} all-gather(bf16[2,384,128]{2,1,0:T(8,128)(2,1)S(1)} %pad_maximum_fusion), channel_id=2, replica_groups={{0,32,64,96},{8,40,72,104},{16,48,80,112},{24,56,88,120},{128,160,192,2..., dimensions={0}, use_global_device_ids=true | all-gather | bytes 983040 | tf_op jit(solution)/shard_map/all_gather | solution.py:318
  45.9 1.2 attend_remote.5
  47.1 3.5 %collective-permute-start.7 = (bf16[432,128]{1,0:T(8,128)(2,1)S(1)}, bf16[432,128]{1,0:T(8,128)(2,1)S(1)}, u32[]{:S(2)}, u32[]{:S(2)}) collective-permute-start(bf16[432,128]{1,0:T(8,128)(2,1)S(1)} %attend_remote.5), channel_id=1, source_target_pairs={{0,144},{8,152},{16,128},{24,136},{32,176},{40,184},{48,160},{56,1... | collective-permute-start | bytes 331784 | tf_op jit(solution)/shard_map/ppermute | solution.py:310
  50.6 1.2 attend_remote.4
  51.8 2.1 %collective-permute-start.5 = (bf16[432,128]{1,0:T(8,128)(2,1)S(1)}, bf16[432,128]{1,0:T(8,128)(2,1)S(1)}, u32[]{:S(2)}, u32[]{:S(2)}) collective-permute-start(bf16[432,128]{1,0:T(8,128)(2,1)S(1)} %attend_remote.4), channel_id=1, source_target_pairs={{0,128},{8,136},{16,144},{24,152},{32,160},{40,168},{48,176},{56,1... | collective-permute-start | bytes 331784 | tf_op jit(solution)/shard_map/ppermute | solution.py:310
  53.9 1.2 attend_remote.3
  55.2 1.9 %attend_local.1.local_ref = f32[384,256]{1,0:T(8,128)S(1)} custom-call(s32[2]{0:T(128)S(1)} %pad_add_fusion.c_ref, bf16[384,128]{1,0:T(8,128)(2,1)S(1)} %get-tuple-element.12.q_ref, bf16[2,192,128]{2,1,0:T(8,128)(2,1)S(1)} %get-tuple-element.13.own_ref, bf16[2,192,128]{2,1,0:T(8,128)(2,1)S(1)} %get-tuple-element.14.other_ref, ...), custom_call_target="tpu_custom_call" | custom-call | tf_op jit(solution)/shard_map/attend_local/pallas_call | solution.py:174
  57.2 0.9 collective-permute-done.5.p2_ref
  58.1 1.8 %collective-permute-done.3.p1_ref = bf16[432,128]{1,0:T(8,128)(2,1)S(1)} collective-permute-done((bf16[432,128]{1,0:T(8,128)(2,1)S(1)}, bf16[432,128]{1,0:T(8,128)(2,1)S(1)}, u32[]{:S(2)}, u32[]{:S(2)}) %collective-permute-start.3) | collective-permute-done | bytes 110624 | tf_op jit(solution)/shard_map/ppermute | solution.py:310
  60.2 1.2 collective-permute-done.8.swapped_ref
  61.4 1.5 %spread.1 = bf16[8,192,256]{2,1,0:T(8,128)(2,1)} custom-call(s32[2]{0:T(128)S(1)} %pad_add_fusion.c_ref, bf16[192,128]{1,0:T(8,128)(2,1)S(1)} %get-tuple-element.17.kept_ref, bf16[192,128]{1,0:T(8,128)(2,1)S(1)} %collective-permute-done.8.swapped_ref), custom_call_target="tpu_custom_call" | custom-call | tf_op jit(solution)/shard_map/spread/pallas_call | solution.py:231
  62.9 4.3 %all-to-all-start = ((bf16[8,192,256]{2,1,0:T(8,128)(2,1)}), bf16[8,192,256]{2,1,0:T(8,128)(2,1)S(1)}, u32[]{:S(2)}, u32[]{:S(2)}) async-start(bf16[8,192,256]{2,1,0:T(8,128)(2,1)} %spread.1), calls=%async_computation | async-start | bytes 1572864 | tf_op jit(solution)/shard_map/all_to_all | solution.py:338
  67.3 3.0 %cut.1 = bf16[8,256,384]{2,1,0:T(8,128)(2,1)} custom-call(bf16[256,3072]{1,0:T(8,128)(2,1)S(1)} %copy-done.3), custom_call_target="tpu_custom_call" | custom-call | tf_op jit(solution)/shard_map/cut/pallas_call | solution.py:248
  70.3 10.2 %all-to-all-done.a_ref = bf16[8,192,256]{2,1,0:T(8,128)(2,1)S(1)} async-done(((bf16[8,192,256]{2,1,0:T(8,128)(2,1)}), bf16[8,192,256]{2,1,0:T(8,128)(2,1)S(1)}, u32[]{:S(2)}, u32[]{:S(2)}) %all-to-all-start) | async-done | bytes 786464 | tf_op jit(solution)/shard_map/all_to_all | solution.py:338
  80.5 3.6 %all-to-all-start.1 = ((bf16[8,256,384]{2,1,0:T(8,128)(2,1)}), bf16[8,256,384]{2,1,0:T(8,128)(2,1)S(1)}, u32[]{:S(2)}, u32[]{:S(2)}) async-start(bf16[8,256,384]{2,1,0:T(8,128)(2,1)} %cut.1), calls=%async_computation.1 | async-start | bytes 3145728 | tf_op jit(solution)/shard_map/all_to_all | solution.py:341
  84.1 21.4 %all-to-all-done.1.w_ref = bf16[8,256,384]{2,1,0:T(8,128)(2,1)S(1)} async-done(((bf16[8,256,384]{2,1,0:T(8,128)(2,1)}), bf16[8,256,384]{2,1,0:T(8,128)(2,1)S(1)}, u32[]{:S(2)}, u32[]{:S(2)}) %all-to-all-start.1) | async-done | bytes 1572896 | tf_op jit(solution)/shard_map/all_to_all | solution.py:341
  105.5 0.7 copy-done.13
  106.9 1.0 copy-done.2
  107.9 3.7 %all-to-all-start.2 = ((bf16[8,192,384]{2,1,0:T(8,128)(2,1)}), bf16[8,192,384]{2,1,0:T(8,128)(2,1)S(1)}, u32[]{:S(2)}, u32[]{:S(2)}) async-start(bf16[8,192,384]{2,1,0:T(8,128)(2,1)} %copy-done.2), calls=%async_computation.2 | async-start | bytes 2359296 | tf_op jit(solution)/shard_map/all_to_all | solution.py:343
  111.7 1.3 collective-permute-done.9
  113.0 0.7 maximum_select_fusion
  113.7 15.0 %all-to-all-done.2 = bf16[8,192,384]{2,1,0:T(8,128)(2,1)S(1)} async-done(((bf16[8,192,384]{2,1,0:T(8,128)(2,1)}), bf16[8,192,384]{2,1,0:T(8,128)(2,1)S(1)}, u32[]{:S(2)}, u32[]{:S(2)}) %all-to-all-start.2) | async-done | bytes 1179680 | tf_op jit(solution)/shard_map/all_to_all | solution.py:343
  128.8 1.2 copy.19
  (44 shorter events, 2.0 us)
Async XLA Ops:
  0.7 1.3 copy-start
  2.0 0.9 copy-start.7
  2.9 0.7 copy-start.10
  3.6 0.7 copy-start.11
  6.0 7.3 %collective-permute-start = (bf16[192,3072]{1,0:T(8,128)(2,1)S(1)}, bf16[192,3072]{1,0:T(8,128)(2,1)S(1)}, u32[]{:S(2)}, u32[]{:S(2)}) collective-permute-start(bf16[192,3072]{1,0:T(8,128)(2,1)S(1)} %get-tuple-element.11.own_ref), channel_id=1, source_target_pairs={{0,8},{8,0},{16,24},{24,16},{32,40},{40,32},{48,56},{56,48},{64,72... | collective-permute-start | bytes 3538952 | tf_op jit(solution)/shard_map/ppermute | solution.py:310
  6.1 7.2 %copy-start.14 = (f32[3,256]{1,0:T(4,128)S(1)}, f32[3,256]{1,0:T(4,128)}, u32[]{:S(2)}) copy-start(f32[3,256]{1,0:T(4,128)} %bias_ref.1) | copy-start | bytes 9220
  6.1 7.2 %copy-start.15 = (f32[128]{0:T(128)S(1)}, f32[128]{0:T(128)}, u32[]{:S(2)}) copy-start(f32[128]{0:T(128)} %param.18) | copy-start | bytes 1540
  6.1 7.2 %copy-start.16 = (f32[128]{0:T(128)S(1)}, f32[128]{0:T(128)}, u32[]{:S(2)}) copy-start(f32[128]{0:T(128)} %param.19) | copy-start | bytes 1540
  6.1 7.1 %collective-permute-start.1 = (bf16[2,192,128]{2,1,0:T(8,128)(2,1)S(1)}, bf16[2,192,128]{2,1,0:T(8,128)(2,1)S(1)}, u32[]{:S(2)}, u32[]{:S(2)}) collective-permute-start(bf16[2,192,128]{2,1,0:T(8,128)(2,1)S(1)} %get-tuple-element.16), channel_id=1, source_target_pairs={{0,8},{8,0},{16,24},{24,16},{32,40},{40,32},{48,56},{56,48},{64,72... | collective-permute-start | bytes 294920 | tf_op jit(solution)/shard_map/ppermute | solution.py:310
  18.2 37.0 %copy-start.5 = (bf16[2,192,128]{2,1,0:T(8,128)(2,1)}, bf16[2,192,128]{2,1,0:T(8,128)(2,1)S(1)}, u32[]{:S(2)}) copy-start(bf16[2,192,128]{2,1,0:T(8,128)(2,1)S(1)} %get-tuple-element.13.own_ref) | copy-start | bytes 294916
  18.2 37.0 %copy-start.8 = (bf16[2,192,128]{2,1,0:T(8,128)(2,1)}, bf16[2,192,128]{2,1,0:T(8,128)(2,1)S(1)}, u32[]{:S(2)}) copy-start(bf16[2,192,128]{2,1,0:T(8,128)(2,1)S(1)} %get-tuple-element.14.other_ref) | copy-start | bytes 294916
  18.3 27.6 %collective-permute-start.6 = (bf16[384,128]{1,0:T(8,128)(2,1)S(1)}, bf16[384,128]{1,0:T(8,128)(2,1)S(1)}, u32[]{:S(2)}, u32[]{:S(2)}) collective-permute-start(bf16[384,128]{1,0:T(8,128)(2,1)S(1)} %get-tuple-element.12.q_ref), channel_id=1, source_target_pairs={{0,144},{8,152},{16,128},{24,136},{32,176},{40,184},{48,160},{56,1... | collective-permute-start | bytes 294920 | tf_op jit(solution)/shard_map/ppermute | solution.py:310
  21.1 29.5 %collective-permute-start.4 = (bf16[384,128]{1,0:T(8,128)(2,1)S(1)}, bf16[384,128]{1,0:T(8,128)(2,1)S(1)}, u32[]{:S(2)}, u32[]{:S(2)}) collective-permute-start(bf16[384,128]{1,0:T(8,128)(2,1)S(1)} %get-tuple-element.12.q_ref), channel_id=1, source_target_pairs={{0,128},{8,136},{16,144},{24,152},{32,160},{40,168},{48,176},{56,1... | collective-permute-start | bytes 294920 | tf_op jit(solution)/shard_map/ppermute | solution.py:310
  23.2 30.8 %collective-permute-start.2 = (bf16[384,128]{1,0:T(8,128)(2,1)S(1)}, bf16[384,128]{1,0:T(8,128)(2,1)S(1)}, u32[]{:S(2)}, u32[]{:S(2)}) collective-permute-start(bf16[384,128]{1,0:T(8,128)(2,1)S(1)} %get-tuple-element.12.q_ref), channel_id=1, source_target_pairs={{0,16},{8,24},{16,0},{24,8},{32,48},{40,56},{48,32},{56,40},{64,80... | collective-permute-start | bytes 294920 | tf_op jit(solution)/shard_map/ppermute | solution.py:310
  47.1 8.2 %copy-start.4 = (bf16[2,512,256]{2,1,0:T(8,128)(2,1)S(1)}, bf16[2,512,256]{2,1,0:T(8,128)(2,1)}, u32[]{:S(2)}) copy-start(bf16[2,512,256]{2,1,0:T(8,128)(2,1)} %text_ref.1) | copy-start | bytes 1572868
  47.1 10.1 %collective-permute-start.7 = (bf16[432,128]{1,0:T(8,128)(2,1)S(1)}, bf16[432,128]{1,0:T(8,128)(2,1)S(1)}, u32[]{:S(2)}, u32[]{:S(2)}) collective-permute-start(bf16[432,128]{1,0:T(8,128)(2,1)S(1)} %attend_remote.5), channel_id=1, source_target_pairs={{0,144},{8,152},{16,128},{24,136},{32,176},{40,184},{48,160},{56,1... | collective-permute-start | bytes 331784 | tf_op jit(solution)/shard_map/ppermute | solution.py:310
  51.8 6.3 %collective-permute-start.5 = (bf16[432,128]{1,0:T(8,128)(2,1)S(1)}, bf16[432,128]{1,0:T(8,128)(2,1)S(1)}, u32[]{:S(2)}, u32[]{:S(2)}) collective-permute-start(bf16[432,128]{1,0:T(8,128)(2,1)S(1)} %attend_remote.4), channel_id=1, source_target_pairs={{0,128},{8,136},{16,144},{24,152},{32,160},{40,168},{48,176},{56,1... | collective-permute-start | bytes 331784 | tf_op jit(solution)/shard_map/ppermute | solution.py:310
  55.1 4.8 %collective-permute-start.3 = (bf16[432,128]{1,0:T(8,128)(2,1)S(1)}, bf16[432,128]{1,0:T(8,128)(2,1)S(1)}, u32[]{:S(2)}, u32[]{:S(2)}) collective-permute-start(bf16[432,128]{1,0:T(8,128)(2,1)S(1)} %attend_remote.3), channel_id=1, source_target_pairs={{0,16},{8,24},{16,0},{24,8},{32,48},{40,56},{48,32},{56,40},{64,80... | collective-permute-start | bytes 331784 | tf_op jit(solution)/shard_map/ppermute | solution.py:310
  60.1 1.3 %collective-permute-start.8 = (bf16[192,128]{1,0:T(8,128)(2,1)S(1)}, bf16[192,128]{1,0:T(8,128)(2,1)S(1)}, u32[]{:S(2)}, u32[]{:S(2)}) collective-permute-start(bf16[192,128]{1,0:T(8,128)(2,1)S(1)} %get-tuple-element.18), channel_id=1, source_target_pairs={{0,8},{8,0},{16,24},{24,16},{32,40},{40,32},{48,56},{56,48},{64,72... | collective-permute-start | bytes 147464 | tf_op jit(solution)/shard_map/ppermute | solution.py:310
  61.4 5.9 %copy-start.3 = (bf16[256,3072]{1,0:T(8,128)(2,1)S(1)}, bf16[256,3072]{1,0:T(8,128)(2,1)}, u32[]{:S(2)}) copy-start(bf16[256,3072]{1,0:T(8,128)(2,1)} %x_ref) | copy-start | bytes 4718596
  62.9 17.6 %all-to-all-start = ((bf16[8,192,256]{2,1,0:T(8,128)(2,1)}), bf16[8,192,256]{2,1,0:T(8,128)(2,1)S(1)}, u32[]{:S(2)}, u32[]{:S(2)}) async-start(bf16[8,192,256]{2,1,0:T(8,128)(2,1)} %spread.1), calls=%async_computation | async-start | bytes 1572864 | tf_op jit(solution)/shard_map/all_to_all | solution.py:338
  70.3 35.2 %copy-start.1 = (bf16[192,3072]{1,0:T(8,128)(2,1)S(1)}, bf16[192,3072]{1,0:T(8,128)(2,1)}, u32[]{:S(2)}) copy-start(bf16[192,3072]{1,0:T(8,128)(2,1)} %image_ref.3) | copy-start | bytes 3538948
  70.3 35.2 %copy-start.12 = (f32[3072]{0:T(1024)S(1)}, f32[3072]{0:T(1024)}, u32[]{:S(2)}) copy-start(f32[3072]{0:T(1024)} %param.15) | copy-start | bytes 36868
  80.5 25.0 %all-to-all-start.1 = ((bf16[8,256,384]{2,1,0:T(8,128)(2,1)}), bf16[8,256,384]{2,1,0:T(8,128)(2,1)S(1)}, u32[]{:S(2)}, u32[]{:S(2)}) async-start(bf16[8,256,384]{2,1,0:T(8,128)(2,1)} %cut.1), calls=%async_computation.1 | async-start | bytes 3145728 | tf_op jit(solution)/shard_map/all_to_all | solution.py:341
  105.5 0.7 copy-start.13
  106.8 1.0 copy-start.2
  107.9 3.7 %copy-start.9 = (bf16[2,192,128]{2,1,0:T(8,128)(2,1)S(1)}, bf16[2,192,128]{2,1,0:T(8,128)(2,1)}, u32[]{:S(2)}) copy-start(bf16[2,192,128]{2,1,0:T(8,128)(2,1)} %copy-done.8) | copy-start | bytes 294916
  107.9 5.1 %copy-start.6 = (bf16[2,192,128]{2,1,0:T(8,128)(2,1)S(1)}, bf16[2,192,128]{2,1,0:T(8,128)(2,1)}, u32[]{:S(2)}) copy-start(bf16[2,192,128]{2,1,0:T(8,128)(2,1)} %copy-done.5) | copy-start | bytes 294916
  107.9 20.9 %all-to-all-start.2 = ((bf16[8,192,384]{2,1,0:T(8,128)(2,1)}), bf16[8,192,384]{2,1,0:T(8,128)(2,1)S(1)}, u32[]{:S(2)}, u32[]{:S(2)}) async-start(bf16[8,192,384]{2,1,0:T(8,128)(2,1)} %copy-done.2), calls=%async_computation.2 | async-start | bytes 2359296 | tf_op jit(solution)/shard_map/all_to_all | solution.py:343
  111.6 1.4 %collective-permute-start.9 = (bf16[2,192,128]{2,1,0:T(8,128)(2,1)S(1)}, bf16[2,192,128]{2,1,0:T(8,128)(2,1)S(1)}, u32[]{:S(2)}, u32[]{:S(2)}) collective-permute-start(bf16[2,192,128]{2,1,0:T(8,128)(2,1)S(1)} %copy-done.9), channel_id=1, source_target_pairs={{0,8},{8,0},{16,24},{24,16},{32,40},{40,32},{48,56},{56,48},{64,72... | collective-permute-start | bytes 294920 | tf_op jit(solution)/shard_map/ppermute | solution.py:310

commit v3 on v2

v3 whole, which is shorter than its diff:
```python
import math

import jax
import jax.numpy as jnp
from jax import lax
from jax.experimental import pallas as pl
from jax.experimental.pallas import tpu as pltpu
from jax.sharding import PartitionSpec as P

BF = jnp.bfloat16
F32 = jnp.float32
VMEM = pl.BlockSpec(memory_space=pltpu.VMEM)
SMEM = pl.BlockSpec(memory_space=pltpu.SMEM)
HBM = pl.BlockSpec(memory_space=pltpu.HBM)
ANY = pl.BlockSpec(memory_space=pl.ANY)
LIMIT = 48 * 1024 * 1024


def params(**kw):
    return pltpu.CompilerParams(vmem_limit_bytes=LIMIT, **kw)


def fetch(pairs, sems):
    copies = [pltpu.make_async_copy(src, dst, sems.at[i]) for i, (src, dst) in enumerate(pairs)]
    for copy in copies:
        copy.start()
    return copies


def copies_kernel(stale_ref, out_ref, sems):
    n, _, _, hd = out_ref.shape
    heads = stale_ref.shape[2] // hd
    copies = fetch([(stale_ref.at[:, :, pl.ds(i % heads * hd, hd)], out_ref.at[i]) for i in range(n)], sems)
    for copy in copies:
        copy.wait()


def copies_of(stale, n, hd):
    return pl.pallas_call(
        copies_kernel,
        in_specs=[HBM],
        out_specs=HBM,
        out_shape=jax.ShapeDtypeStruct((n,) + stale.shape[:2] + (hd,), BF),
        scratch_shapes=[pltpu.SemaphoreType.DMA((n,))],
        compiler_params=params(),
        name="copies_of",
    )(stale)


def modulate_kernel(image_ref, shift_ref, scale_ref, mod_ref, image, shift, scale, sems):
    copies = fetch([(shift_ref, shift), (scale_ref, scale)], sems)
    rows = image_ref.shape[0]
    parts = 4
    part = rows // parts
    blocks = [
        pltpu.make_async_copy(image_ref.at[pl.ds(j * part, part)], image.at[pl.ds(j * part, part)], sems.at[2 + j])
        for j in range(parts)
    ]
    for copy in blocks:
        copy.start()
    for copy in copies:
        copy.wait()
    step = 16
    for j in range(parts):
        blocks[j].wait()
        for i in range(j * part // step, (j + 1) * part // step):
            at = slice(i * step, (i + 1) * step)
            wide = image[at, :].astype(F32)
            average = jnp.mean(wide, -1, keepdims=True)
            centred = wide - average
            spread = jnp.mean(centred * centred, -1, keepdims=True)
            normed = centred * lax.rsqrt(spread + 1e-06)
            mod_ref[at, :] = (normed * (1.0 + scale[...]) + shift[...]).astype(BF)


def modulate(image, shift, scale):
    return pl.pallas_call(
        modulate_kernel,
        in_specs=[HBM] * 3,
        out_specs=VMEM,
        out_shape=jax.ShapeDtypeStruct(image.shape, BF),
        scratch_shapes=[
            pltpu.VMEM(image.shape, BF),
            pltpu.VMEM(shift.shape, F32),
            pltpu.VMEM(scale.shape, F32),
            pltpu.SemaphoreType.DMA((6,)),
        ],
        compiler_params=params(),
        name="modulate",
    )(image, shift, scale)


def project_kernel(c_ref, own_ref, other_ref, w_ref, bias_ref, q_gain_ref, k_gain_ref, q_ref, kv_own_ref, kv_other_ref, wide, sems):
    rows, features = own_ref.shape
    hd = q_gain_ref.shape[1]
    home = pl.ds(pl.multiple_of(c_ref[0] * hd, hd), hd)
    parts = 4
    depth = features // parts
    copies = []
    for k in range(parts):
        at = pl.ds(k * depth, depth)
        copies += fetch(
            [(w_ref.at[j, at, home], wide.at[at, pl.ds(j * hd, hd)]) for j in range(3)], sems.at[pl.ds(3 * k, 3)]
        )
    sums = [None, None]
    for k in range(parts):
        for copy in copies[3 * k : 3 * k + 3]:
            copy.wait()
        at = slice(k * depth, (k + 1) * depth)
        for i, m_ref in enumerate((own_ref, other_ref)):
            term = jnp.dot(m_ref[:, at], wide[at, :], preferred_element_type=F32)
            sums[i] = term if k == 0 else sums[i] + term

    def norm(part, gain):
        return part * lax.rsqrt(jnp.mean(part * part, -1, keepdims=True) + 1e-06) * gain

    for i, out_ref in enumerate((kv_own_ref, kv_other_ref)):
        q = sums[i][:, :hd] + bias_ref[0:1, home]
        q_ref[pl.ds(i * rows, rows), :] = norm(q, q_gain_ref[...]).astype(BF)
        out_ref[0] = norm(sums[i][:, hd : 2 * hd] + bias_ref[1:2, home], k_gain_ref[...]).astype(BF)
        out_ref[1] = (sums[i][:, 2 * hd :] + bias_ref[2:3, home]).astype(BF)


def project(core, own, other, weight, bias, q_gain, k_gain):
    rows, features = own.shape
    hd = q_gain.shape[1]
    return pl.pallas_call(
        project_kernel,
        in_specs=[SMEM, VMEM, VMEM, ANY, VMEM, VMEM, VMEM],
        out_specs=[VMEM] * 3,
        out_shape=[
            jax.ShapeDtypeStruct((2 * rows, hd), BF),
            jax.ShapeDtypeStruct((2, rows, hd), BF),
            jax.ShapeDtypeStruct((2, rows, hd), BF),
        ],
        scratch_shapes=[pltpu.VMEM((features, 3 * hd), BF), pltpu.SemaphoreType.DMA((12,))],
        compiler_params=params(),
        name="project",
    )(core, own, other, jnp.transpose(weight, (1, 0, 2)), bias, q_gain, k_gain)


def block_sums(q, k, v_ref_value):
    hd = q.shape[1]
    scores = lax.dot_general(q, k, (((1,), (1,)), ((), ())), preferred_element_type=F32)
    weights = jnp.exp2(scores * (math.log2(math.e) / math.sqrt(hd))).astype(BF)
    ones = jnp.ones_like(v_ref_value)
    return jnp.dot(weights, jnp.concatenate([v_ref_value, ones], 1), preferred_element_type=F32)


def eye(n):
    return (lax.broadcasted_iota(jnp.int32, (n, n), 0) == lax.broadcasted_iota(jnp.int32, (n, n), 1)).astype(F32)


def remote_kernel(q_ref, kv_ref, out_ref):
    rows, hd = q_ref.shape
    same = eye(hd)
    for i in range(rows // hd):
        at = slice(i * hd, (i + 1) * hd)
        q = q_ref[at, :]
        total = None
        for j in range(0, kv_ref.shape[0], 2):
            k, v = (kv_ref[j : j + 2, part].reshape(-1, hd) for part in (0, 1))
            part = block_sums(q, k, v)
            total = part if total is None else total + part
        out_ref[at, :] = total[:, :hd].astype(BF)
        line = jnp.sum(total[:, hd:] * same, 0, keepdims=True)
        high = line.astype(BF).astype(F32)
        out_ref[pl.ds(rows + 16 * i, 16), :] = jnp.concatenate(
            [jnp.broadcast_to(high, (8, hd)), jnp.broadcast_to(line - high, (8, hd))], 0
        ).astype(BF)


def attend_remote(q, kv):
    rows, hd = q.shape
    return pl.pallas_call(
        remote_kernel,
        in_specs=[VMEM] * 2,
        out_specs=VMEM,
        out_shape=jax.ShapeDtypeStruct((rows + 16 * (rows // hd), hd), BF),
        compiler_params=params(),
        name="attend_remote",
    )(q, kv)


def local_kernel(c_ref, q_ref, own_ref, other_ref, kv_ref, text_ref, out_ref):
    rows = own_ref.shape[1]
    hd = q_ref.shape[1]
    n = kv_ref.shape[0]
    core, chip = c_ref[0], c_ref[1]
    head = pl.ds(pl.multiple_of(core * hd, hd), hd)
    for i, fresh in enumerate((own_ref, other_ref)):
        at = pl.ds(i * rows, rows)
        q = q_ref[at, :]
        beside = 2 * chip + (1 - core if i == 0 else core)
        total = block_sums(q, fresh[0], fresh[1])
        total += block_sums(q, kv_ref[beside, 0], kv_ref[beside, 1])
        total += block_sums(q, text_ref[0, :, head], text_ref[1, :, head])
        for j in range(1, n // 2):
            there = pl.ds(2 * lax.rem(chip + j, n // 2), 2)
            k, v = (kv_ref[there, part].reshape(-1, hd) for part in (0, 1))
            total += block_sums(q, k, v)
        out_ref[at, :] = total


def attend_local(core_slot, q, own, other, kv, text):
    rows, hd = q.shape
    return pl.pallas_call(
        local_kernel,
        in_specs=[SMEM] + [VMEM] * 5,
        out_specs=VMEM,
        out_shape=jax.ShapeDtypeStruct((rows, 2 * hd), F32),
        compiler_params=params(),
        name="attend_local",
    )(core_slot, q, own, other, kv, text)


def combine_kernel(local_ref, p1_ref, p2_ref, p3_ref, own_ref, other_ref):
    rows, hd = local_ref.shape[0], own_ref.shape[1]
    same = eye(hd)
    for i in range(rows // hd):
        at = slice(i * hd, (i + 1) * hd)
        summed = local_ref[at, :hd]
        totals = local_ref[at, hd:]
        line = None
        for p in (p1_ref, p2_ref, p3_ref):
            summed += p[at, :].astype(F32)
            pair = p[pl.ds(rows + 16 * i, 16), :].astype(F32)
            both = pair[0:1] + pair[8:9]
            line = both if line is None else line + both
        column = jnp.sum(jnp.broadcast_to(line, (hd, hd)) * same, 1, keepdims=True)
        done = (summed / (totals + column)).astype(BF)
        half = rows // 2
        for out_ref, start in ((own_ref, 0), (other_ref, half)):
            low, high = max(i * hd, start), min((i + 1) * hd, start + half)
            if low < high:
                out_ref[low - start : high - start, :] = done[low - i * hd : high - i * hd]


def combine(local, parts):
    rows, hd = local.shape[0], local.shape[1] // 2
    return pl.pallas_call(
        combine_kernel,
        in_specs=[VMEM] * 4,
        out_specs=[VMEM] * 2,
        out_shape=[jax.ShapeDtypeStruct((rows // 2, hd), BF)] * 2,
        compiler_params=params(),
        name="combine",
    )(local, *parts)


def terms_kernel(c_ref, kept_ref, swapped_ref, w_ref, out_ref, heads, pieces, sems):
    n, rows, columns = out_ref.shape
    hd = kept_ref.shape[1]
    core = c_ref[0]
    heads[:, pl.ds(pl.multiple_of(core * hd, hd), hd)] = kept_ref[...]
    heads[:, pl.ds(pl.multiple_of((1 - core) * hd, hd), hd)] = swapped_ref[...]
    copies = []
    for i in range(n):
        pieces[i] = jnp.dot(heads[...], w_ref[:, i * columns : (i + 1) * columns], preferred_element_type=F32).astype(BF)
        copies += fetch([(pieces.at[i], out_ref.at[i])], sems.at[pl.ds(i, 1)])
    for copy in copies:
        copy.wait()


def terms_of(core, kept, swapped, weight, n):
    rows, hd = kept.shape
    shape = (n, rows, weight.shape[1] // n)
    return pl.pallas_call(
        terms_kernel,
        in_specs=[SMEM, VMEM, VMEM, VMEM],
        out_specs=HBM,
        out_shape=jax.ShapeDtypeStruct(shape, BF),
        scratch_shapes=[pltpu.VMEM((rows, weight.shape[0]), BF), pltpu.VMEM(shape, BF), pltpu.SemaphoreType.DMA((n,))],
        compiler_params=params(),
        name="terms_of",
    )(core, kept, swapped, weight)


def mix_kernel(t_ref, terms_ref, image_ref, gate_ref, bias_ref, out_ref, piece, sems):
    n = terms_ref.shape[0]
    projection = terms_ref[0].astype(F32)
    for i in range(1, n):
        projection += terms_ref[i].astype(F32)
    projection += bias_ref[...]
    piece[...] = (image_ref[...].astype(F32) + gate_ref[...] * projection).astype(BF)
    for copy in fetch([(piece, out_ref.at[i]) for i in range(n)], sems):
        copy.wait()


def mix(tp, terms, image, gate, bias):
    n, rows, columns = terms.shape
    return pl.pallas_call(
        mix_kernel,
        grid_spec=pltpu.PrefetchScalarGridSpec(
            num_scalar_prefetch=1,
            grid=(1,),
            in_specs=[
                pl.BlockSpec((n, rows, columns), lambda k, t: (0, 0, 0)),
                pl.BlockSpec((rows, columns), lambda k, t: (0, t[0])),
                pl.BlockSpec((1, columns), lambda k, t: (0, t[0])),
                pl.BlockSpec((1, columns), lambda k, t: (0, t[0])),
            ],
            out_specs=HBM,
            scratch_shapes=[pltpu.VMEM((rows, columns), BF), pltpu.SemaphoreType.DMA((n,))],
        ),
        out_shape=jax.ShapeDtypeStruct((n, rows, columns), BF),
        compiler_params=params(),
        name="mix",
    )(tp, terms, image, gate, bias)


def join_kernel(pieces_ref, out_ref, sems):
    n, _, columns = pieces_ref.shape
    copies = fetch([(pieces_ref.at[i], out_ref.at[:, pl.ds(i * columns, columns)]) for i in range(n)], sems)
    for copy in copies:
        copy.wait()


def join(pieces):
    n, rows, columns = pieces.shape
    return pl.pallas_call(
        join_kernel,
        in_specs=[ANY],
        out_specs=HBM,
        out_shape=jax.ShapeDtypeStruct((rows, n * columns), BF),
        scratch_shapes=[pltpu.SemaphoreType.DMA((n,))],
        compiler_params=params(),
        name="join",
    )(pieces)


def shards(image, mod_shift, mod_scale, mod_gate, qkv_weight, qkv_bias, q_gain, k_gain, stale_kv, text_kv, out_weight, out_bias):
    hd = q_gain.shape[0]
    rows, features = image.shape
    n_patch = lax.axis_size("patch")
    n_tp = lax.axis_size("tp")
    patch = lax.axis_index("patch")
    tp = lax.axis_index("tp")
    core = patch % 2
    slot = (patch // 4) % 4
    core_at = jnp.stack([core, slot]).astype(jnp.int32)
    tp_at = tp.astype(jnp.int32).reshape(1)

    def flip(bits):
        return [(i, i ^ bits) for i in range(n_patch)]

    def send(x, perm):
        return lax.ppermute(x, "patch", perm)

    groups = [[i | 4 * j | c for j in range(4) for c in (0, 1)] for i in range(n_patch) if not i & 13]

    modulated = modulate(image, mod_shift.reshape(1, -1), mod_scale.reshape(1, -1))
    other = send(modulated, flip(1))
    copies = copies_of(stale_kv, len(groups[0]), hd)
    kv = lax.all_to_all(copies, "patch", 0, 0, axis_index_groups=groups)
    gains = (q_gain.reshape(1, -1), k_gain.reshape(1, -1))
    q, kv_own, kv_other = project(core_at, modulated, other, qkv_weight, qkv_bias, *gains)

    hops = (2, 16, 18)
    partial = []
    for bits in hops:
        there = send(q, flip(bits))
        partial.append(send(attend_remote(there, kv), flip(bits)))
    local = attend_local(core_at, q, kv_own, kv_other, kv, text_kv)
    kept, leaving = combine(local, partial)

    back = send(kv_other, flip(1))
    first = core == 0
    fresh_kv = jnp.where(first, jnp.concatenate([kv_own, back], 2), jnp.concatenate([back, kv_own], 2))

    terms = terms_of(core_at, kept, send(leaving, flip(1)), out_weight, n_tp)
    terms = lax.all_to_all(terms, "tp", 0, 0)
    pieces = mix(tp_at, terms, image, mod_gate.reshape(1, -1), out_bias.reshape(1, -1))
    mixed = join(lax.all_to_all(pieces, "tp", 0, 0))
    return (mixed, fresh_kv)


def solution(mesh):
    placed = (
        P("patch", None),
        P(),
        P(),
        P(),
        P(None, None, "tp"),
        P(None, "tp"),
        P(),
        P(),
        P(None, "patch", "tp"),
        P(None, None, "tp"),
        P("tp", None),
        P(),
    )
    return jax.shard_map(
        shards,
        mesh=mesh,
        in_specs=placed,
        out_specs=(P("patch", None), P(None, "patch", "tp")),
        check_vma=False,
    )
```

time: 132 us -> 99.8 us (0.76)
  blocking collectives: 22.5 us -> 0 us
  local copies, waits for them, and re-layouts: 13.2 us -> 1.07 us
  starting transfers between devices: 23.2 us -> 26.7 us
    all_gather x1 -> x0, blocking collectives: 22.5 us -> none  [shards(): kv = lax.all_gather(kv_chip, 'patch', axis_index_groups=groups)]
    unnamed x35 -> x22, local copies, waits for them, and re-layouts: 12 us -> 1.07 us
    all_to_all x3, waiting for transfers between devices: 46.7 us -> 36.2 us  [the longest x1 17.4 us: shards(): terms = lax.all_to_all(terms, 'tp', 0, 0)]
    ppermute x10 -> x9, waiting for transfers between devices: 5.26 us -> 15.3 us  [send(): return lax.ppermute(x, 'patch', perm)]
    all_to_all x3, starting transfers between devices: 11.6 us -> 15.6 us  [the longest x1 7.58 us: shards(): kv = lax.all_to_all(copies, 'patch', 0, 0, axis_index_groups=groups)]
    ppermute x10 -> x9, starting transfers between devices: 11.5 us -> 11.1 us  [send(): return lax.ppermute(x, 'patch', perm)]
    pallas_call x5 -> x6, Pallas kernels: 11.7 us -> 11.3 us  [the longest x1 4.52 us: project(): pl.pallas_call(project_kernel, in_specs=[SMEM, VMEM, VMEM, ANY, VMEM, VME...]
  transfers between devices with their start and end apart: 13 -> 12, of which waited for: 7 -> 8; matrix products, arithmetic and copies ran while one was open for 6% -> 1% of each run, Pallas kernels for 7% -> 12%
where the time goes in v3:
time: 99.8 us; the launch traced here: 97.8 us
  waiting for transfers between devices  51.5 us (52%)
  starting transfers between devices  26.7 us (27%)
  Pallas kernels  16.9 us (17%)
  local copies, waits for them, and re-layouts  1.07 us (1%)
    all_to_all x1, waiting for transfers between devices, shards(): terms = lax.all_to_all(terms, 'tp', 0, 0)  17.4 us
    ppermute x9, waiting for transfers between devices, send(): return lax.ppermute(x, 'patch', perm)  15.3 us
    all_to_all x1, waiting for transfers between devices, shards(): mixed = join(lax.all_to_all(pieces, 'tp', 0, 0))  15.1 us
    ppermute x9, starting transfers between devices, send(): return lax.ppermute(x, 'patch', perm)  11.1 us
    all_to_all x1, starting transfers between devices, shards(): kv = lax.all_to_all(copies, 'patch', 0, 0, axis_index_groups=groups)  7.58 us
    pallas_call x1, Pallas kernels, project(): pl.pallas_call(project_kernel, in_specs=[SMEM, VMEM, VMEM, ANY, VMEM, VME...  4.52 us
    all_to_all x1, starting transfers between devices, shards(): terms = lax.all_to_all(terms, 'tp', 0, 0)  4.42 us
    all_to_all x1, waiting for transfers between devices, shards(): kv = lax.all_to_all(copies, 'patch', 0, 0, axis_index_groups=groups)  3.66 us
  transfers between devices with their start and end apart: 12, of which 8 were waited for; matrix products, arithmetic and copies ran while one was open for 1% of the time, Pallas kernels for 12%

profile of v3, /device:TPU:32, one launch (start us, length us, event | category | flops | bytes accessed | tf_op | source)
XLA Modules:
  0.0 97.8 jit_solution(2007609981784717542)
XLA Ops:
  0.7 1.0 %copy-done.3 = bf16[2,192,256]{2,1,0:T(8,128)(2,1)S(1)} copy-done((bf16[2,192,256]{2,1,0:T(8,128)(2,1)S(1)}, bf16[2,192,256]{2,1,0:T(8,128)(2,1)}, u32[]{:S(2)}) %copy-start.3) | copy-done | bytes 196632
  1.7 0.9 copies_of.1
  2.6 7.6 %all-to-all-start = ((bf16[8,2,192,128]{3,2,1,0:T(8,128)(2,1)}), bf16[8,2,192,128]{3,2,1,0:T(8,128)(2,1)S(1)}, u32[]{:S(2)}, u32[]{:S(2)}) async-start(bf16[8,2,192,128]{3,2,1,0:T(8,128)(2,1)} %copies_of.1), calls=%async_computation | async-start | bytes 1572864 | tf_op jit(solution)/shard_map/all_to_all | solution.py:355
  10.3 1.6 %modulate.1.own_ref = bf16[192,3072]{1,0:T(8,128)(2,1)S(1)} custom-call(bf16[192,3072]{1,0:T(8,128)(2,1)S(1)} %copy-done, f32[1,3072]{1,0:T(1,128)S(1)} %bitcast.10, f32[1,3072]{1,0:T(1,128)S(1)} %bitcast.11), custom_call_target="tpu_custom_call" | custom-call | tf_op jit(solution)/shard_map/modulate/pallas_call | solution.py:77
  11.8 0.6 collective-permute-start
  12.5 2.5 %collective-permute-done.other_ref = bf16[192,3072]{1,0:T(8,128)(2,1)} collective-permute-done((bf16[192,3072]{1,0:T(8,128)(2,1)S(1)}, bf16[192,3072]{1,0:T(8,128)(2,1)}, u32[]{:S(2)}, u32[]{:S(2)}) %collective-permute-start) | collective-permute-done | bytes 1179680 | tf_op jit(solution)/shard_map/ppermute | solution.py:348
  15.0 4.5 %project.1 = (bf16[384,128]{1,0:T(8,128)(2,1)S(1)}, bf16[2,192,128]{2,1,0:T(8,128)(2,1)S(1)}, bf16[2,192,128]{2,1,0:T(8,128)(2,1)S(1)}) custom-call(s32[2]{0:T(128)S(1)} %pad_add_fusion.c_ref, bf16[192,3072]{1,0:T(8,128)(2,1)S(1)} %modulate.1.own_ref, bf16[192,3072]{1,0:T(8,128)(2,1)} %collective-permute-done.other_ref, bf16[3,3072,256]{2,1,0:T(8,128)(2,1)} %bitcast.16, ...), custom_call_target="tpu_custom_call" | custom-call | tf_op jit(solution)/shard_map/project/pallas_call | solution.py:127
  19.5 1.1 %collective-permute-start.1 = (bf16[384,128]{1,0:T(8,128)(2,1)S(1)}, bf16[384,128]{1,0:T(8,128)(2,1)S(1)}, u32[]{:S(2)}, u32[]{:S(2)}) collective-permute-start(bf16[384,128]{1,0:T(8,128)(2,1)S(1)} %get-tuple-element.7.q_ref), channel_id=1, source_target_pairs={{0,16},{8,24},{16,0},{24,8},{32,48},{40,56},{48,32},{56,40},{64,80... | collective-permute-start | bytes 294920 | tf_op jit(solution)/shard_map/ppermute | solution.py:348
  20.7 3.2 %collective-permute-start.3 = (bf16[384,128]{1,0:T(8,128)(2,1)S(1)}, bf16[384,128]{1,0:T(8,128)(2,1)S(1)}, u32[]{:S(2)}, u32[]{:S(2)}) collective-permute-start(bf16[384,128]{1,0:T(8,128)(2,1)S(1)} %get-tuple-element.7.q_ref), channel_id=1, source_target_pairs={{0,128},{8,136},{16,144},{24,152},{32,160},{40,168},{48,176},{56,1... | collective-permute-start | bytes 294920 | tf_op jit(solution)/shard_map/ppermute | solution.py:348
  23.8 0.8 collective-permute-start.5
  24.6 5.8 %collective-permute-done.1.q_ref = bf16[384,128]{1,0:T(8,128)(2,1)S(1)} collective-permute-done((bf16[384,128]{1,0:T(8,128)(2,1)S(1)}, bf16[384,128]{1,0:T(8,128)(2,1)S(1)}, u32[]{:S(2)}, u32[]{:S(2)}) %collective-permute-start.1) | collective-permute-done | bytes 98336 | tf_op jit(solution)/shard_map/ppermute | solution.py:348
  30.5 3.7 %all-to-all-done.kv_ref = bf16[8,2,192,128]{3,2,1,0:T(8,128)(2,1)S(1)} async-done(((bf16[8,2,192,128]{3,2,1,0:T(8,128)(2,1)}), bf16[8,2,192,128]{3,2,1,0:T(8,128)(2,1)S(1)}, u32[]{:S(2)}, u32[]{:S(2)}) %all-to-all-start) | async-done | bytes 786464 | tf_op jit(solution)/shard_map/all_to_all | solution.py:355
  34.1 1.2 %attend_remote.3 = bf16[432,128]{1,0:T(8,128)(2,1)S(1)} custom-call(bf16[384,128]{1,0:T(8,128)(2,1)S(1)} %collective-permute-done.1.q_ref, bf16[8,2,192,128]{3,2,1,0:T(8,128)(2,1)S(1)} %all-to-all-done.kv_ref), custom_call_target="tpu_custom_call" | custom-call | tf_op jit(solution)/shard_map/attend_remote/pallas_call | solution.py:175
  35.3 1.2 %collective-permute-start.2 = (bf16[432,128]{1,0:T(8,128)(2,1)S(1)}, bf16[432,128]{1,0:T(8,128)(2,1)S(1)}, u32[]{:S(2)}, u32[]{:S(2)}) collective-permute-start(bf16[432,128]{1,0:T(8,128)(2,1)S(1)} %attend_remote.3), channel_id=1, source_target_pairs={{0,16},{8,24},{16,0},{24,8},{32,48},{40,56},{48,32},{56,40},{64,80... | collective-permute-start | bytes 331784 | tf_op jit(solution)/shard_map/ppermute | solution.py:348
  36.5 1.2 %attend_remote.4 = bf16[432,128]{1,0:T(8,128)(2,1)S(1)} custom-call(bf16[384,128]{1,0:T(8,128)(2,1)S(1)} %collective-permute-done.3.q_ref, bf16[8,2,192,128]{3,2,1,0:T(8,128)(2,1)S(1)} %all-to-all-done.kv_ref), custom_call_target="tpu_custom_call" | custom-call | tf_op jit(solution)/shard_map/attend_remote/pallas_call | solution.py:175
  37.7 3.3 %collective-permute-start.4 = (bf16[432,128]{1,0:T(8,128)(2,1)S(1)}, bf16[432,128]{1,0:T(8,128)(2,1)S(1)}, u32[]{:S(2)}, u32[]{:S(2)}) collective-permute-start(bf16[432,128]{1,0:T(8,128)(2,1)S(1)} %attend_remote.4), channel_id=1, source_target_pairs={{0,128},{8,136},{16,144},{24,152},{32,160},{40,168},{48,176},{56,1... | collective-permute-start | bytes 331784 | tf_op jit(solution)/shard_map/ppermute | solution.py:348
  41.0 1.2 %attend_remote.5 = bf16[432,128]{1,0:T(8,128)(2,1)S(1)} custom-call(bf16[384,128]{1,0:T(8,128)(2,1)S(1)} %collective-permute-done.5.q_ref, bf16[8,2,192,128]{3,2,1,0:T(8,128)(2,1)S(1)} %all-to-all-done.kv_ref), custom_call_target="tpu_custom_call" | custom-call | tf_op jit(solution)/shard_map/attend_remote/pallas_call | solution.py:175
  42.2 0.8 collective-permute-start.6
  43.0 1.9 %attend_local.1.local_ref = f32[384,256]{1,0:T(8,128)S(1)} custom-call(s32[2]{0:T(128)S(1)} %pad_add_fusion.c_ref, bf16[384,128]{1,0:T(8,128)(2,1)S(1)} %get-tuple-element.7.q_ref, bf16[2,192,128]{2,1,0:T(8,128)(2,1)S(1)} %get-tuple-element.8.own_ref, bf16[2,192,128]{2,1,0:T(8,128)(2,1)S(1)} %get-tuple-element.9.other_ref, ...), custom_call_target="tpu_custom_call" | custom-call | tf_op jit(solution)/shard_map/attend_local/pallas_call | solution.py:207
  45.0 4.4 %collective-permute-done.6.p3_ref = bf16[432,128]{1,0:T(8,128)(2,1)S(1)} collective-permute-done((bf16[432,128]{1,0:T(8,128)(2,1)S(1)}, bf16[432,128]{1,0:T(8,128)(2,1)S(1)}, u32[]{:S(2)}, u32[]{:S(2)}) %collective-permute-start.6) | collective-permute-done | bytes 110624 | tf_op jit(solution)/shard_map/ppermute | solution.py:348
  49.4 0.1 combine.1
  49.6 0.1 collective-permute-start.7
  49.7 1.2 %collective-permute-done.7.swapped_ref = bf16[192,128]{1,0:T(8,128)(2,1)S(1)} collective-permute-done((bf16[192,128]{1,0:T(8,128)(2,1)S(1)}, bf16[192,128]{1,0:T(8,128)(2,1)S(1)}, u32[]{:S(2)}, u32[]{:S(2)}) %collective-permute-start.7) | collective-permute-done | bytes 49184 | tf_op jit(solution)/shard_map/ppermute | solution.py:348
  50.9 1.8 %terms_of.1 = bf16[8,192,384]{2,1,0:T(8,128)(2,1)} custom-call(s32[2]{0:T(128)S(1)} %pad_add_fusion.c_ref, bf16[192,128]{1,0:T(8,128)(2,1)S(1)} %get-tuple-element.10.kept_ref, bf16[192,128]{1,0:T(8,128)(2,1)S(1)} %collective-permute-done.7.swapped_ref, bf16[256,3072]{1,0:T(8,128)(2,1)S(1)} %copy-done.1), custom_call_target="tpu_custom_call" | custom-call | tf_op jit(solution)/shard_map/terms_of/pallas_call | solution.py:268
  52.8 4.4 %all-to-all-start.1 = ((bf16[8,192,384]{2,1,0:T(8,128)(2,1)}), bf16[8,192,384]{2,1,0:T(8,128)(2,1)S(1)}, u32[]{:S(2)}, u32[]{:S(2)}) async-start(bf16[8,192,384]{2,1,0:T(8,128)(2,1)} %terms_of.1), calls=%async_computation.1 | async-start | bytes 2359296 | tf_op jit(solution)/shard_map/all_to_all | solution.py:372
  57.2 17.4 %all-to-all-done.1.terms_ref = bf16[8,192,384]{2,1,0:T(8,128)(2,1)S(1)} async-done(((bf16[8,192,384]{2,1,0:T(8,128)(2,1)}), bf16[8,192,384]{2,1,0:T(8,128)(2,1)S(1)}, u32[]{:S(2)}, u32[]{:S(2)}) %all-to-all-start.1) | async-done | bytes 1179680 | tf_op jit(solution)/shard_map/all_to_all | solution.py:372
  74.6 1.4 %mix.1 = bf16[8,192,384]{2,1,0:T(8,128)(2,1)} custom-call(s32[1]{0:T(128)} %bitcast.t_ref, bf16[8,192,384]{2,1,0:T(8,128)(2,1)S(1)} %all-to-all-done.1.terms_ref, bf16[192,3072]{1,0:T(8,128)(2,1)S(1)} %copy-done, f32[1,3072]{1,0:T(1,128)S(1)} %bitcast.12, f32[1,3072]{1,0:T(1,128)S(1)} %bitcast.13), custom_call_target="tpu_custom_call" | custom-call | tf_op jit(solution)/shard_map/mix/pallas_call | solution.py:292
  76.0 3.6 %all-to-all-start.2 = ((bf16[8,192,384]{2,1,0:T(8,128)(2,1)}), bf16[8,192,384]{2,1,0:T(8,128)(2,1)S(1)}, u32[]{:S(2)}, u32[]{:S(2)}) async-start(bf16[8,192,384]{2,1,0:T(8,128)(2,1)} %mix.1), calls=%async_computation.2 | async-start | bytes 2359296 | tf_op jit(solution)/shard_map/all_to_all | solution.py:374
  79.7 1.3 %collective-permute-done.8 = bf16[2,192,128]{2,1,0:T(8,128)(2,1)S(1)} collective-permute-done((bf16[2,192,128]{2,1,0:T(8,128)(2,1)S(1)}, bf16[2,192,128]{2,1,0:T(8,128)(2,1)S(1)}, u32[]{:S(2)}, u32[]{:S(2)}) %collective-permute-start.8) | collective-permute-done | bytes 98336 | tf_op jit(solution)/shard_map/ppermute | solution.py:348
  81.0 0.7 maximum_select_fusion
  81.7 15.1 %all-to-all-done.2.pieces_ref = bf16[8,192,384]{2,1,0:T(8,128)(2,1)S(1)} async-done(((bf16[8,192,384]{2,1,0:T(8,128)(2,1)}), bf16[8,192,384]{2,1,0:T(8,128)(2,1)S(1)}, u32[]{:S(2)}, u32[]{:S(2)}) %all-to-all-start.2) | async-done | bytes 1179680 | tf_op jit(solution)/shard_map/all_to_all | solution.py:374
  96.8 1.1 %join.1 = bf16[192,3072]{1,0:T(8,128)(2,1)} custom-call(bf16[8,192,384]{2,1,0:T(8,128)(2,1)S(1)} %all-to-all-done.2.pieces_ref), custom_call_target="tpu_custom_call" | custom-call | tf_op jit(solution)/shard_map/join/pallas_call | solution.py:321
  (27 shorter events, 0.2 us)
Async XLA Ops:
  0.6 9.6 %copy-start = (bf16[192,3072]{1,0:T(8,128)(2,1)S(1)}, bf16[192,3072]{1,0:T(8,128)(2,1)}, u32[]{:S(2)}) copy-start(bf16[192,3072]{1,0:T(8,128)(2,1)} %image_ref.3) | copy-start | bytes 3538948
  0.6 1.0 %copy-start.3 = (bf16[2,192,256]{2,1,0:T(8,128)(2,1)S(1)}, bf16[2,192,256]{2,1,0:T(8,128)(2,1)}, u32[]{:S(2)}) copy-start(bf16[2,192,256]{2,1,0:T(8,128)(2,1)} %stale_ref.1) | copy-start | bytes 589828
  1.7 8.5 %copy-start.4 = (f32[3072]{0:T(1024)S(1)}, f32[3072]{0:T(1024)}, u32[]{:S(2)}) copy-start(f32[3072]{0:T(1024)} %param.13) | copy-start | bytes 36868
  1.7 8.5 %copy-start.5 = (f32[3072]{0:T(1024)S(1)}, f32[3072]{0:T(1024)}, u32[]{:S(2)}) copy-start(f32[3072]{0:T(1024)} %param.14) | copy-start | bytes 36868
  2.6 31.5 %all-to-all-start = ((bf16[8,2,192,128]{3,2,1,0:T(8,128)(2,1)}), bf16[8,2,192,128]{3,2,1,0:T(8,128)(2,1)S(1)}, u32[]{:S(2)}, u32[]{:S(2)}) async-start(bf16[8,2,192,128]{3,2,1,0:T(8,128)(2,1)} %copies_of.1), calls=%async_computation | async-start | bytes 1572864 | tf_op jit(solution)/shard_map/all_to_all | solution.py:355
  10.2 4.8 %copy-start.8 = (f32[3,256]{1,0:T(4,128)S(1)}, f32[3,256]{1,0:T(4,128)}, u32[]{:S(2)}) copy-start(f32[3,256]{1,0:T(4,128)} %bias_ref.1) | copy-start | bytes 9220
  10.2 4.8 %copy-start.9 = (f32[128]{0:T(128)S(1)}, f32[128]{0:T(128)}, u32[]{:S(2)}) copy-start(f32[128]{0:T(128)} %param.18) | copy-start | bytes 1540
  10.2 4.8 %copy-start.10 = (f32[128]{0:T(128)S(1)}, f32[128]{0:T(128)}, u32[]{:S(2)}) copy-start(f32[128]{0:T(128)} %param.19) | copy-start | bytes 1540
  11.8 3.2 %collective-permute-start = (bf16[192,3072]{1,0:T(8,128)(2,1)S(1)}, bf16[192,3072]{1,0:T(8,128)(2,1)}, u32[]{:S(2)}, u32[]{:S(2)}) collective-permute-start(bf16[192,3072]{1,0:T(8,128)(2,1)S(1)} %modulate.1.own_ref), channel_id=1, source_target_pairs={{0,8},{8,0},{16,24},{24,16},{32,40},{40,32},{48,56},{56,48},{64,72... | collective-permute-start | bytes 3538952 | tf_op jit(solution)/shard_map/ppermute | solution.py:348
  19.5 10.9 %collective-permute-start.1 = (bf16[384,128]{1,0:T(8,128)(2,1)S(1)}, bf16[384,128]{1,0:T(8,128)(2,1)S(1)}, u32[]{:S(2)}, u32[]{:S(2)}) collective-permute-start(bf16[384,128]{1,0:T(8,128)(2,1)S(1)} %get-tuple-element.7.q_ref), channel_id=1, source_target_pairs={{0,16},{8,24},{16,0},{24,8},{32,48},{40,56},{48,32},{56,40},{64,80... | collective-permute-start | bytes 294920 | tf_op jit(solution)/shard_map/ppermute | solution.py:348
  20.7 15.8 %collective-permute-start.3 = (bf16[384,128]{1,0:T(8,128)(2,1)S(1)}, bf16[384,128]{1,0:T(8,128)(2,1)S(1)}, u32[]{:S(2)}, u32[]{:S(2)}) collective-permute-start(bf16[384,128]{1,0:T(8,128)(2,1)S(1)} %get-tuple-element.7.q_ref), channel_id=1, source_target_pairs={{0,128},{8,136},{16,144},{24,152},{32,160},{40,168},{48,176},{56,1... | collective-permute-start | bytes 294920 | tf_op jit(solution)/shard_map/ppermute | solution.py:348
  23.8 17.1 %collective-permute-start.5 = (bf16[384,128]{1,0:T(8,128)(2,1)S(1)}, bf16[384,128]{1,0:T(8,128)(2,1)S(1)}, u32[]{:S(2)}, u32[]{:S(2)}) collective-permute-start(bf16[384,128]{1,0:T(8,128)(2,1)S(1)} %get-tuple-element.7.q_ref), channel_id=1, source_target_pairs={{0,144},{8,152},{16,128},{24,136},{32,176},{40,184},{48,160},{56,1... | collective-permute-start | bytes 294920 | tf_op jit(solution)/shard_map/ppermute | solution.py:348
  35.3 7.7 %copy-start.2 = (bf16[2,512,256]{2,1,0:T(8,128)(2,1)S(1)}, bf16[2,512,256]{2,1,0:T(8,128)(2,1)}, u32[]{:S(2)}) copy-start(bf16[2,512,256]{2,1,0:T(8,128)(2,1)} %text_ref.1) | copy-start | bytes 1572868
  35.3 9.6 %collective-permute-start.2 = (bf16[432,128]{1,0:T(8,128)(2,1)S(1)}, bf16[432,128]{1,0:T(8,128)(2,1)S(1)}, u32[]{:S(2)}, u32[]{:S(2)}) collective-permute-start(bf16[432,128]{1,0:T(8,128)(2,1)S(1)} %attend_remote.3), channel_id=1, source_target_pairs={{0,16},{8,24},{16,0},{24,8},{32,48},{40,56},{48,32},{56,40},{64,80... | collective-permute-start | bytes 331784 | tf_op jit(solution)/shard_map/ppermute | solution.py:348
  37.7 7.3 %collective-permute-start.4 = (bf16[432,128]{1,0:T(8,128)(2,1)S(1)}, bf16[432,128]{1,0:T(8,128)(2,1)S(1)}, u32[]{:S(2)}, u32[]{:S(2)}) collective-permute-start(bf16[432,128]{1,0:T(8,128)(2,1)S(1)} %attend_remote.4), channel_id=1, source_target_pairs={{0,128},{8,136},{16,144},{24,152},{32,160},{40,168},{48,176},{56,1... | collective-permute-start | bytes 331784 | tf_op jit(solution)/shard_map/ppermute | solution.py:348
  42.2 7.2 %collective-permute-start.6 = (bf16[432,128]{1,0:T(8,128)(2,1)S(1)}, bf16[432,128]{1,0:T(8,128)(2,1)S(1)}, u32[]{:S(2)}, u32[]{:S(2)}) collective-permute-start(bf16[432,128]{1,0:T(8,128)(2,1)S(1)} %attend_remote.5), channel_id=1, source_target_pairs={{0,144},{8,152},{16,128},{24,136},{32,176},{40,184},{48,160},{56,1... | collective-permute-start | bytes 331784 | tf_op jit(solution)/shard_map/ppermute | solution.py:348
  43.0 7.9 %copy-start.1 = (bf16[256,3072]{1,0:T(8,128)(2,1)S(1)}, bf16[256,3072]{1,0:T(8,128)(2,1)}, u32[]{:S(2)}) copy-start(bf16[256,3072]{1,0:T(8,128)(2,1)} %w_ref.1) | copy-start | bytes 4718596
  49.6 1.3 %collective-permute-start.7 = (bf16[192,128]{1,0:T(8,128)(2,1)S(1)}, bf16[192,128]{1,0:T(8,128)(2,1)S(1)}, u32[]{:S(2)}, u32[]{:S(2)}) collective-permute-start(bf16[192,128]{1,0:T(8,128)(2,1)S(1)} %get-tuple-element.11), channel_id=1, source_target_pairs={{0,8},{8,0},{16,24},{24,16},{32,40},{40,32},{48,56},{56,48},{64,72... | collective-permute-start | bytes 147464 | tf_op jit(solution)/shard_map/ppermute | solution.py:348
  52.7 21.9 %copy-start.6 = (f32[3072]{0:T(1024)S(1)}, f32[3072]{0:T(1024)}, u32[]{:S(2)}) copy-start(f32[3072]{0:T(1024)} %param.15) | copy-start | bytes 36868
  52.8 21.9 %copy-start.7 = (f32[3072]{0:T(1024)S(1)}, f32[3072]{0:T(1024)}, u32[]{:S(2)}) copy-start(f32[3072]{0:T(1024)} %param.23) | copy-start | bytes 36868
  52.8 21.9 %all-to-all-start.1 = ((bf16[8,192,384]{2,1,0:T(8,128)(2,1)}), bf16[8,192,384]{2,1,0:T(8,128)(2,1)S(1)}, u32[]{:S(2)}, u32[]{:S(2)}) async-start(bf16[8,192,384]{2,1,0:T(8,128)(2,1)} %terms_of.1), calls=%async_computation.1 | async-start | bytes 2359296 | tf_op jit(solution)/shard_map/all_to_all | solution.py:372
  76.0 20.8 %all-to-all-start.2 = ((bf16[8,192,384]{2,1,0:T(8,128)(2,1)}), bf16[8,192,384]{2,1,0:T(8,128)(2,1)S(1)}, u32[]{:S(2)}, u32[]{:S(2)}) async-start(bf16[8,192,384]{2,1,0:T(8,128)(2,1)} %mix.1), calls=%async_computation.2 | async-start | bytes 2359296 | tf_op jit(solution)/shard_map/all_to_all | solution.py:374
  79.6 1.4 %collective-permute-start.8 = (bf16[2,192,128]{2,1,0:T(8,128)(2,1)S(1)}, bf16[2,192,128]{2,1,0:T(8,128)(2,1)S(1)}, u32[]{:S(2)}, u32[]{:S(2)}) collective-permute-start(bf16[2,192,128]{2,1,0:T(8,128)(2,1)S(1)} %get-tuple-element.9.other_ref), channel_id=1, source_target_pairs={{0,8},{8,0},{16,24},{24,16},{32,40},{40,32},{48,56},{56,48},{64,72... | collective-permute-start | bytes 294920 | tf_op jit(solution)/shard_map/ppermute | solution.py:348

commit v4 on v3

--- a/solution.py
+++ b/solution.py
@@ -13,13 +13,17 @@
 SMEM = pl.BlockSpec(memory_space=pltpu.SMEM)
 HBM = pl.BlockSpec(memory_space=pltpu.HBM)
 ANY = pl.BlockSpec(memory_space=pl.ANY)
-LIMIT = 48 * 1024 * 1024
+LIMIT = 16 * 1024 * 1024
 
 
 def params(**kw):
     return pltpu.CompilerParams(vmem_limit_bytes=LIMIT, **kw)
 
 
+def in_hbm(x):
+    return pltpu.with_memory_space_constraint(x, pltpu.HBM)
+
+
 def fetch(pairs, sems):
     copies = [pltpu.make_async_copy(src, dst, sems.at[i]) for i, (src, dst) in enumerate(pairs)]
     for copy in copies:
@@ -27,10 +31,12 @@
     return copies
 
 
-def copies_kernel(stale_ref, out_ref, sems):
+def copies_kernel(stale_ref, out_ref, held, sems):
     n, _, _, hd = out_ref.shape
     heads = stale_ref.shape[2] // hd
-    copies = fetch([(stale_ref.at[:, :, pl.ds(i % heads * hd, hd)], out_ref.at[i]) for i in range(n)], sems)
+    for copy in fetch([(stale_ref.at[:, :, pl.ds(i * hd, hd)], held.at[i]) for i in range(heads)], sems):
+        copy.wait()
+    copies = fetch([(held.at[i % heads], out_ref.at[i]) for i in range(n)], sems)
     for copy in copies:
         copy.wait()
 
@@ -41,13 +47,16 @@
         in_specs=[HBM],
         out_specs=HBM,
         out_shape=jax.ShapeDtypeStruct((n,) + stale.shape[:2] + (hd,), BF),
-        scratch_shapes=[pltpu.SemaphoreType.DMA((n,))],
+        scratch_shapes=[
+            pltpu.VMEM((stale.shape[2] // hd,) + stale.shape[:2] + (hd,), BF),
+            pltpu.SemaphoreType.DMA((n,)),
+        ],
         compiler_params=params(),
         name="copies_of",
-    )(stale)
-
-
-def modulate_kernel(image_ref, shift_ref, scale_ref, mod_ref, image, shift, scale, sems):
+    )(in_hbm(stale))
+
+
+def modulate_kernel(image_ref, shift_ref, scale_ref, _, mod_ref, image, shift, scale, sems):
     copies = fetch([(shift_ref, shift), (scale_ref, scale)], sems)
     rows = image_ref.shape[0]
     parts = 4
@@ -60,6 +69,8 @@
         copy.start()
     for copy in copies:
         copy.wait()
+    gain = 1.0 + scale[...].reshape(1, -1)
+    lift = shift[...].reshape(1, -1)
     step = 16
     for j in range(parts):
         blocks[j].wait()
@@ -70,13 +81,13 @@
             centred = wide - average
             spread = jnp.mean(centred * centred, -1, keepdims=True)
             normed = centred * lax.rsqrt(spread + 1e-06)
-            mod_ref[at, :] = (normed * (1.0 + scale[...]) + shift[...]).astype(BF)
-
-
-def modulate(image, shift, scale):
+            mod_ref[at, :] = (normed * gain + lift).astype(BF)
+
+
+def modulate(image, shift, scale, awaited):
     return pl.pallas_call(
         modulate_kernel,
-        in_specs=[HBM] * 3,
+        in_specs=[HBM] * 3 + [ANY],
         out_specs=VMEM,
         out_shape=jax.ShapeDtypeStruct(image.shape, BF),
         scratch_shapes=[
@@ -87,56 +98,45 @@
         ],
         compiler_params=params(),
         name="modulate",
-    )(image, shift, scale)
-
-
-def project_kernel(c_ref, own_ref, other_ref, w_ref, bias_ref, q_gain_ref, k_gain_ref, q_ref, kv_own_ref, kv_other_ref, wide, sems):
-    rows, features = own_ref.shape
+    )(*(in_hbm(x) for x in (image, shift, scale)), awaited)
+
+
+def finish_kernel(c_ref, sums_ref, bias_ref, q_gain_ref, k_gain_ref, fresh_ref, home_ref, away_ref):
+    _, rows, width = sums_ref.shape
     hd = q_gain_ref.shape[1]
-    home = pl.ds(pl.multiple_of(c_ref[0] * hd, hd), hd)
-    parts = 4
-    depth = features // parts
-    copies = []
-    for k in range(parts):
-        at = pl.ds(k * depth, depth)
-        copies += fetch(
-            [(w_ref.at[j, at, home], wide.at[at, pl.ds(j * hd, hd)]) for j in range(3)], sems.at[pl.ds(3 * k, 3)]
-        )
-    sums = [None, None]
-    for k in range(parts):
-        for copy in copies[3 * k : 3 * k + 3]:
-            copy.wait()
-        at = slice(k * depth, (k + 1) * depth)
-        for i, m_ref in enumerate((own_ref, other_ref)):
-            term = jnp.dot(m_ref[:, at], wide[at, :], preferred_element_type=F32)
-            sums[i] = term if k == 0 else sums[i] + term
 
     def norm(part, gain):
         return part * lax.rsqrt(jnp.mean(part * part, -1, keepdims=True) + 1e-06) * gain
 
-    for i, out_ref in enumerate((kv_own_ref, kv_other_ref)):
-        q = sums[i][:, :hd] + bias_ref[0:1, home]
-        q_ref[pl.ds(i * rows, rows), :] = norm(q, q_gain_ref[...]).astype(BF)
-        out_ref[0] = norm(sums[i][:, hd : 2 * hd] + bias_ref[1:2, home], k_gain_ref[...]).astype(BF)
-        out_ref[1] = (sums[i][:, 2 * hd :] + bias_ref[2:3, home]).astype(BF)
-
-
-def project(core, own, other, weight, bias, q_gain, k_gain):
-    rows, features = own.shape
+    for h in range(width // hd):
+        at = slice(h * hd, (h + 1) * hd)
+        q = norm(sums_ref[0, :, at] + bias_ref[0:1, at], q_gain_ref[...]).astype(BF)
+        k = norm(sums_ref[1, :, at] + bias_ref[1:2, at], k_gain_ref[...]).astype(BF)
+        v = (sums_ref[2, :, at] + bias_ref[2:3, at]).astype(BF)
+        fresh_ref[0, :, at] = k
+        fresh_ref[1, :, at] = v
+
+        def put(out_ref, q=q, k=k, v=v):
+            for j, x in enumerate((q, k, v)):
+                out_ref[j] = x
+
+        pl.when(c_ref[0] == h)(lambda: put(home_ref))
+        pl.when(c_ref[0] != h)(lambda: put(away_ref))
+
+
+def project(core, modulated, weight, bias, q_gain, k_gain):
+    rows, features = modulated.shape
     hd = q_gain.shape[1]
-    return pl.pallas_call(
-        project_kernel,
-        in_specs=[SMEM, VMEM, VMEM, ANY, VMEM, VMEM, VMEM],
+    sums = jnp.einsum("tf,jfc->jtc", modulated, jnp.transpose(weight, (1, 0, 2)), preferred_element_type=F32)
+    part = jax.ShapeDtypeStruct((3, rows, hd), BF)
+    return pl.pallas_call(
+        finish_kernel,
+        in_specs=[SMEM] + [VMEM] * 4,
         out_specs=[VMEM] * 3,
-        out_shape=[
-            jax.ShapeDtypeStruct((2 * rows, hd), BF),
-            jax.ShapeDtypeStruct((2, rows, hd), BF),
-            jax.ShapeDtypeStruct((2, rows, hd), BF),
-        ],
-        scratch_shapes=[pltpu.VMEM((features, 3 * hd), BF), pltpu.SemaphoreType.DMA((12,))],
-        compiler_params=params(),
-        name="project",
-    )(core, own, other, jnp.transpose(weight, (1, 0, 2)), bias, q_gain, k_gain)
+        out_shape=[jax.ShapeDtypeStruct((2, rows, weight.shape[2]), BF), part, part],
+        compiler_params=params(),
+        name="finish",
+    )(core, sums, bias, q_gain, k_gain)
 
 
 def block_sums(q, k, v_ref_value):
@@ -154,16 +154,11 @@
 def remote_kernel(q_ref, kv_ref, out_ref):
     rows, hd = q_ref.shape
     same = eye(hd)
+    k, v = (kv_ref[:, part].reshape(-1, hd) for part in (0, 1))
+    total = block_sums(q_ref[...], k, v)
+    out_ref[pl.ds(0, rows), :] = total[:, :hd].astype(BF)
     for i in range(rows // hd):
-        at = slice(i * hd, (i + 1) * hd)
-        q = q_ref[at, :]
-        total = None
-        for j in range(0, kv_ref.shape[0], 2):
-            k, v = (kv_ref[j : j + 2, part].reshape(-1, hd) for part in (0, 1))
-            part = block_sums(q, k, v)
-            total = part if total is None else total + part
-        out_ref[at, :] = total[:, :hd].astype(BF)
-        line = jnp.sum(total[:, hd:] * same, 0, keepdims=True)
+        line = jnp.sum(total[i * hd : (i + 1) * hd, hd:] * same, 0, keepdims=True)
         high = line.astype(BF).astype(F32)
         out_ref[pl.ds(rows + 16 * i, 16), :] = jnp.concatenate(
             [jnp.broadcast_to(high, (8, hd)), jnp.broadcast_to(line - high, (8, hd))], 0
@@ -183,26 +178,22 @@
 
 
 def local_kernel(c_ref, q_ref, own_ref, other_ref, kv_ref, text_ref, out_ref):
-    rows = own_ref.shape[1]
-    hd = q_ref.shape[1]
-    n = kv_ref.shape[0]
-    core, chip = c_ref[0], c_ref[1]
-    head = pl.ds(pl.multiple_of(core * hd, hd), hd)
-    for i, fresh in enumerate((own_ref, other_ref)):
+    rows, hd = own_ref.shape[1:]
+    head = pl.ds(pl.multiple_of(c_ref[0] * hd, hd), hd)
+    core, chip, chips = c_ref[0], c_ref[1], kv_ref.shape[0] // 2
+    out_ref[...] = block_sums(q_ref[...], text_ref[0, :, head], text_ref[1, :, head])
+    for j in range(1, chips):
+        there = pl.ds(2 * lax.rem(chip + j, chips), 2)
+        k, v = (kv_ref[there, part].reshape(-1, hd) for part in (0, 1))
+        out_ref[...] += block_sums(q_ref[...], k, v)
+    for i, fresh in enumerate((own_ref.at[1:3], other_ref.at[1:3])):
         at = pl.ds(i * rows, rows)
-        q = q_ref[at, :]
         beside = 2 * chip + (1 - core if i == 0 else core)
-        total = block_sums(q, fresh[0], fresh[1])
-        total += block_sums(q, kv_ref[beside, 0], kv_ref[beside, 1])
-        total += block_sums(q, text_ref[0, :, head], text_ref[1, :, head])
-        for j in range(1, n // 2):
-            there = pl.ds(2 * lax.rem(chip + j, n // 2), 2)
-            k, v = (kv_ref[there, part].reshape(-1, hd) for part in (0, 1))
-            total += block_sums(q, k, v)
-        out_ref[at, :] = total
-
-
-def attend_local(core_slot, q, own, other, kv, text):
+        k, v = (jnp.concatenate([fresh[j], kv_ref[beside, j]], 0) for j in (0, 1))
+        out_ref[at, :] += block_sums(q_ref[at, :], k, v)
+
+
+def attend_local(core, q, own, other, kv, text):
     rows, hd = q.shape
     return pl.pallas_call(
         local_kernel,
@@ -211,7 +202,7 @@
         out_shape=jax.ShapeDtypeStruct((rows, 2 * hd), F32),
         compiler_params=params(),
         name="attend_local",
-    )(core_slot, q, own, other, kv, text)
+    )(core, q, own, other, kv, text)
 
 
 def combine_kernel(local_ref, p1_ref, p2_ref, p3_ref, own_ref, other_ref):
@@ -337,36 +328,35 @@
     patch = lax.axis_index("patch")
     tp = lax.axis_index("tp")
     core = patch % 2
-    slot = (patch // 4) % 4
-    core_at = jnp.stack([core, slot]).astype(jnp.int32)
+    chip = (patch // 16) * 2 + (patch // 2) % 2
+    core_at = jnp.stack([core, chip]).astype(jnp.int32)
     tp_at = tp.astype(jnp.int32).reshape(1)
 
     def flip(bits):
         return [(i, i ^ bits) for i in range(n_patch)]
 
+    def turn(k):
+        return [(i, (i & ~12) | ((i + 4 * k) & 12)) for i in range(n_patch)]
+
     def send(x, perm):
         return lax.ppermute(x, "patch", perm)
 
-    groups = [[i | 4 * j | c for j in range(4) for c in (0, 1)] for i in range(n_patch) if not i & 13]
-
-    modulated = modulate(image, mod_shift.reshape(1, -1), mod_scale.reshape(1, -1))
-    other = send(modulated, flip(1))
+    groups = [[i | y | z | c for y in (0, 16) for z in (0, 2) for c in (0, 1)] for i in range(n_patch) if not i & 19]
     copies = copies_of(stale_kv, len(groups[0]), hd)
     kv = lax.all_to_all(copies, "patch", 0, 0, axis_index_groups=groups)
+
+    modulated = modulate(image, mod_shift, mod_scale, copies)
     gains = (q_gain.reshape(1, -1), k_gain.reshape(1, -1))
-    q, kv_own, kv_other = project(core_at, modulated, other, qkv_weight, qkv_bias, *gains)
-
-    hops = (2, 16, 18)
+    fresh_kv, own, away = project(core_at, modulated, qkv_weight, qkv_bias, *gains)
+    other = send(away, flip(1))
+    q = jnp.concatenate([own[0], other[0]], 0)
+
     partial = []
-    for bits in hops:
-        there = send(q, flip(bits))
-        partial.append(send(attend_remote(there, kv), flip(bits)))
-    local = attend_local(core_at, q, kv_own, kv_other, kv, text_kv)
+    for k in (1, 3, 2):
+        there = send(q, turn(k))
+        partial.append(send(attend_remote(there, kv), turn(4 - k)))
+    local = attend_local(core_at, q, own, other, kv, text_kv)
     kept, leaving = combine(local, partial)
-
-    back = send(kv_other, flip(1))
-    first = core == 0
-    fresh_kv = jnp.where(first, jnp.concatenate([kv_own, back], 2), jnp.concatenate([back, kv_own], 2))
 
     terms = terms_of(core_at, kept, send(leaving, flip(1)), out_weight, n_tp)
     terms = lax.all_to_all(terms, "tp", 0, 0)

time: 99.8 us -> 94.9 us (0.951); the launches traced: 97.8 us -> 94.1 us
  waiting for transfers between devices: 51.5 us -> 25.1 us
  blocking collectives: 0 us -> 19.7 us
  matrix products: 0 us -> 3.48 us
  starting transfers between devices: 26.7 us -> 29.7 us
  Pallas kernels: 16.9 us -> 15.2 us
  local copies, waits for them, and re-layouts: 1.07 us -> 0.05 us
    all_to_all x0 -> x1, blocking collectives: none -> 19.7 us  [shards(): mixed = join(lax.all_to_all(pieces, 'tp', 0, 0))]
    all_to_all x1 -> x0, waiting for transfers between devices: 15.1 us -> none  [shards(): mixed = join(lax.all_to_all(pieces, 'tp', 0, 0))]
    ppermute x9 -> x8, starting transfers between devices: 11.1 us -> 19.2 us  [send(): return lax.ppermute(x, 'patch', perm)]
    ppermute x9 -> x8, waiting for transfers between devices: 15.3 us -> 7.66 us  [send(): return lax.ppermute(x, 'patch', perm)]
    all_to_all x1, waiting for transfers between devices: 3.66 us -> 0.01 us  [shards(): kv = lax.all_to_all(copies, 'patch', 0, 0, axis_index_groups=groups)]
    all_to_all x1 -> x0, starting transfers between devices: 3.58 us -> none  [shards(): mixed = join(lax.all_to_all(pieces, 'tp', 0, 0))]
    dot_general x0 -> x1, matrix products: none -> 3.48 us  [project(): jnp.einsum('tf,jfc->jtc', modulated, jnp.transpose(weight, (1, 0, 2)), pr...]
    pallas_call x2, Pallas kernels: 6.07 us -> 3.75 us  [the longest x1 2.24 us: modulate(): pl.pallas_call(modulate_kernel, in_specs=[HBM] * 3 + [ANY], out_specs=VME...]
  transfers between devices with their start and end apart: 12 -> 10, of which waited for: 8 -> 5; matrix products, arithmetic and copies ran while one was open for 1% -> 4% of each run, Pallas kernels for 12% -> 9%
where the time goes in v4:
time: 94.9 us; the launch traced here: 94.1 us
  starting transfers between devices  29.7 us (31%)
  waiting for transfers between devices  25.1 us (26%)
  blocking collectives  19.7 us (21%)
  Pallas kernels  15.2 us (16%)
  matrix products  3.48 us (4%)
    all_to_all x1, blocking collectives, shards(): mixed = join(lax.all_to_all(pieces, 'tp', 0, 0))  19.7 us
    ppermute x8, starting transfers between devices, send(): return lax.ppermute(x, 'patch', perm)  19.2 us
    all_to_all x1, waiting for transfers between devices, shards(): terms = lax.all_to_all(terms, 'tp', 0, 0)  17.4 us
    ppermute x8, waiting for transfers between devices, send(): return lax.ppermute(x, 'patch', perm)  7.66 us
    all_to_all x1, starting transfers between devices, shards(): kv = lax.all_to_all(copies, 'patch', 0, 0, axis_index_groups=groups)  5.94 us
    all_to_all x1, starting transfers between devices, shards(): terms = lax.all_to_all(terms, 'tp', 0, 0)  4.48 us
    dot_general x1, matrix products, project(): jnp.einsum('tf,jfc->jtc', modulated, jnp.transpose(weight, (1, 0, 2)), pr...  3.48 us
    pallas_call x3, Pallas kernels, attend_remote(): pl.pallas_call(remote_kernel, in_specs=[VMEM] * 2, out_specs=VMEM, out_sh...  2.69 us
  transfers between devices with their start and end apart: 10, of which 5 were waited for; matrix products, arithmetic and copies ran while one was open for 4% of the time, Pallas kernels for 9%

profile of v4, /device:TPU:32, one launch (start us, length us, event | category | flops | bytes accessed | tf_op | source)
XLA Modules:
  0.0 94.1 jit_solution(10397508155335943195)
XLA Ops:
  0.6 1.9 %copies_of.1._ = bf16[8,2,192,128]{3,2,1,0:T(8,128)(2,1)} custom-call(bf16[2,192,256]{2,1,0:T(8,128)(2,1)} %stale_ref.1), custom_call_target="tpu_custom_call" | custom-call | tf_op jit(solution)/shard_map/copies_of/pallas_call | solution.py:45
  2.5 5.9 %all-to-all-start = ((bf16[8,2,192,128]{3,2,1,0:T(8,128)(2,1)}), bf16[8,2,192,128]{3,2,1,0:T(8,128)(2,1)S(1)}, u32[]{:S(2)}, u32[]{:S(2)}) async-start(bf16[8,2,192,128]{3,2,1,0:T(8,128)(2,1)} %copies_of.1._), calls=%async_computation | async-start | bytes 1572864 | tf_op jit(solution)/shard_map/all_to_all | solution.py:346
  8.5 2.2 %modulate.1 = bf16[192,3072]{1,0:T(8,128)(2,1)S(1)} custom-call(bf16[192,3072]{1,0:T(8,128)(2,1)} %image_ref.3, f32[3072]{0:T(1024)} %shift_ref.1, f32[3072]{0:T(1024)} %scale_ref.1, bf16[8,2,192,128]{3,2,1,0:T(8,128)(2,1)} %copies_of.1._), custom_call_target="tpu_custom_call" | custom-call | tf_op jit(solution)/shard_map/modulate/pallas_call | solution.py:88
  10.7 0.1 pad_add_fusion.c_ref
  10.8 3.5 %fusion.2.sums_ref = f32[3,192,256]{2,1,0:T(8,128)S(1)} fusion(bf16[3072,3,256]{2,0,1:T(8,128)(2,1)} %param.16, bf16[192,3072]{1,0:T(8,128)(2,1)S(1)} %modulate.1), kind=kOutput, calls=%fused_computation.2 | convolution fusion | flops 905969664 | bytes 6488064 | tf_op jit(solution)/shard_map/tf,jfc->jtc/dot_general | solution.py:130
  14.3 1.5 %finish.1 = (bf16[2,192,256]{2,1,0:T(8,128)(2,1)}, bf16[3,192,128]{2,1,0:T(8,128)(2,1)S(1)}, bf16[3,192,128]{2,1,0:T(8,128)(2,1)S(1)}) custom-call(s32[2]{0:T(128)S(1)} %pad_add_fusion.c_ref, f32[3,192,256]{2,1,0:T(8,128)S(1)} %fusion.2.sums_ref, f32[3,256]{1,0:T(4,128)S(1)} %copy-done.5, f32[1,128]{1,0:T(1,128)S(1)} %bitcast.23, f32[1,128]{1,0:T(1,128)S(1)} %bitcast.24), custom_call_target="tpu_custom_call" | custom-call | tf_op jit(solution)/shard_map/finish/pallas_call | solution.py:132
  15.8 0.1 collective-permute-start
  16.0 1.2 %collective-permute-done.other_ref = bf16[3,192,128]{2,1,0:T(8,128)(2,1)S(1)} collective-permute-done((bf16[3,192,128]{2,1,0:T(8,128)(2,1)S(1)}, bf16[3,192,128]{2,1,0:T(8,128)(2,1)S(1)}, u32[]{:S(2)}, u32[]{:S(2)}) %collective-permute-start) | collective-permute-done | bytes 147488 | tf_op jit(solution)/shard_map/ppermute | solution.py:342
  17.2 6.4 %collective-permute-start.5 = (bf16[384,128]{1,0:T(8,128)(2,1)S(1)}, bf16[384,128]{1,0:T(8,128)(2,1)S(1)}, u32[]{:S(2)}, u32[]{:S(2)}) collective-permute-start(bf16[384,128]{1,0:T(8,128)(2,1)S(1)} %pad_maximum_fusion.q_ref), channel_id=1, source_target_pairs={{0,64},{8,72},{16,80},{24,88},{32,96},{40,104},{48,112},{56,120},{... | collective-permute-start | bytes 294920 | tf_op jit(solution)/shard_map/ppermute | solution.py:342
  23.6 0.6 collective-permute-start.3
  24.1 2.4 %collective-permute-start.1 = (bf16[384,128]{1,0:T(8,128)(2,1)S(1)}, bf16[384,128]{1,0:T(8,128)(2,1)S(1)}, u32[]{:S(2)}, u32[]{:S(2)}) collective-permute-start(bf16[384,128]{1,0:T(8,128)(2,1)S(1)} %pad_maximum_fusion.q_ref), channel_id=1, source_target_pairs={{0,32},{8,40},{16,48},{24,56},{32,64},{40,72},{48,80},{56,88},{64,... | collective-permute-start | bytes 294920 | tf_op jit(solution)/shard_map/ppermute | solution.py:342
  26.5 4.4 %collective-permute-done.5.q_ref = bf16[384,128]{1,0:T(8,128)(2,1)S(1)} collective-permute-done((bf16[384,128]{1,0:T(8,128)(2,1)S(1)}, bf16[384,128]{1,0:T(8,128)(2,1)S(1)}, u32[]{:S(2)}, u32[]{:S(2)}) %collective-permute-start.5) | collective-permute-done | bytes 98336 | tf_op jit(solution)/shard_map/ppermute | solution.py:342
  30.9 0.9 attend_remote.5
  31.8 0.0 copy-start.2
  31.8 5.4 %collective-permute-start.6 = (bf16[432,128]{1,0:T(8,128)(2,1)S(1)}, bf16[432,128]{1,0:T(8,128)(2,1)S(1)}, u32[]{:S(2)}, u32[]{:S(2)}) collective-permute-start(bf16[432,128]{1,0:T(8,128)(2,1)S(1)} %attend_remote.5), channel_id=1, source_target_pairs={{0,64},{8,72},{16,80},{24,88},{32,96},{40,104},{48,112},{56,120},{... | collective-permute-start | bytes 331784 | tf_op jit(solution)/shard_map/ppermute | solution.py:342
  37.2 0.9 attend_remote.4
  38.1 0.2 collective-permute-start.4
  38.3 0.9 attend_remote.3
  39.2 0.0 copy-start.1
  39.2 4.1 %collective-permute-start.2 = (bf16[432,128]{1,0:T(8,128)(2,1)S(1)}, bf16[432,128]{1,0:T(8,128)(2,1)S(1)}, u32[]{:S(2)}, u32[]{:S(2)}) collective-permute-start(bf16[432,128]{1,0:T(8,128)(2,1)S(1)} %attend_remote.3), channel_id=1, source_target_pairs={{0,96},{8,104},{16,112},{24,120},{32,0},{40,8},{48,16},{56,24},{64... | collective-permute-start | bytes 331784 | tf_op jit(solution)/shard_map/ppermute | solution.py:342
  43.3 1.9 %attend_local.1.local_ref = f32[384,256]{1,0:T(8,128)S(1)} custom-call(s32[2]{0:T(128)S(1)} %pad_add_fusion.c_ref, bf16[384,128]{1,0:T(8,128)(2,1)S(1)} %pad_maximum_fusion.q_ref, bf16[3,192,128]{2,1,0:T(8,128)(2,1)S(1)} %get-tuple-element.7.own_ref, bf16[3,192,128]{2,1,0:T(8,128)(2,1)S(1)} %collective-permute-done.other_ref, ...), custom_call_target="tpu_custom_call" | custom-call | tf_op jit(solution)/shard_map/attend_local/pallas_call | solution.py:198
  45.3 0.8 collective-permute-done.2.p1_ref
  46.1 0.1 combine.1
  46.3 0.1 collective-permute-start.7
  46.4 1.2 %collective-permute-done.7.swapped_ref = bf16[192,128]{1,0:T(8,128)(2,1)S(1)} collective-permute-done((bf16[192,128]{1,0:T(8,128)(2,1)S(1)}, bf16[192,128]{1,0:T(8,128)(2,1)S(1)}, u32[]{:S(2)}, u32[]{:S(2)}) %collective-permute-start.7) | collective-permute-done | bytes 49184 | tf_op jit(solution)/shard_map/ppermute | solution.py:342
  47.6 1.8 %terms_of.1 = bf16[8,192,384]{2,1,0:T(8,128)(2,1)} custom-call(s32[2]{0:T(128)S(1)} %pad_add_fusion.c_ref, bf16[192,128]{1,0:T(8,128)(2,1)S(1)} %get-tuple-element.9.kept_ref, bf16[192,128]{1,0:T(8,128)(2,1)S(1)} %collective-permute-done.7.swapped_ref, bf16[256,3072]{1,0:T(8,128)(2,1)S(1)} %copy-done.1), custom_call_target="tpu_custom_call" | custom-call | tf_op jit(solution)/shard_map/terms_of/pallas_call | solution.py:259
  49.5 0.0 copy-start
  49.5 4.5 %all-to-all-start.1 = ((bf16[8,192,384]{2,1,0:T(8,128)(2,1)}), bf16[8,192,384]{2,1,0:T(8,128)(2,1)S(1)}, u32[]{:S(2)}, u32[]{:S(2)}) async-start(bf16[8,192,384]{2,1,0:T(8,128)(2,1)} %terms_of.1), calls=%async_computation.1 | async-start | bytes 2359296 | tf_op jit(solution)/shard_map/all_to_all | solution.py:362
  54.0 17.4 %all-to-all-done.1.terms_ref = bf16[8,192,384]{2,1,0:T(8,128)(2,1)S(1)} async-done(((bf16[8,192,384]{2,1,0:T(8,128)(2,1)}), bf16[8,192,384]{2,1,0:T(8,128)(2,1)S(1)}, u32[]{:S(2)}, u32[]{:S(2)}) %all-to-all-start.1) | async-done | bytes 1179680 | tf_op jit(solution)/shard_map/all_to_all | solution.py:362
  71.4 1.9 %mix.1 = bf16[8,192,384]{2,1,0:T(8,128)(2,1)S(1)} custom-call(s32[1]{0:T(128)} %bitcast.t_ref, bf16[8,192,384]{2,1,0:T(8,128)(2,1)S(1)} %all-to-all-done.1.terms_ref, bf16[192,3072]{1,0:T(8,128)(2,1)S(1)} %copy-done, f32[1,3072]{1,0:T(1,128)S(1)} %bitcast.21, f32[1,3072]{1,0:T(1,128)S(1)} %bitcast.22), custom_call_target="tpu_custom_call" | custom-call | tf_op jit(solution)/shard_map/mix/pallas_call | solution.py:283
  73.3 19.7 %all_to_all.15.pieces_ref = bf16[8,192,384]{2,1,0:T(8,128)(2,1)S(1)} all-to-all(bf16[8,192,384]{2,1,0:T(8,128)(2,1)S(1)} %mix.1), channel_id=1, replica_groups=mesh['patch'=32,'tp'=8] {'tp'}, dimensions={0} | all-to-all | bytes 2359296 | tf_op jit(solution)/shard_map/all_to_all | solution.py:364
  93.0 1.1 %join.1 = bf16[192,3072]{1,0:T(8,128)(2,1)} custom-call(bf16[8,192,384]{2,1,0:T(8,128)(2,1)S(1)} %all_to_all.15.pieces_ref), custom_call_target="tpu_custom_call" | custom-call | tf_op jit(solution)/shard_map/join/pallas_call | solution.py:312
  (21 shorter events, 0.1 us)
Async XLA Ops:
  2.5 28.4 %all-to-all-start = ((bf16[8,2,192,128]{3,2,1,0:T(8,128)(2,1)}), bf16[8,2,192,128]{3,2,1,0:T(8,128)(2,1)S(1)}, u32[]{:S(2)}, u32[]{:S(2)}) async-start(bf16[8,2,192,128]{3,2,1,0:T(8,128)(2,1)} %copies_of.1._), calls=%async_computation | async-start | bytes 1572864 | tf_op jit(solution)/shard_map/all_to_all | solution.py:346
  10.8 3.5 %copy-start.5 = (f32[3,256]{1,0:T(4,128)S(1)}, f32[3,256]{1,0:T(4,128)}, u32[]{:S(2)}) copy-start(f32[3,256]{1,0:T(4,128)} %bias_ref.1) | copy-start | bytes 9220
  10.8 3.5 %copy-start.6 = (f32[128]{0:T(128)S(1)}, f32[128]{0:T(128)}, u32[]{:S(2)}) copy-start(f32[128]{0:T(128)} %param.18) | copy-start | bytes 1540
  10.8 3.5 %copy-start.7 = (f32[128]{0:T(128)S(1)}, f32[128]{0:T(128)}, u32[]{:S(2)}) copy-start(f32[128]{0:T(128)} %param.19) | copy-start | bytes 1540
  15.8 1.4 %collective-permute-start = (bf16[3,192,128]{2,1,0:T(8,128)(2,1)S(1)}, bf16[3,192,128]{2,1,0:T(8,128)(2,1)S(1)}, u32[]{:S(2)}, u32[]{:S(2)}) collective-permute-start(bf16[3,192,128]{2,1,0:T(8,128)(2,1)S(1)} %get-tuple-element.8), channel_id=1, source_target_pairs={{0,8},{8,0},{16,24},{24,16},{32,40},{40,32},{48,56},{56,48},{64,72... | collective-permute-start | bytes 442376 | tf_op jit(solution)/shard_map/ppermute | solution.py:342
  17.2 13.7 %collective-permute-start.5 = (bf16[384,128]{1,0:T(8,128)(2,1)S(1)}, bf16[384,128]{1,0:T(8,128)(2,1)S(1)}, u32[]{:S(2)}, u32[]{:S(2)}) collective-permute-start(bf16[384,128]{1,0:T(8,128)(2,1)S(1)} %pad_maximum_fusion.q_ref), channel_id=1, source_target_pairs={{0,64},{8,72},{16,80},{24,88},{32,96},{40,104},{48,112},{56,120},{... | collective-permute-start | bytes 294920 | tf_op jit(solution)/shard_map/ppermute | solution.py:342
  23.6 13.6 %collective-permute-start.3 = (bf16[384,128]{1,0:T(8,128)(2,1)S(1)}, bf16[384,128]{1,0:T(8,128)(2,1)S(1)}, u32[]{:S(2)}, u32[]{:S(2)}) collective-permute-start(bf16[384,128]{1,0:T(8,128)(2,1)S(1)} %pad_maximum_fusion.q_ref), channel_id=1, source_target_pairs={{0,96},{8,104},{16,112},{24,120},{32,0},{40,8},{48,16},{56,24},{64... | collective-permute-start | bytes 294920 | tf_op jit(solution)/shard_map/ppermute | solution.py:342
  24.1 14.2 %collective-permute-start.1 = (bf16[384,128]{1,0:T(8,128)(2,1)S(1)}, bf16[384,128]{1,0:T(8,128)(2,1)S(1)}, u32[]{:S(2)}, u32[]{:S(2)}) collective-permute-start(bf16[384,128]{1,0:T(8,128)(2,1)S(1)} %pad_maximum_fusion.q_ref), channel_id=1, source_target_pairs={{0,32},{8,40},{16,48},{24,56},{32,64},{40,72},{48,80},{56,88},{64,... | collective-permute-start | bytes 294920 | tf_op jit(solution)/shard_map/ppermute | solution.py:342
  31.8 11.5 %copy-start.2 = (bf16[2,512,256]{2,1,0:T(8,128)(2,1)S(1)}, bf16[2,512,256]{2,1,0:T(8,128)(2,1)}, u32[]{:S(2)}) copy-start(bf16[2,512,256]{2,1,0:T(8,128)(2,1)} %text_ref.1) | copy-start | bytes 1572868
  31.8 13.5 %collective-permute-start.6 = (bf16[432,128]{1,0:T(8,128)(2,1)S(1)}, bf16[432,128]{1,0:T(8,128)(2,1)S(1)}, u32[]{:S(2)}, u32[]{:S(2)}) collective-permute-start(bf16[432,128]{1,0:T(8,128)(2,1)S(1)} %attend_remote.5), channel_id=1, source_target_pairs={{0,64},{8,72},{16,80},{24,88},{32,96},{40,104},{48,112},{56,120},{... | collective-permute-start | bytes 331784 | tf_op jit(solution)/shard_map/ppermute | solution.py:342
  38.1 7.2 %collective-permute-start.4 = (bf16[432,128]{1,0:T(8,128)(2,1)S(1)}, bf16[432,128]{1,0:T(8,128)(2,1)S(1)}, u32[]{:S(2)}, u32[]{:S(2)}) collective-permute-start(bf16[432,128]{1,0:T(8,128)(2,1)S(1)} %attend_remote.4), channel_id=1, source_target_pairs={{0,32},{8,40},{16,48},{24,56},{32,64},{40,72},{48,80},{56,88},{64,... | collective-permute-start | bytes 331784 | tf_op jit(solution)/shard_map/ppermute | solution.py:342
  39.2 8.4 %copy-start.1 = (bf16[256,3072]{1,0:T(8,128)(2,1)S(1)}, bf16[256,3072]{1,0:T(8,128)(2,1)}, u32[]{:S(2)}) copy-start(bf16[256,3072]{1,0:T(8,128)(2,1)} %w_ref.1) | copy-start | bytes 4718596
  39.2 6.9 %collective-permute-start.2 = (bf16[432,128]{1,0:T(8,128)(2,1)S(1)}, bf16[432,128]{1,0:T(8,128)(2,1)S(1)}, u32[]{:S(2)}, u32[]{:S(2)}) collective-permute-start(bf16[432,128]{1,0:T(8,128)(2,1)S(1)} %attend_remote.3), channel_id=1, source_target_pairs={{0,96},{8,104},{16,112},{24,120},{32,0},{40,8},{48,16},{56,24},{64... | collective-permute-start | bytes 331784 | tf_op jit(solution)/shard_map/ppermute | solution.py:342
  46.3 1.3 %collective-permute-start.7 = (bf16[192,128]{1,0:T(8,128)(2,1)S(1)}, bf16[192,128]{1,0:T(8,128)(2,1)S(1)}, u32[]{:S(2)}, u32[]{:S(2)}) collective-permute-start(bf16[192,128]{1,0:T(8,128)(2,1)S(1)} %get-tuple-element.10), channel_id=1, source_target_pairs={{0,8},{8,0},{16,24},{24,16},{32,40},{40,32},{48,56},{56,48},{64,72... | collective-permute-start | bytes 147464 | tf_op jit(solution)/shard_map/ppermute | solution.py:342
  49.5 22.0 %copy-start = (bf16[192,3072]{1,0:T(8,128)(2,1)S(1)}, bf16[192,3072]{1,0:T(8,128)(2,1)}, u32[]{:S(2)}) copy-start(bf16[192,3072]{1,0:T(8,128)(2,1)} %image_ref.3) | copy-start | bytes 3538948
  49.5 21.9 %copy-start.3 = (f32[3072]{0:T(1024)S(1)}, f32[3072]{0:T(1024)}, u32[]{:S(2)}) copy-start(f32[3072]{0:T(1024)} %param.15) | copy-start | bytes 36868
  49.5 21.9 %copy-start.4 = (f32[3072]{0:T(1024)S(1)}, f32[3072]{0:T(1024)}, u32[]{:S(2)}) copy-start(f32[3072]{0:T(1024)} %param.23) | copy-start | bytes 36868
  49.5 21.9 %all-to-all-start.1 = ((bf16[8,192,384]{2,1,0:T(8,128)(2,1)}), bf16[8,192,384]{2,1,0:T(8,128)(2,1)S(1)}, u32[]{:S(2)}, u32[]{:S(2)}) async-start(bf16[8,192,384]{2,1,0:T(8,128)(2,1)} %terms_of.1), calls=%async_computation.1 | async-start | bytes 2359296 | tf_op jit(solution)/shard_map/all_to_all | solution.py:362

commit v5 on v4

--- a/solution.py
+++ b/solution.py
@@ -56,7 +56,8 @@
     )(in_hbm(stale))
 
 
-def modulate_kernel(image_ref, shift_ref, scale_ref, _, mod_ref, image, shift, scale, sems):
+def modulate_kernel(image_ref, shift_ref, scale_ref, w_ref, _, mod_ref, near_ref, image, shift, scale, sems):
+    brought = pltpu.make_async_copy(w_ref, near_ref, sems.at[6])
     copies = fetch([(shift_ref, shift), (scale_ref, scale)], sems)
     rows = image_ref.shape[0]
     parts = 4
@@ -67,6 +68,7 @@
     ]
     for copy in blocks:
         copy.start()
+    brought.start()
     for copy in copies:
         copy.wait()
     gain = 1.0 + scale[...].reshape(1, -1)
@@ -82,52 +84,48 @@
             spread = jnp.mean(centred * centred, -1, keepdims=True)
             normed = centred * lax.rsqrt(spread + 1e-06)
             mod_ref[at, :] = (normed * gain + lift).astype(BF)
-
-
-def modulate(image, shift, scale, awaited):
+    brought.wait()
+
+
+def modulate(image, shift, scale, weight, awaited):
     return pl.pallas_call(
         modulate_kernel,
-        in_specs=[HBM] * 3 + [ANY],
-        out_specs=VMEM,
-        out_shape=jax.ShapeDtypeStruct(image.shape, BF),
+        in_specs=[ANY] * 3 + [HBM, ANY],
+        out_specs=[VMEM] * 2,
+        out_shape=[jax.ShapeDtypeStruct(image.shape, BF), jax.ShapeDtypeStruct(weight.shape, BF)],
         scratch_shapes=[
             pltpu.VMEM(image.shape, BF),
             pltpu.VMEM(shift.shape, F32),
             pltpu.VMEM(scale.shape, F32),
-            pltpu.SemaphoreType.DMA((6,)),
+            pltpu.SemaphoreType.DMA((7,)),
         ],
         compiler_params=params(),
         name="modulate",
-    )(*(in_hbm(x) for x in (image, shift, scale)), awaited)
+    )(image, shift, scale, in_hbm(weight), awaited)
 
 
 def finish_kernel(c_ref, sums_ref, bias_ref, q_gain_ref, k_gain_ref, fresh_ref, home_ref, away_ref):
-    _, rows, width = sums_ref.shape
     hd = q_gain_ref.shape[1]
+    first = c_ref[0] == 0
 
     def norm(part, gain):
         return part * lax.rsqrt(jnp.mean(part * part, -1, keepdims=True) + 1e-06) * gain
 
-    for h in range(width // hd):
-        at = slice(h * hd, (h + 1) * hd)
-        q = norm(sums_ref[0, :, at] + bias_ref[0:1, at], q_gain_ref[...]).astype(BF)
-        k = norm(sums_ref[1, :, at] + bias_ref[1:2, at], k_gain_ref[...]).astype(BF)
-        v = (sums_ref[2, :, at] + bias_ref[2:3, at]).astype(BF)
-        fresh_ref[0, :, at] = k
-        fresh_ref[1, :, at] = v
-
-        def put(out_ref, q=q, k=k, v=v):
-            for j, x in enumerate((q, k, v)):
-                out_ref[j] = x
-
-        pl.when(c_ref[0] == h)(lambda: put(home_ref))
-        pl.when(c_ref[0] != h)(lambda: put(away_ref))
+    for j, gain_ref in enumerate((q_gain_ref, k_gain_ref, None)):
+        pair = []
+        for at in (slice(0, hd), slice(hd, 2 * hd)):
+            part = sums_ref[j, :, at] + bias_ref[j : j + 1, at]
+            pair.append((part if gain_ref is None else norm(part, gain_ref[...])).astype(BF))
+            if j > 0:
+                fresh_ref[j - 1, :, at] = pair[-1]
+        home_ref[j] = jnp.where(first, pair[0], pair[1])
+        away_ref[j] = jnp.where(first, pair[1], pair[0])
 
 
 def project(core, modulated, weight, bias, q_gain, k_gain):
     rows, features = modulated.shape
     hd = q_gain.shape[1]
-    sums = jnp.einsum("tf,jfc->jtc", modulated, jnp.transpose(weight, (1, 0, 2)), preferred_element_type=F32)
+    sums = jnp.einsum("tf,jfc->jtc", modulated, weight, preferred_element_type=F32)
     part = jax.ShapeDtypeStruct((3, rows, hd), BF)
     return pl.pallas_call(
         finish_kernel,
@@ -205,7 +203,7 @@
     )(core, q, own, other, kv, text)
 
 
-def combine_kernel(local_ref, p1_ref, p2_ref, p3_ref, own_ref, other_ref):
+def combine_kernel(local_ref, p1_ref, p2_ref, p3_ref, _, own_ref, other_ref):
     rows, hd = local_ref.shape[0], own_ref.shape[1]
     same = eye(hd)
     for i in range(rows // hd):
@@ -227,77 +225,92 @@
                 out_ref[low - start : high - start, :] = done[low - i * hd : high - i * hd]
 
 
-def combine(local, parts):
+def combine(local, parts, awaited):
     rows, hd = local.shape[0], local.shape[1] // 2
     return pl.pallas_call(
         combine_kernel,
-        in_specs=[VMEM] * 4,
+        in_specs=[VMEM] * 4 + [ANY],
         out_specs=[VMEM] * 2,
         out_shape=[jax.ShapeDtypeStruct((rows // 2, hd), BF)] * 2,
         compiler_params=params(),
         name="combine",
-    )(local, *parts)
-
-
-def terms_kernel(c_ref, kept_ref, swapped_ref, w_ref, out_ref, heads, pieces, sems):
-    n, rows, columns = out_ref.shape
+    )(local, *parts, awaited)
+
+
+def terms_kernel(c_ref, kept_ref, swapped_ref, w_ref, out_ref, heads):
+    n, _, columns = out_ref.shape
     hd = kept_ref.shape[1]
-    core = c_ref[0]
-    heads[:, pl.ds(pl.multiple_of(core * hd, hd), hd)] = kept_ref[...]
-    heads[:, pl.ds(pl.multiple_of((1 - core) * hd, hd), hd)] = swapped_ref[...]
-    copies = []
+    first = c_ref[0] == 0
+    heads[:, :hd] = jnp.where(first, kept_ref[...], swapped_ref[...])
+    heads[:, hd:] = jnp.where(first, swapped_ref[...], kept_ref[...])
     for i in range(n):
-        pieces[i] = jnp.dot(heads[...], w_ref[:, i * columns : (i + 1) * columns], preferred_element_type=F32).astype(BF)
-        copies += fetch([(pieces.at[i], out_ref.at[i])], sems.at[pl.ds(i, 1)])
-    for copy in copies:
-        copy.wait()
+        at = slice(i * columns, (i + 1) * columns)
+        out_ref[i] = jnp.dot(heads[...], w_ref[:, at], preferred_element_type=F32).astype(BF)
 
 
 def terms_of(core, kept, swapped, weight, n):
     rows, hd = kept.shape
-    shape = (n, rows, weight.shape[1] // n)
     return pl.pallas_call(
         terms_kernel,
-        in_specs=[SMEM, VMEM, VMEM, VMEM],
-        out_specs=HBM,
-        out_shape=jax.ShapeDtypeStruct(shape, BF),
-        scratch_shapes=[pltpu.VMEM((rows, weight.shape[0]), BF), pltpu.VMEM(shape, BF), pltpu.SemaphoreType.DMA((n,))],
+        in_specs=[SMEM] + [VMEM] * 3,
+        out_specs=VMEM,
+        out_shape=jax.ShapeDtypeStruct((n, rows, weight.shape[1] // n), BF),
+        scratch_shapes=[pltpu.VMEM((rows, weight.shape[0]), BF)],
         compiler_params=params(),
         name="terms_of",
     )(core, kept, swapped, weight)
 
 
-def mix_kernel(t_ref, terms_ref, image_ref, gate_ref, bias_ref, out_ref, piece, sems):
-    n = terms_ref.shape[0]
-    projection = terms_ref[0].astype(F32)
-    for i in range(1, n):
-        projection += terms_ref[i].astype(F32)
-    projection += bias_ref[...]
-    piece[...] = (image_ref[...].astype(F32) + gate_ref[...] * projection).astype(BF)
-    for copy in fetch([(piece, out_ref.at[i]) for i in range(n)], sems):
+def edge_kernel(t_ref, w_ref, image_ref, gate_ref, bias_ref, _, w_out_ref, rows_ref, gate_out_ref, bias_out_ref, sems):
+    columns = rows_ref.shape[1]
+    mine = pl.ds(pl.multiple_of(t_ref[0] * columns, columns), columns)
+    pairs = [(ref.at[:, mine], out) for ref, out in ((image_ref, rows_ref), (gate_ref, gate_out_ref), (bias_ref, bias_out_ref))]
+    for copy in fetch(pairs + [(w_ref, w_out_ref)], sems):
         copy.wait()
 
 
-def mix(tp, terms, image, gate, bias):
+def edge(tp, weight, image, gate, bias, n, awaited):
+    rows, columns = image.shape[0], image.shape[1] // n
+    return pl.pallas_call(
+        edge_kernel,
+        in_specs=[SMEM, HBM] + [ANY] * 4,
+        out_specs=[VMEM] * 4,
+        out_shape=[
+            jax.ShapeDtypeStruct(weight.shape, BF),
+            jax.ShapeDtypeStruct((rows, columns), BF),
+            jax.ShapeDtypeStruct((1, columns), F32),
+            jax.ShapeDtypeStruct((1, columns), F32),
+        ],
+        scratch_shapes=[pltpu.SemaphoreType.DMA((4,))],
+        compiler_params=params(),
+        name="edge",
+    )(tp, in_hbm(weight), image, gate, bias, awaited)
+
+
+def mix_kernel(terms_ref, image_ref, gate_ref, bias_ref, out_ref):
+    n, rows, _ = terms_ref.shape
+    step = rows // 4
+    for k in range(4):
+        at = pl.ds(k * step, step)
+        projection = terms_ref[0, at, :].astype(F32)
+        for i in range(1, n):
+            projection += terms_ref[i, at, :].astype(F32)
+        projection += bias_ref[...]
+        piece = (image_ref[at, :].astype(F32) + gate_ref[...] * projection).astype(BF)
+        for i in range(n):
+            out_ref[i, at, :] = piece
+
+
+def mix(terms, image, gate, bias):
     n, rows, columns = terms.shape
     return pl.pallas_call(
         mix_kernel,
-        grid_spec=pltpu.PrefetchScalarGridSpec(
-            num_scalar_prefetch=1,
-            grid=(1,),
-            in_specs=[
-                pl.BlockSpec((n, rows, columns), lambda k, t: (0, 0, 0)),
-                pl.BlockSpec((rows, columns), lambda k, t: (0, t[0])),
-                pl.BlockSpec((1, columns), lambda k, t: (0, t[0])),
-                pl.BlockSpec((1, columns), lambda k, t: (0, t[0])),
-            ],
-            out_specs=HBM,
-            scratch_shapes=[pltpu.VMEM((rows, columns), BF), pltpu.SemaphoreType.DMA((n,))],
-        ),
+        in_specs=[VMEM] * 4,
+        out_specs=VMEM,
         out_shape=jax.ShapeDtypeStruct((n, rows, columns), BF),
         compiler_params=params(),
         name="mix",
-    )(tp, terms, image, gate, bias)
+    )(terms, image, gate, bias)
 
 
 def join_kernel(pieces_ref, out_ref, sems):
@@ -336,7 +349,9 @@
         return [(i, i ^ bits) for i in range(n_patch)]
 
     def turn(k):
-        return [(i, (i & ~12) | ((i + 4 * k) & 12)) for i in range(n_patch)]
+        return [(i, (i & ~14) | ((i + 2 * k) & 14)) for i in range(n_patch)]
+
+    across = [(i, (i & ~14) | ((i + (6 if i & 2 else -6)) & 14)) for i in range(n_patch)]
 
     def send(x, perm):
         return lax.ppermute(x, "patch", perm)
@@ -345,22 +360,22 @@
     copies = copies_of(stale_kv, len(groups[0]), hd)
     kv = lax.all_to_all(copies, "patch", 0, 0, axis_index_groups=groups)
 
-    modulated = modulate(image, mod_shift, mod_scale, copies)
+    modulated, weight = modulate(image, mod_shift, mod_scale, jnp.transpose(qkv_weight, (1, 0, 2)), copies)
     gains = (q_gain.reshape(1, -1), k_gain.reshape(1, -1))
-    fresh_kv, own, away = project(core_at, modulated, qkv_weight, qkv_bias, *gains)
+    fresh_kv, own, away = project(core_at, modulated, weight, qkv_bias, *gains)
     other = send(away, flip(1))
     q = jnp.concatenate([own[0], other[0]], 0)
 
     partial = []
-    for k in (1, 3, 2):
-        there = send(q, turn(k))
-        partial.append(send(attend_remote(there, kv), turn(4 - k)))
+    for there, back in ((across, across), (turn(2), turn(6)), (turn(6), turn(2))):
+        partial.append(send(attend_remote(send(q, there), kv), back))
     local = attend_local(core_at, q, own, other, kv, text_kv)
-    kept, leaving = combine(local, partial)
-
-    terms = terms_of(core_at, kept, send(leaving, flip(1)), out_weight, n_tp)
+    near_weight, *rim = edge(tp_at, out_weight, image, mod_gate.reshape(1, -1), out_bias.reshape(1, -1), n_tp, local)
+    kept, leaving = combine(local, partial, near_weight)
+
+    terms = terms_of(core_at, kept, send(leaving, flip(1)), near_weight, n_tp)
     terms = lax.all_to_all(terms, "tp", 0, 0)
-    pieces = mix(tp_at, terms, image, mod_gate.reshape(1, -1), out_bias.reshape(1, -1))
+    pieces = mix(terms, *rim)
     mixed = join(lax.all_to_all(pieces, "tp", 0, 0))
     return (mixed, fresh_kv)
 

time: 94.9 us -> 90 us (0.948)
  blocking collectives: 19.7 us -> 41 us
  waiting for transfers between devices: 25.1 us -> 9.49 us
  starting transfers between devices: 29.7 us -> 22.4 us
  matrix products: 3.48 us -> 1.11 us
    all_to_all x0 -> x1, blocking collectives: none -> 21.6 us  [shards(): terms = lax.all_to_all(terms, 'tp', 0, 0)]
    all_to_all x1 -> x0, waiting for transfers between devices: 17.4 us -> none  [shards(): terms = lax.all_to_all(terms, 'tp', 0, 0)]
    all_to_all x1 -> x0, starting transfers between devices: 4.48 us -> none  [shards(): terms = lax.all_to_all(terms, 'tp', 0, 0)]
    ppermute x8, starting transfers between devices: 19.2 us -> 16.5 us  [send(): return lax.ppermute(x, 'patch', perm)]
    dot_general x1, matrix products: 3.48 us -> 1.11 us  [project(): jnp.einsum('tf,jfc->jtc', modulated, weight, preferred_element_type=F32)]
    ppermute x8, waiting for transfers between devices: 7.66 us -> 9.49 us  [send(): return lax.ppermute(x, 'patch', perm)]
    pallas_call x4 -> x5, Pallas kernels: 6.11 us -> 5.6 us  [the longest x1 2.67 us: modulate(): pl.pallas_call(modulate_kernel, in_specs=[ANY] * 3 + [HBM, ANY], out_spec...]
  transfers between devices with their start and end apart: 10 -> 9, of which waited for: 5 -> 6; matrix products, arithmetic and copies ran while one was open for 4% -> 1% of each run, Pallas kernels for 9% -> 11%
where the time goes in v5:
time: 90 us; the launch traced here: 89.7 us
  blocking collectives  41 us (46%)
  starting transfers between devices  22.4 us (25%)
  Pallas kernels  14.7 us (16%)
  waiting for transfers between devices  9.49 us (11%)
  matrix products  1.11 us (1%)
    all_to_all x1, blocking collectives, shards(): terms = lax.all_to_all(terms, 'tp', 0, 0)  21.6 us
    all_to_all x1, blocking collectives, shards(): mixed = join(lax.all_to_all(pieces, 'tp', 0, 0))  19.3 us
    ppermute x8, starting transfers between devices, send(): return lax.ppermute(x, 'patch', perm)  16.5 us
    ppermute x8, waiting for transfers between devices, send(): return lax.ppermute(x, 'patch', perm)  9.49 us
    all_to_all x1, starting transfers between devices, shards(): kv = lax.all_to_all(copies, 'patch', 0, 0, axis_index_groups=groups)  5.94 us
    pallas_call x3, Pallas kernels, attend_remote(): pl.pallas_call(remote_kernel, in_specs=[VMEM] * 2, out_specs=VMEM, out_sh...  2.69 us
    pallas_call x1, Pallas kernels, modulate(): pl.pallas_call(modulate_kernel, in_specs=[ANY] * 3 + [HBM, ANY], out_spec...  2.67 us
    pallas_call x1, Pallas kernels, copies_of(): pl.pallas_call(copies_kernel, in_specs=[HBM], out_specs=HBM, out_shape=ja...  1.97 us
  transfers between devices with their start and end apart: 9, of which 6 were waited for; matrix products, arithmetic and copies ran while one was open for 1% of the time, Pallas kernels for 11%

profile of v5, /device:TPU:32, one launch (start us, length us, event | category | flops | bytes accessed | tf_op | source)
XLA Modules:
  0.0 89.7 jit_solution(17767038802299809933)
XLA Ops:
  0.7 2.0 %copies_of.1._ = bf16[8,2,192,128]{3,2,1,0:T(8,128)(2,1)} custom-call(bf16[2,192,256]{2,1,0:T(8,128)(2,1)} %stale_ref.1), custom_call_target="tpu_custom_call" | custom-call | tf_op jit(solution)/shard_map/copies_of/pallas_call | solution.py:45
  2.6 5.9 %all-to-all-start = ((bf16[8,2,192,128]{3,2,1,0:T(8,128)(2,1)}), bf16[8,2,192,128]{3,2,1,0:T(8,128)(2,1)S(1)}, u32[]{:S(2)}, u32[]{:S(2)}) async-start(bf16[8,2,192,128]{3,2,1,0:T(8,128)(2,1)} %copies_of.1._), calls=%async_computation | async-start | bytes 1572864 | tf_op jit(solution)/shard_map/all_to_all | solution.py:361
  8.6 2.7 %modulate.1 = (bf16[192,3072]{1,0:T(8,128)(2,1)S(1)}, bf16[3,3072,256]{2,1,0:T(8,128)(2,1)S(1)}) custom-call(bf16[192,3072]{1,0:T(8,128)(2,1)S(1)} %copy-done, f32[3072]{0:T(1024)S(1)} %copy-done.2, f32[3072]{0:T(1024)S(1)} %copy-done.3, bf16[3,3072,256]{2,1,0:T(8,128)(2,1)} %bitcast.22, bf16[8,2,192,128]{3,2,1,0:T(8,128)(2,1)} %copies_of.1._), custom_call_target="tpu_custom_call" | custom-call | tf_op jit(solution)/shard_map/modulate/pallas_call | solution.py:91
  11.3 0.1 pad_add_fusion.c_ref
  11.4 1.1 %convolution_bitcast_fusion.sums_ref = f32[3,192,256]{2,1,0:T(8,128)S(1)} fusion(bf16[3,3072,256]{2,1,0:T(8,128)(2,1)S(1)} %get-tuple-element.13, bf16[192,3072]{1,0:T(8,128)(2,1)S(1)} %get-tuple-element.14), kind=kOutput, calls=%fused_computation | convolution fusion | flops 905969664 | bytes 6488064 | tf_op jit(solution)/shard_map/tf,jfc->jtc/dot_general | solution.py:128
  12.5 1.4 %finish.1 = (bf16[2,192,256]{2,1,0:T(8,128)(2,1)}, bf16[3,192,128]{2,1,0:T(8,128)(2,1)S(1)}, bf16[3,192,128]{2,1,0:T(8,128)(2,1)S(1)}) custom-call(s32[2]{0:T(128)S(1)} %pad_add_fusion.c_ref, f32[3,192,256]{2,1,0:T(8,128)S(1)} %convolution_bitcast_fusion.sums_ref, f32[3,256]{1,0:T(4,128)S(1)} %copy-done.6, f32[1,128]{1,0:T(1,128)S(1)} %bitcast.20, ...), custom_call_target="tpu_custom_call" | custom-call | tf_op jit(solution)/shard_map/finish/pallas_call | solution.py:130
  13.9 0.1 collective-permute-start
  14.1 1.2 %collective-permute-done.other_ref = bf16[3,192,128]{2,1,0:T(8,128)(2,1)S(1)} collective-permute-done((bf16[3,192,128]{2,1,0:T(8,128)(2,1)S(1)}, bf16[3,192,128]{2,1,0:T(8,128)(2,1)S(1)}, u32[]{:S(2)}, u32[]{:S(2)}) %collective-permute-start) | collective-permute-done | bytes 147488 | tf_op jit(solution)/shard_map/ppermute | solution.py:357
  15.3 5.5 %collective-permute-start.5 = (bf16[384,128]{1,0:T(8,128)(2,1)S(1)}, bf16[384,128]{1,0:T(8,128)(2,1)S(1)}, u32[]{:S(2)}, u32[]{:S(2)}) collective-permute-start(bf16[384,128]{1,0:T(8,128)(2,1)S(1)} %pad_maximum_fusion.q_ref), channel_id=1, source_target_pairs={{0,96},{8,104},{16,112},{24,120},{32,0},{40,8},{48,16},{56,24},{64... | collective-permute-start | bytes 294920 | tf_op jit(solution)/shard_map/ppermute | solution.py:357
  20.8 2.5 %collective-permute-start.1 = (bf16[384,128]{1,0:T(8,128)(2,1)S(1)}, bf16[384,128]{1,0:T(8,128)(2,1)S(1)}, u32[]{:S(2)}, u32[]{:S(2)}) collective-permute-start(bf16[384,128]{1,0:T(8,128)(2,1)S(1)} %pad_maximum_fusion.q_ref), channel_id=1, source_target_pairs={{0,80},{8,88},{16,64},{24,72},{32,112},{40,120},{48,96},{56,104},{... | collective-permute-start | bytes 294920 | tf_op jit(solution)/shard_map/ppermute | solution.py:357
  23.3 2.4 %collective-permute-done.5.q_ref = bf16[384,128]{1,0:T(8,128)(2,1)S(1)} collective-permute-done((bf16[384,128]{1,0:T(8,128)(2,1)S(1)}, bf16[384,128]{1,0:T(8,128)(2,1)S(1)}, u32[]{:S(2)}, u32[]{:S(2)}) %collective-permute-start.5) | collective-permute-done | bytes 98336 | tf_op jit(solution)/shard_map/ppermute | solution.py:357
  25.7 0.9 %attend_remote.5 = bf16[432,128]{1,0:T(8,128)(2,1)S(1)} custom-call(bf16[384,128]{1,0:T(8,128)(2,1)S(1)} %collective-permute-done.5.q_ref, bf16[8,2,192,128]{3,2,1,0:T(8,128)(2,1)S(1)} %all-to-all-done.kv_ref), custom_call_target="tpu_custom_call" | custom-call | tf_op jit(solution)/shard_map/attend_remote/pallas_call | solution.py:168
  26.6 0.0 copy-start.1
  26.6 3.9 %collective-permute-start.6 = (bf16[432,128]{1,0:T(8,128)(2,1)S(1)}, bf16[432,128]{1,0:T(8,128)(2,1)S(1)}, u32[]{:S(2)}, u32[]{:S(2)}) collective-permute-start(bf16[432,128]{1,0:T(8,128)(2,1)S(1)} %attend_remote.5), channel_id=1, source_target_pairs={{0,32},{8,40},{16,48},{24,56},{32,64},{40,72},{48,80},{56,88},{64,... | collective-permute-start | bytes 331784 | tf_op jit(solution)/shard_map/ppermute | solution.py:357
  30.5 0.3 collective-permute-done.3.q_ref
  30.9 0.9 %attend_remote.4 = bf16[432,128]{1,0:T(8,128)(2,1)S(1)} custom-call(bf16[384,128]{1,0:T(8,128)(2,1)S(1)} %collective-permute-done.3.q_ref, bf16[8,2,192,128]{3,2,1,0:T(8,128)(2,1)S(1)} %all-to-all-done.kv_ref), custom_call_target="tpu_custom_call" | custom-call | tf_op jit(solution)/shard_map/attend_remote/pallas_call | solution.py:168
  31.8 0.1 collective-permute-start.4
  31.8 0.1 collective-permute-done.1.q_ref
  32.0 0.9 attend_remote.3
  32.9 4.3 %collective-permute-start.2 = (bf16[432,128]{1,0:T(8,128)(2,1)S(1)}, bf16[432,128]{1,0:T(8,128)(2,1)S(1)}, u32[]{:S(2)}, u32[]{:S(2)}) collective-permute-start(bf16[432,128]{1,0:T(8,128)(2,1)S(1)} %attend_remote.3), channel_id=1, source_target_pairs={{0,80},{8,88},{16,64},{24,72},{32,112},{40,120},{48,96},{56,104},{... | collective-permute-start | bytes 331784 | tf_op jit(solution)/shard_map/ppermute | solution.py:357
  37.2 1.9 %attend_local.1._.local_ref = f32[384,256]{1,0:T(8,128)S(1)} custom-call(s32[2]{0:T(128)S(1)} %pad_add_fusion.c_ref, bf16[384,128]{1,0:T(8,128)(2,1)S(1)} %pad_maximum_fusion.q_ref, bf16[3,192,128]{2,1,0:T(8,128)(2,1)S(1)} %get-tuple-element.15.own_ref, bf16[3,192,128]{2,1,0:T(8,128)(2,1)S(1)} %collective-permute-done.other_ref, ...), custom_call_target="tpu_custom_call" | custom-call | tf_op jit(solution)/shard_map/attend_local/pallas_call | solution.py:196
  39.2 1.5 %edge.1 = (bf16[256,3072]{1,0:T(8,128)(2,1)S(1)}, bf16[192,384]{1,0:T(8,128)(2,1)S(1)}, f32[1,384]{1,0:T(1,128)S(1)}, f32[1,384]{1,0:T(1,128)S(1)}) custom-call(s32[1]{0:T(128)} %bitcast.9.t_ref, bf16[256,3072]{1,0:T(8,128)(2,1)} %w_ref.1, bf16[192,3072]{1,0:T(8,128)(2,1)S(1)} %copy-done, f32[1,3072]{1,0:T(1,128)S(1)} %bitcast.18, f32[1,3072]{1,0:T(1,128)S(1)} %bitcast.19, ...), custom_call_target="tpu_custom_call" | custom-call | tf_op jit(solution)/shard_map/edge/pallas_call | solution.py:274
  40.7 0.0 collective-permute-done.4.p2_ref
  40.7 4.2 %collective-permute-done.2.p1_ref = bf16[432,128]{1,0:T(8,128)(2,1)S(1)} collective-permute-done((bf16[432,128]{1,0:T(8,128)(2,1)S(1)}, bf16[432,128]{1,0:T(8,128)(2,1)S(1)}, u32[]{:S(2)}, u32[]{:S(2)}) %collective-permute-start.2) | collective-permute-done | bytes 110624 | tf_op jit(solution)/shard_map/ppermute | solution.py:357
  44.8 0.1 combine.1
  45.0 0.1 collective-permute-start.7
  45.1 1.2 %collective-permute-done.7.swapped_ref = bf16[192,128]{1,0:T(8,128)(2,1)S(1)} collective-permute-done((bf16[192,128]{1,0:T(8,128)(2,1)S(1)}, bf16[192,128]{1,0:T(8,128)(2,1)S(1)}, u32[]{:S(2)}, u32[]{:S(2)}) %collective-permute-start.7) | collective-permute-done | bytes 49184 | tf_op jit(solution)/shard_map/ppermute | solution.py:357
  46.3 1.1 %terms_of.1 = bf16[8,192,384]{2,1,0:T(8,128)(2,1)S(1)} custom-call(s32[2]{0:T(128)S(1)} %pad_add_fusion.c_ref, bf16[192,128]{1,0:T(8,128)(2,1)S(1)} %get-tuple-element.18.kept_ref, bf16[192,128]{1,0:T(8,128)(2,1)S(1)} %collective-permute-done.7.swapped_ref, bf16[256,3072]{1,0:T(8,128)(2,1)S(1)} %get-tuple-element.17._.w_ref), custom_call_target="tpu_custom_call" | custom-call | tf_op jit(solution)/shard_map/terms_of/pallas_call | solution.py:253
  47.4 21.6 %all_to_all.15.terms_ref = bf16[8,192,384]{2,1,0:T(8,128)(2,1)S(1)} all-to-all(bf16[8,192,384]{2,1,0:T(8,128)(2,1)S(1)} %terms_of.1), channel_id=1, replica_groups=mesh['patch'=32,'tp'=8] {'tp'}, dimensions={0} | all-to-all | bytes 2359296 | tf_op jit(solution)/shard_map/all_to_all | solution.py:377
  69.1 0.2 mix.1
  69.3 19.3 %all_to_all.16.pieces_ref = bf16[8,192,384]{2,1,0:T(8,128)(2,1)S(1)} all-to-all(bf16[8,192,384]{2,1,0:T(8,128)(2,1)S(1)} %mix.1), channel_id=1, replica_groups=mesh['patch'=32,'tp'=8] {'tp'}, dimensions={0} | all-to-all | bytes 2359296 | tf_op jit(solution)/shard_map/all_to_all | solution.py:379
  88.6 1.1 %join.1 = bf16[192,3072]{1,0:T(8,128)(2,1)} custom-call(bf16[8,192,384]{2,1,0:T(8,128)(2,1)S(1)} %all_to_all.16.pieces_ref), custom_call_target="tpu_custom_call" | custom-call | tf_op jit(solution)/shard_map/join/pallas_call | solution.py:325
  (23 shorter events, 0.1 us)
Async XLA Ops:
  0.6 7.9 %copy-start = (bf16[192,3072]{1,0:T(8,128)(2,1)S(1)}, bf16[192,3072]{1,0:T(8,128)(2,1)}, u32[]{:S(2)}) copy-start(bf16[192,3072]{1,0:T(8,128)(2,1)} %image_ref.3) | copy-start | bytes 3538948
  0.6 7.9 %copy-start.2 = (f32[3072]{0:T(1024)S(1)}, f32[3072]{0:T(1024)}, u32[]{:S(2)}) copy-start(f32[3072]{0:T(1024)} %shift_ref.1) | copy-start | bytes 36868
  0.7 7.9 %copy-start.3 = (f32[3072]{0:T(1024)S(1)}, f32[3072]{0:T(1024)}, u32[]{:S(2)}) copy-start(f32[3072]{0:T(1024)} %scale_ref.1) | copy-start | bytes 36868
  2.6 23.1 %all-to-all-start = ((bf16[8,2,192,128]{3,2,1,0:T(8,128)(2,1)}), bf16[8,2,192,128]{3,2,1,0:T(8,128)(2,1)S(1)}, u32[]{:S(2)}, u32[]{:S(2)}) async-start(bf16[8,2,192,128]{3,2,1,0:T(8,128)(2,1)} %copies_of.1._), calls=%async_computation | async-start | bytes 1572864 | tf_op jit(solution)/shard_map/all_to_all | solution.py:361
  11.4 1.1 %copy-start.6 = (f32[3,256]{1,0:T(4,128)S(1)}, f32[3,256]{1,0:T(4,128)}, u32[]{:S(2)}) copy-start(f32[3,256]{1,0:T(4,128)} %bias_ref.1) | copy-start | bytes 9220
  11.4 1.1 %copy-start.7 = (f32[128]{0:T(128)S(1)}, f32[128]{0:T(128)}, u32[]{:S(2)}) copy-start(f32[128]{0:T(128)} %param.18) | copy-start | bytes 1540
  11.4 1.1 %copy-start.8 = (f32[128]{0:T(128)S(1)}, f32[128]{0:T(128)}, u32[]{:S(2)}) copy-start(f32[128]{0:T(128)} %param.19) | copy-start | bytes 1540
  13.9 1.4 %collective-permute-start = (bf16[3,192,128]{2,1,0:T(8,128)(2,1)S(1)}, bf16[3,192,128]{2,1,0:T(8,128)(2,1)S(1)}, u32[]{:S(2)}, u32[]{:S(2)}) collective-permute-start(bf16[3,192,128]{2,1,0:T(8,128)(2,1)S(1)} %get-tuple-element.16), channel_id=1, source_target_pairs={{0,8},{8,0},{16,24},{24,16},{32,40},{40,32},{48,56},{56,48},{64,72... | collective-permute-start | bytes 442376 | tf_op jit(solution)/shard_map/ppermute | solution.py:357
  15.3 10.4 %collective-permute-start.5 = (bf16[384,128]{1,0:T(8,128)(2,1)S(1)}, bf16[384,128]{1,0:T(8,128)(2,1)S(1)}, u32[]{:S(2)}, u32[]{:S(2)}) collective-permute-start(bf16[384,128]{1,0:T(8,128)(2,1)S(1)} %pad_maximum_fusion.q_ref), channel_id=1, source_target_pairs={{0,96},{8,104},{16,112},{24,120},{32,0},{40,8},{48,16},{56,24},{64... | collective-permute-start | bytes 294920 | tf_op jit(solution)/shard_map/ppermute | solution.py:357
  20.8 10.1 %collective-permute-start.3 = (bf16[384,128]{1,0:T(8,128)(2,1)S(1)}, bf16[384,128]{1,0:T(8,128)(2,1)S(1)}, u32[]{:S(2)}, u32[]{:S(2)}) collective-permute-start(bf16[384,128]{1,0:T(8,128)(2,1)S(1)} %pad_maximum_fusion.q_ref), channel_id=1, source_target_pairs={{0,32},{8,40},{16,48},{24,56},{32,64},{40,72},{48,80},{56,88},{64,... | collective-permute-start | bytes 294920 | tf_op jit(solution)/shard_map/ppermute | solution.py:357
  20.8 11.2 %collective-permute-start.1 = (bf16[384,128]{1,0:T(8,128)(2,1)S(1)}, bf16[384,128]{1,0:T(8,128)(2,1)S(1)}, u32[]{:S(2)}, u32[]{:S(2)}) collective-permute-start(bf16[384,128]{1,0:T(8,128)(2,1)S(1)} %pad_maximum_fusion.q_ref), channel_id=1, source_target_pairs={{0,80},{8,88},{16,64},{24,72},{32,112},{40,120},{48,96},{56,104},{... | collective-permute-start | bytes 294920 | tf_op jit(solution)/shard_map/ppermute | solution.py:357
  26.6 10.6 %copy-start.1 = (bf16[2,512,256]{2,1,0:T(8,128)(2,1)S(1)}, bf16[2,512,256]{2,1,0:T(8,128)(2,1)}, u32[]{:S(2)}) copy-start(bf16[2,512,256]{2,1,0:T(8,128)(2,1)} %text_ref.1) | copy-start | bytes 1572868
  26.6 14.0 %collective-permute-start.6 = (bf16[432,128]{1,0:T(8,128)(2,1)S(1)}, bf16[432,128]{1,0:T(8,128)(2,1)S(1)}, u32[]{:S(2)}, u32[]{:S(2)}) collective-permute-start(bf16[432,128]{1,0:T(8,128)(2,1)S(1)} %attend_remote.5), channel_id=1, source_target_pairs={{0,32},{8,40},{16,48},{24,56},{32,64},{40,72},{48,80},{56,88},{64,... | collective-permute-start | bytes 331784 | tf_op jit(solution)/shard_map/ppermute | solution.py:357
  31.8 8.9 %collective-permute-start.4 = (bf16[432,128]{1,0:T(8,128)(2,1)S(1)}, bf16[432,128]{1,0:T(8,128)(2,1)S(1)}, u32[]{:S(2)}, u32[]{:S(2)}) collective-permute-start(bf16[432,128]{1,0:T(8,128)(2,1)S(1)} %attend_remote.4), channel_id=1, source_target_pairs={{0,96},{8,104},{16,112},{24,120},{32,0},{40,8},{48,16},{56,24},{64... | collective-permute-start | bytes 331784 | tf_op jit(solution)/shard_map/ppermute | solution.py:357
  32.9 12.0 %collective-permute-start.2 = (bf16[432,128]{1,0:T(8,128)(2,1)S(1)}, bf16[432,128]{1,0:T(8,128)(2,1)S(1)}, u32[]{:S(2)}, u32[]{:S(2)}) collective-permute-start(bf16[432,128]{1,0:T(8,128)(2,1)S(1)} %attend_remote.3), channel_id=1, source_target_pairs={{0,80},{8,88},{16,64},{24,72},{32,112},{40,120},{48,96},{56,104},{... | collective-permute-start | bytes 331784 | tf_op jit(solution)/shard_map/ppermute | solution.py:357
  37.2 2.0 %copy-start.4 = (f32[3072]{0:T(1024)S(1)}, f32[3072]{0:T(1024)}, u32[]{:S(2)}) copy-start(f32[3072]{0:T(1024)} %param.15) | copy-start | bytes 36868
  37.2 2.0 %copy-start.5 = (f32[3072]{0:T(1024)S(1)}, f32[3072]{0:T(1024)}, u32[]{:S(2)}) copy-start(f32[3072]{0:T(1024)} %param.23) | copy-start | bytes 36868
  45.0 1.3 %collective-permute-start.7 = (bf16[192,128]{1,0:T(8,128)(2,1)S(1)}, bf16[192,128]{1,0:T(8,128)(2,1)S(1)}, u32[]{:S(2)}, u32[]{:S(2)}) collective-permute-start(bf16[192,128]{1,0:T(8,128)(2,1)S(1)} %get-tuple-element.19), channel_id=1, source_target_pairs={{0,8},{8,0},{16,24},{24,16},{32,40},{40,32},{48,56},{56,48},{64,72... | collective-permute-start | bytes 147464 | tf_op jit(solution)/shard_map/ppermute | solution.py:357

commit v6 on v5

--- a/solution.py
+++ b/solution.py
@@ -348,10 +348,10 @@
     def flip(bits):
         return [(i, i ^ bits) for i in range(n_patch)]
 
-    def turn(k):
-        return [(i, (i & ~14) | ((i + 2 * k) & 14)) for i in range(n_patch)]
-
-    across = [(i, (i & ~14) | ((i + (6 if i & 2 else -6)) & 14)) for i in range(n_patch)]
+    def swap(of):
+        return [(i, (i & ~14) | (of(i >> 1 & 7) % 8 << 1)) for i in range(n_patch)]
+
+    swaps = [swap(lambda z: z + 3 if z % 2 else z - 3), swap(lambda z: z ^ 3), swap(lambda z: (z + 2 ^ 3) - 2)]
 
     def send(x, perm):
         return lax.ppermute(x, "patch", perm)
@@ -367,8 +367,8 @@
     q = jnp.concatenate([own[0], other[0]], 0)
 
     partial = []
-    for there, back in ((across, across), (turn(2), turn(6)), (turn(6), turn(2))):
-        partial.append(send(attend_remote(send(q, there), kv), back))
+    for there in swaps:
+        partial.append(send(attend_remote(send(q, there), kv), there))
     local = attend_local(core_at, q, own, other, kv, text_kv)
     near_weight, *rim = edge(tp_at, out_weight, image, mod_gate.reshape(1, -1), out_bias.reshape(1, -1), n_tp, local)
     kept, leaving = combine(local, partial, near_weight)

time: 90 us -> 89.3 us (level); the launches traced: 89.7 us -> 87.6 us
  starting transfers between devices: 22.4 us -> 18.3 us
  waiting for transfers between devices: 9.49 us -> 11.5 us
    ppermute x8, starting transfers between devices: 16.5 us -> 12.4 us  [send(): return lax.ppermute(x, 'patch', perm)]
    ppermute x8, waiting for transfers between devices: 9.49 us -> 11.5 us  [send(): return lax.ppermute(x, 'patch', perm)]
  transfers between devices with their start and end apart: 9 -> 9, of which waited for: 6 -> 4; matrix products, arithmetic and copies ran while one was open for 1% -> 1% of each run, Pallas kernels for 11% -> 12%
where the time goes in v6:
time: 89.3 us; the launch traced here: 87.6 us
  blocking collectives  41 us (46%)
  starting transfers between devices  18.3 us (20%)
  Pallas kernels  14.7 us (16%)
  waiting for transfers between devices  11.5 us (13%)
  matrix products  1.11 us (1%)
    all_to_all x1, blocking collectives, shards(): terms = lax.all_to_all(terms, 'tp', 0, 0)  21.7 us
    all_to_all x1, blocking collectives, shards(): mixed = join(lax.all_to_all(pieces, 'tp', 0, 0))  19.3 us
    ppermute x8, starting transfers between devices, send(): return lax.ppermute(x, 'patch', perm)  12.4 us
    ppermute x8, waiting for transfers between devices, send(): return lax.ppermute(x, 'patch', perm)  11.5 us
    all_to_all x1, starting transfers between devices, shards(): kv = lax.all_to_all(copies, 'patch', 0, 0, axis_index_groups=groups)  5.94 us
    pallas_call x3, Pallas kernels, attend_remote(): pl.pallas_call(remote_kernel, in_specs=[VMEM] * 2, out_specs=VMEM, out_sh...  2.7 us
    pallas_call x1, Pallas kernels, modulate(): pl.pallas_call(modulate_kernel, in_specs=[ANY] * 3 + [HBM, ANY], out_spec...  2.67 us
    pallas_call x1, Pallas kernels, copies_of(): pl.pallas_call(copies_kernel, in_specs=[HBM], out_specs=HBM, out_shape=ja...  1.97 us
  transfers between devices with their start and end apart: 9, of which 4 were waited for; matrix products, arithmetic and copies ran while one was open for 1% of the time, Pallas kernels for 12%

profile of v6, /device:TPU:32, one launch (start us, length us, event | category | flops | bytes accessed | tf_op | source)
XLA Modules:
  0.0 87.6 jit_solution(12139395381016352952)
XLA Ops:
  0.7 2.0 %copies_of.1._ = bf16[8,2,192,128]{3,2,1,0:T(8,128)(2,1)} custom-call(bf16[2,192,256]{2,1,0:T(8,128)(2,1)} %stale_ref.1), custom_call_target="tpu_custom_call" | custom-call | tf_op jit(solution)/shard_map/copies_of/pallas_call | solution.py:45
  2.6 5.9 %all-to-all-start = ((bf16[8,2,192,128]{3,2,1,0:T(8,128)(2,1)}), bf16[8,2,192,128]{3,2,1,0:T(8,128)(2,1)S(1)}, u32[]{:S(2)}, u32[]{:S(2)}) async-start(bf16[8,2,192,128]{3,2,1,0:T(8,128)(2,1)} %copies_of.1._), calls=%async_computation | async-start | bytes 1572864 | tf_op jit(solution)/shard_map/all_to_all | solution.py:361
  8.6 2.7 %modulate.1 = (bf16[192,3072]{1,0:T(8,128)(2,1)S(1)}, bf16[3,3072,256]{2,1,0:T(8,128)(2,1)S(1)}) custom-call(bf16[192,3072]{1,0:T(8,128)(2,1)S(1)} %copy-done, f32[3072]{0:T(1024)S(1)} %copy-done.2, f32[3072]{0:T(1024)S(1)} %copy-done.3, bf16[3,3072,256]{2,1,0:T(8,128)(2,1)} %bitcast.22, bf16[8,2,192,128]{3,2,1,0:T(8,128)(2,1)} %copies_of.1._), custom_call_target="tpu_custom_call" | custom-call | tf_op jit(solution)/shard_map/modulate/pallas_call | solution.py:91
  11.3 0.1 pad_add_fusion.c_ref
  11.4 1.1 %convolution_bitcast_fusion.sums_ref = f32[3,192,256]{2,1,0:T(8,128)S(1)} fusion(bf16[3,3072,256]{2,1,0:T(8,128)(2,1)S(1)} %get-tuple-element.13, bf16[192,3072]{1,0:T(8,128)(2,1)S(1)} %get-tuple-element.14), kind=kOutput, calls=%fused_computation | convolution fusion | flops 905969664 | bytes 6488064 | tf_op jit(solution)/shard_map/tf,jfc->jtc/dot_general | solution.py:128
  12.5 1.4 %finish.1 = (bf16[2,192,256]{2,1,0:T(8,128)(2,1)}, bf16[3,192,128]{2,1,0:T(8,128)(2,1)S(1)}, bf16[3,192,128]{2,1,0:T(8,128)(2,1)S(1)}) custom-call(s32[2]{0:T(128)S(1)} %pad_add_fusion.c_ref, f32[3,192,256]{2,1,0:T(8,128)S(1)} %convolution_bitcast_fusion.sums_ref, f32[3,256]{1,0:T(4,128)S(1)} %copy-done.6, f32[1,128]{1,0:T(1,128)S(1)} %bitcast.20, ...), custom_call_target="tpu_custom_call" | custom-call | tf_op jit(solution)/shard_map/finish/pallas_call | solution.py:130
  13.9 0.1 collective-permute-start
  14.1 1.2 %collective-permute-done.other_ref = bf16[3,192,128]{2,1,0:T(8,128)(2,1)S(1)} collective-permute-done((bf16[3,192,128]{2,1,0:T(8,128)(2,1)S(1)}, bf16[3,192,128]{2,1,0:T(8,128)(2,1)S(1)}, u32[]{:S(2)}, u32[]{:S(2)}) %collective-permute-start) | collective-permute-done | bytes 147488 | tf_op jit(solution)/shard_map/ppermute | solution.py:357
  15.3 5.1 %collective-permute-start.5 = (bf16[384,128]{1,0:T(8,128)(2,1)S(1)}, bf16[384,128]{1,0:T(8,128)(2,1)S(1)}, u32[]{:S(2)}, u32[]{:S(2)}) collective-permute-start(bf16[384,128]{1,0:T(8,128)(2,1)S(1)} %pad_maximum_fusion.q_ref), channel_id=1, source_target_pairs={{0,112},{8,120},{16,96},{24,104},{32,80},{40,88},{48,64},{56,72},{... | collective-permute-start | bytes 294920 | tf_op jit(solution)/shard_map/ppermute | solution.py:357
  20.4 1.9 %collective-permute-start.3 = (bf16[384,128]{1,0:T(8,128)(2,1)S(1)}, bf16[384,128]{1,0:T(8,128)(2,1)S(1)}, u32[]{:S(2)}, u32[]{:S(2)}) collective-permute-start(bf16[384,128]{1,0:T(8,128)(2,1)S(1)} %pad_maximum_fusion.q_ref), channel_id=1, source_target_pairs={{0,48},{8,56},{16,32},{24,40},{32,16},{40,24},{48,0},{56,8},{64,11... | collective-permute-start | bytes 294920 | tf_op jit(solution)/shard_map/ppermute | solution.py:357
  22.3 1.0 %collective-permute-start.1 = (bf16[384,128]{1,0:T(8,128)(2,1)S(1)}, bf16[384,128]{1,0:T(8,128)(2,1)S(1)}, u32[]{:S(2)}, u32[]{:S(2)}) collective-permute-start(bf16[384,128]{1,0:T(8,128)(2,1)S(1)} %pad_maximum_fusion.q_ref), channel_id=1, source_target_pairs={{0,80},{8,88},{16,64},{24,72},{32,112},{40,120},{48,96},{56,104},{... | collective-permute-start | bytes 294920 | tf_op jit(solution)/shard_map/ppermute | solution.py:357
  23.3 6.5 %collective-permute-done.5.q_ref = bf16[384,128]{1,0:T(8,128)(2,1)S(1)} collective-permute-done((bf16[384,128]{1,0:T(8,128)(2,1)S(1)}, bf16[384,128]{1,0:T(8,128)(2,1)S(1)}, u32[]{:S(2)}, u32[]{:S(2)}) %collective-permute-start.5) | collective-permute-done | bytes 98336 | tf_op jit(solution)/shard_map/ppermute | solution.py:357
  29.7 0.0 all-to-all-done.kv_ref
  29.7 0.9 %attend_remote.5 = bf16[432,128]{1,0:T(8,128)(2,1)S(1)} custom-call(bf16[384,128]{1,0:T(8,128)(2,1)S(1)} %collective-permute-done.5.q_ref, bf16[8,2,192,128]{3,2,1,0:T(8,128)(2,1)S(1)} %all-to-all-done.kv_ref), custom_call_target="tpu_custom_call" | custom-call | tf_op jit(solution)/shard_map/attend_remote/pallas_call | solution.py:168
  30.6 0.0 copy-start.1
  30.6 0.1 collective-permute-start.6
  30.8 0.9 %attend_remote.4 = bf16[432,128]{1,0:T(8,128)(2,1)S(1)} custom-call(bf16[384,128]{1,0:T(8,128)(2,1)S(1)} %collective-permute-done.3.q_ref, bf16[8,2,192,128]{3,2,1,0:T(8,128)(2,1)S(1)} %all-to-all-done.kv_ref), custom_call_target="tpu_custom_call" | custom-call | tf_op jit(solution)/shard_map/attend_remote/pallas_call | solution.py:168
  31.7 1.0 %collective-permute-start.4 = (bf16[432,128]{1,0:T(8,128)(2,1)S(1)}, bf16[432,128]{1,0:T(8,128)(2,1)S(1)}, u32[]{:S(2)}, u32[]{:S(2)}) collective-permute-start(bf16[432,128]{1,0:T(8,128)(2,1)S(1)} %attend_remote.4), channel_id=1, source_target_pairs={{0,48},{8,56},{16,32},{24,40},{32,16},{40,24},{48,0},{56,8},{64,11... | collective-permute-start | bytes 331784 | tf_op jit(solution)/shard_map/ppermute | solution.py:357
  32.7 0.0 collective-permute-done.1.q_ref
  32.7 0.9 %attend_remote.3 = bf16[432,128]{1,0:T(8,128)(2,1)S(1)} custom-call(bf16[384,128]{1,0:T(8,128)(2,1)S(1)} %collective-permute-done.1.q_ref, bf16[8,2,192,128]{3,2,1,0:T(8,128)(2,1)S(1)} %all-to-all-done.kv_ref), custom_call_target="tpu_custom_call" | custom-call | tf_op jit(solution)/shard_map/attend_remote/pallas_call | solution.py:168
  33.6 3.1 %collective-permute-start.2 = (bf16[432,128]{1,0:T(8,128)(2,1)S(1)}, bf16[432,128]{1,0:T(8,128)(2,1)S(1)}, u32[]{:S(2)}, u32[]{:S(2)}) collective-permute-start(bf16[432,128]{1,0:T(8,128)(2,1)S(1)} %attend_remote.3), channel_id=1, source_target_pairs={{0,80},{8,88},{16,64},{24,72},{32,112},{40,120},{48,96},{56,104},{... | collective-permute-start | bytes 331784 | tf_op jit(solution)/shard_map/ppermute | solution.py:357
  36.6 1.9 %attend_local.1._.local_ref = f32[384,256]{1,0:T(8,128)S(1)} custom-call(s32[2]{0:T(128)S(1)} %pad_add_fusion.c_ref, bf16[384,128]{1,0:T(8,128)(2,1)S(1)} %pad_maximum_fusion.q_ref, bf16[3,192,128]{2,1,0:T(8,128)(2,1)S(1)} %get-tuple-element.15.own_ref, bf16[3,192,128]{2,1,0:T(8,128)(2,1)S(1)} %collective-permute-done.other_ref, ...), custom_call_target="tpu_custom_call" | custom-call | tf_op jit(solution)/shard_map/attend_local/pallas_call | solution.py:196
  38.6 1.5 %edge.1 = (bf16[256,3072]{1,0:T(8,128)(2,1)S(1)}, bf16[192,384]{1,0:T(8,128)(2,1)S(1)}, f32[1,384]{1,0:T(1,128)S(1)}, f32[1,384]{1,0:T(1,128)S(1)}) custom-call(s32[1]{0:T(128)} %bitcast.9.t_ref, bf16[256,3072]{1,0:T(8,128)(2,1)} %w_ref.1, bf16[192,3072]{1,0:T(8,128)(2,1)S(1)} %copy-done, f32[1,3072]{1,0:T(1,128)S(1)} %bitcast.18, f32[1,3072]{1,0:T(1,128)S(1)} %bitcast.19, ...), custom_call_target="tpu_custom_call" | custom-call | tf_op jit(solution)/shard_map/edge/pallas_call | solution.py:274
  40.1 2.6 %collective-permute-done.2.p1_ref = bf16[432,128]{1,0:T(8,128)(2,1)S(1)} collective-permute-done((bf16[432,128]{1,0:T(8,128)(2,1)S(1)}, bf16[432,128]{1,0:T(8,128)(2,1)S(1)}, u32[]{:S(2)}, u32[]{:S(2)}) %collective-permute-start.2) | collective-permute-done | bytes 110624 | tf_op jit(solution)/shard_map/ppermute | solution.py:357
  42.7 0.1 combine.1
  42.9 0.1 collective-permute-start.7
  43.0 1.2 %collective-permute-done.7.swapped_ref = bf16[192,128]{1,0:T(8,128)(2,1)S(1)} collective-permute-done((bf16[192,128]{1,0:T(8,128)(2,1)S(1)}, bf16[192,128]{1,0:T(8,128)(2,1)S(1)}, u32[]{:S(2)}, u32[]{:S(2)}) %collective-permute-start.7) | collective-permute-done | bytes 49184 | tf_op jit(solution)/shard_map/ppermute | solution.py:357
  44.2 1.1 %terms_of.1 = bf16[8,192,384]{2,1,0:T(8,128)(2,1)S(1)} custom-call(s32[2]{0:T(128)S(1)} %pad_add_fusion.c_ref, bf16[192,128]{1,0:T(8,128)(2,1)S(1)} %get-tuple-element.18.kept_ref, bf16[192,128]{1,0:T(8,128)(2,1)S(1)} %collective-permute-done.7.swapped_ref, bf16[256,3072]{1,0:T(8,128)(2,1)S(1)} %get-tuple-element.17._.w_ref), custom_call_target="tpu_custom_call" | custom-call | tf_op jit(solution)/shard_map/terms_of/pallas_call | solution.py:253
  45.3 21.7 %all_to_all.15.terms_ref = bf16[8,192,384]{2,1,0:T(8,128)(2,1)S(1)} all-to-all(bf16[8,192,384]{2,1,0:T(8,128)(2,1)S(1)} %terms_of.1), channel_id=1, replica_groups=mesh['patch'=32,'tp'=8] {'tp'}, dimensions={0} | all-to-all | bytes 2359296 | tf_op jit(solution)/shard_map/all_to_all | solution.py:377
  67.0 0.2 mix.1
  67.2 19.3 %all_to_all.16.pieces_ref = bf16[8,192,384]{2,1,0:T(8,128)(2,1)S(1)} all-to-all(bf16[8,192,384]{2,1,0:T(8,128)(2,1)S(1)} %mix.1), channel_id=1, replica_groups=mesh['patch'=32,'tp'=8] {'tp'}, dimensions={0} | all-to-all | bytes 2359296 | tf_op jit(solution)/shard_map/all_to_all | solution.py:379
  86.5 1.1 %join.1 = bf16[192,3072]{1,0:T(8,128)(2,1)} custom-call(bf16[8,192,384]{2,1,0:T(8,128)(2,1)S(1)} %all_to_all.16.pieces_ref), custom_call_target="tpu_custom_call" | custom-call | tf_op jit(solution)/shard_map/join/pallas_call | solution.py:325
  (23 shorter events, 0.1 us)
Async XLA Ops:
  0.6 7.9 %copy-start = (bf16[192,3072]{1,0:T(8,128)(2,1)S(1)}, bf16[192,3072]{1,0:T(8,128)(2,1)}, u32[]{:S(2)}) copy-start(bf16[192,3072]{1,0:T(8,128)(2,1)} %image_ref.3) | copy-start | bytes 3538948
  0.6 7.9 %copy-start.2 = (f32[3072]{0:T(1024)S(1)}, f32[3072]{0:T(1024)}, u32[]{:S(2)}) copy-start(f32[3072]{0:T(1024)} %shift_ref.1) | copy-start | bytes 36868
  0.7 7.9 %copy-start.3 = (f32[3072]{0:T(1024)S(1)}, f32[3072]{0:T(1024)}, u32[]{:S(2)}) copy-start(f32[3072]{0:T(1024)} %scale_ref.1) | copy-start | bytes 36868
  2.6 27.1 %all-to-all-start = ((bf16[8,2,192,128]{3,2,1,0:T(8,128)(2,1)}), bf16[8,2,192,128]{3,2,1,0:T(8,128)(2,1)S(1)}, u32[]{:S(2)}, u32[]{:S(2)}) async-start(bf16[8,2,192,128]{3,2,1,0:T(8,128)(2,1)} %copies_of.1._), calls=%async_computation | async-start | bytes 1572864 | tf_op jit(solution)/shard_map/all_to_all | solution.py:361
  11.4 1.1 %copy-start.6 = (f32[3,256]{1,0:T(4,128)S(1)}, f32[3,256]{1,0:T(4,128)}, u32[]{:S(2)}) copy-start(f32[3,256]{1,0:T(4,128)} %bias_ref.1) | copy-start | bytes 9220
  11.4 1.1 %copy-start.7 = (f32[128]{0:T(128)S(1)}, f32[128]{0:T(128)}, u32[]{:S(2)}) copy-start(f32[128]{0:T(128)} %param.18) | copy-start | bytes 1540
  11.4 1.1 %copy-start.8 = (f32[128]{0:T(128)S(1)}, f32[128]{0:T(128)}, u32[]{:S(2)}) copy-start(f32[128]{0:T(128)} %param.19) | copy-start | bytes 1540
  13.9 1.4 %collective-permute-start = (bf16[3,192,128]{2,1,0:T(8,128)(2,1)S(1)}, bf16[3,192,128]{2,1,0:T(8,128)(2,1)S(1)}, u32[]{:S(2)}, u32[]{:S(2)}) collective-permute-start(bf16[3,192,128]{2,1,0:T(8,128)(2,1)S(1)} %get-tuple-element.16), channel_id=1, source_target_pairs={{0,8},{8,0},{16,24},{24,16},{32,40},{40,32},{48,56},{56,48},{64,72... | collective-permute-start | bytes 442376 | tf_op jit(solution)/shard_map/ppermute | solution.py:357
  15.3 14.4 %collective-permute-start.5 = (bf16[384,128]{1,0:T(8,128)(2,1)S(1)}, bf16[384,128]{1,0:T(8,128)(2,1)S(1)}, u32[]{:S(2)}, u32[]{:S(2)}) collective-permute-start(bf16[384,128]{1,0:T(8,128)(2,1)S(1)} %pad_maximum_fusion.q_ref), channel_id=1, source_target_pairs={{0,112},{8,120},{16,96},{24,104},{32,80},{40,88},{48,64},{56,72},{... | collective-permute-start | bytes 294920 | tf_op jit(solution)/shard_map/ppermute | solution.py:357
  20.4 10.3 %collective-permute-start.3 = (bf16[384,128]{1,0:T(8,128)(2,1)S(1)}, bf16[384,128]{1,0:T(8,128)(2,1)S(1)}, u32[]{:S(2)}, u32[]{:S(2)}) collective-permute-start(bf16[384,128]{1,0:T(8,128)(2,1)S(1)} %pad_maximum_fusion.q_ref), channel_id=1, source_target_pairs={{0,48},{8,56},{16,32},{24,40},{32,16},{40,24},{48,0},{56,8},{64,11... | collective-permute-start | bytes 294920 | tf_op jit(solution)/shard_map/ppermute | solution.py:357
  22.3 10.4 %collective-permute-start.1 = (bf16[384,128]{1,0:T(8,128)(2,1)S(1)}, bf16[384,128]{1,0:T(8,128)(2,1)S(1)}, u32[]{:S(2)}, u32[]{:S(2)}) collective-permute-start(bf16[384,128]{1,0:T(8,128)(2,1)S(1)} %pad_maximum_fusion.q_ref), channel_id=1, source_target_pairs={{0,80},{8,88},{16,64},{24,72},{32,112},{40,120},{48,96},{56,104},{... | collective-permute-start | bytes 294920 | tf_op jit(solution)/shard_map/ppermute | solution.py:357
  30.6 6.0 %copy-start.1 = (bf16[2,512,256]{2,1,0:T(8,128)(2,1)S(1)}, bf16[2,512,256]{2,1,0:T(8,128)(2,1)}, u32[]{:S(2)}) copy-start(bf16[2,512,256]{2,1,0:T(8,128)(2,1)} %text_ref.1) | copy-start | bytes 1572868
  30.6 9.5 %collective-permute-start.6 = (bf16[432,128]{1,0:T(8,128)(2,1)S(1)}, bf16[432,128]{1,0:T(8,128)(2,1)S(1)}, u32[]{:S(2)}, u32[]{:S(2)}) collective-permute-start(bf16[432,128]{1,0:T(8,128)(2,1)S(1)} %attend_remote.5), channel_id=1, source_target_pairs={{0,112},{8,120},{16,96},{24,104},{32,80},{40,88},{48,64},{56,72},{... | collective-permute-start | bytes 331784 | tf_op jit(solution)/shard_map/ppermute | solution.py:357
  31.7 8.5 %collective-permute-start.4 = (bf16[432,128]{1,0:T(8,128)(2,1)S(1)}, bf16[432,128]{1,0:T(8,128)(2,1)S(1)}, u32[]{:S(2)}, u32[]{:S(2)}) collective-permute-start(bf16[432,128]{1,0:T(8,128)(2,1)S(1)} %attend_remote.4), channel_id=1, source_target_pairs={{0,48},{8,56},{16,32},{24,40},{32,16},{40,24},{48,0},{56,8},{64,11... | collective-permute-start | bytes 331784 | tf_op jit(solution)/shard_map/ppermute | solution.py:357
  33.6 9.2 %collective-permute-start.2 = (bf16[432,128]{1,0:T(8,128)(2,1)S(1)}, bf16[432,128]{1,0:T(8,128)(2,1)S(1)}, u32[]{:S(2)}, u32[]{:S(2)}) collective-permute-start(bf16[432,128]{1,0:T(8,128)(2,1)S(1)} %attend_remote.3), channel_id=1, source_target_pairs={{0,80},{8,88},{16,64},{24,72},{32,112},{40,120},{48,96},{56,104},{... | collective-permute-start | bytes 331784 | tf_op jit(solution)/shard_map/ppermute | solution.py:357
  36.6 2.0 %copy-start.4 = (f32[3072]{0:T(1024)S(1)}, f32[3072]{0:T(1024)}, u32[]{:S(2)}) copy-start(f32[3072]{0:T(1024)} %param.15) | copy-start | bytes 36868
  36.6 2.0 %copy-start.5 = (f32[3072]{0:T(1024)S(1)}, f32[3072]{0:T(1024)}, u32[]{:S(2)}) copy-start(f32[3072]{0:T(1024)} %param.23) | copy-start | bytes 36868
  42.9 1.3 %collective-permute-start.7 = (bf16[192,128]{1,0:T(8,128)(2,1)S(1)}, bf16[192,128]{1,0:T(8,128)(2,1)S(1)}, u32[]{:S(2)}, u32[]{:S(2)}) collective-permute-start(bf16[192,128]{1,0:T(8,128)(2,1)S(1)} %get-tuple-element.19), channel_id=1, source_target_pairs={{0,8},{8,0},{16,24},{24,16},{32,40},{40,32},{48,56},{56,48},{64,72... | collective-permute-start | bytes 147464 | tf_op jit(solution)/shard_map/ppermute | solution.py:357

commit v7 on v6

--- a/solution.py
+++ b/solution.py
@@ -155,12 +155,13 @@
     k, v = (kv_ref[:, part].reshape(-1, hd) for part in (0, 1))
     total = block_sums(q_ref[...], k, v)
     out_ref[pl.ds(0, rows), :] = total[:, :hd].astype(BF)
+    place = lax.broadcasted_iota(jnp.int32, (16, hd), 0)
+    tile = jnp.zeros((16, hd), F32)
     for i in range(rows // hd):
         line = jnp.sum(total[i * hd : (i + 1) * hd, hd:] * same, 0, keepdims=True)
         high = line.astype(BF).astype(F32)
-        out_ref[pl.ds(rows + 16 * i, 16), :] = jnp.concatenate(
-            [jnp.broadcast_to(high, (8, hd)), jnp.broadcast_to(line - high, (8, hd))], 0
-        ).astype(BF)
+        tile = jnp.where(place == i, high, jnp.where(place == 8 + i, line - high, tile))
+    out_ref[pl.ds(rows, 16), :] = tile.astype(BF)
 
 
 def attend_remote(q, kv):
@@ -169,7 +170,7 @@
         remote_kernel,
         in_specs=[VMEM] * 2,
         out_specs=VMEM,
-        out_shape=jax.ShapeDtypeStruct((rows + 16 * (rows // hd), hd), BF),
+        out_shape=jax.ShapeDtypeStruct((rows + 16, hd), BF),
         compiler_params=params(),
         name="attend_remote",
     )(q, kv)
@@ -213,8 +214,8 @@
         line = None
         for p in (p1_ref, p2_ref, p3_ref):
             summed += p[at, :].astype(F32)
-            pair = p[pl.ds(rows + 16 * i, 16), :].astype(F32)
-            both = pair[0:1] + pair[8:9]
+            pair = p[pl.ds(rows, 16), :].astype(F32)
+            both = pair[i : i + 1] + pair[8 + i : 9 + i]
             line = both if line is None else line + both
         column = jnp.sum(jnp.broadcast_to(line, (hd, hd)) * same, 1, keepdims=True)
         done = (summed / (totals + column)).astype(BF)

time: 89.3 us -> 88.5 us (level)
  no operation moved by 1% of the time
where the time goes in v7:
time: 88.5 us; the launch traced here: 86.8 us
  blocking collectives  41 us (46%)
  starting transfers between devices  18.3 us (21%)
  Pallas kernels  14.7 us (17%)
  waiting for transfers between devices  10.7 us (12%)
  matrix products  1.11 us (1%)
    all_to_all x1, blocking collectives, shards(): terms = lax.all_to_all(terms, 'tp', 0, 0)  21.6 us
    all_to_all x1, blocking collectives, shards(): mixed = join(lax.all_to_all(pieces, 'tp', 0, 0))  19.3 us
    ppermute x8, starting transfers between devices, send(): return lax.ppermute(x, 'patch', perm)  12.4 us
    ppermute x8, waiting for transfers between devices, send(): return lax.ppermute(x, 'patch', perm)  10.7 us
    all_to_all x1, starting transfers between devices, shards(): kv = lax.all_to_all(copies, 'patch', 0, 0, axis_index_groups=groups)  5.94 us
    pallas_call x3, Pallas kernels, attend_remote(): pl.pallas_call(remote_kernel, in_specs=[VMEM] * 2, out_specs=VMEM, out_sh...  2.69 us
    pallas_call x1, Pallas kernels, modulate(): pl.pallas_call(modulate_kernel, in_specs=[ANY] * 3 + [HBM, ANY], out_spec...  2.67 us
    pallas_call x1, Pallas kernels, copies_of(): pl.pallas_call(copies_kernel, in_specs=[HBM], out_specs=HBM, out_shape=ja...  1.97 us
  transfers between devices with their start and end apart: 9, of which 4 were waited for; matrix products, arithmetic and copies ran while one was open for 1% of the time, Pallas kernels for 12%

profile of v7, /device:TPU:32, one launch (start us, length us, event | category | flops | bytes accessed | tf_op | source)
XLA Modules:
  0.0 86.8 jit_solution(6645409627174845048)
XLA Ops:
  0.7 2.0 %copies_of.1._ = bf16[8,2,192,128]{3,2,1,0:T(8,128)(2,1)} custom-call(bf16[2,192,256]{2,1,0:T(8,128)(2,1)} %stale_ref.1), custom_call_target="tpu_custom_call" | custom-call | tf_op jit(solution)/shard_map/copies_of/pallas_call | solution.py:45
  2.6 5.9 %all-to-all-start = ((bf16[8,2,192,128]{3,2,1,0:T(8,128)(2,1)}), bf16[8,2,192,128]{3,2,1,0:T(8,128)(2,1)S(1)}, u32[]{:S(2)}, u32[]{:S(2)}) async-start(bf16[8,2,192,128]{3,2,1,0:T(8,128)(2,1)} %copies_of.1._), calls=%async_computation | async-start | bytes 1572864 | tf_op jit(solution)/shard_map/all_to_all | solution.py:362
  8.6 2.7 %modulate.1 = (bf16[192,3072]{1,0:T(8,128)(2,1)S(1)}, bf16[3,3072,256]{2,1,0:T(8,128)(2,1)S(1)}) custom-call(bf16[192,3072]{1,0:T(8,128)(2,1)S(1)} %copy-done, f32[3072]{0:T(1024)S(1)} %copy-done.2, f32[3072]{0:T(1024)S(1)} %copy-done.3, bf16[3,3072,256]{2,1,0:T(8,128)(2,1)} %bitcast.22, bf16[8,2,192,128]{3,2,1,0:T(8,128)(2,1)} %copies_of.1._), custom_call_target="tpu_custom_call" | custom-call | tf_op jit(solution)/shard_map/modulate/pallas_call | solution.py:91
  11.3 0.1 pad_add_fusion.c_ref
  11.4 1.1 %convolution_bitcast_fusion.sums_ref = f32[3,192,256]{2,1,0:T(8,128)S(1)} fusion(bf16[3,3072,256]{2,1,0:T(8,128)(2,1)S(1)} %get-tuple-element.13, bf16[192,3072]{1,0:T(8,128)(2,1)S(1)} %get-tuple-element.14), kind=kOutput, calls=%fused_computation | convolution fusion | flops 905969664 | bytes 6488064 | tf_op jit(solution)/shard_map/tf,jfc->jtc/dot_general | solution.py:128
  12.5 1.4 %finish.1 = (bf16[2,192,256]{2,1,0:T(8,128)(2,1)}, bf16[3,192,128]{2,1,0:T(8,128)(2,1)S(1)}, bf16[3,192,128]{2,1,0:T(8,128)(2,1)S(1)}) custom-call(s32[2]{0:T(128)S(1)} %pad_add_fusion.c_ref, f32[3,192,256]{2,1,0:T(8,128)S(1)} %convolution_bitcast_fusion.sums_ref, f32[3,256]{1,0:T(4,128)S(1)} %copy-done.6, f32[1,128]{1,0:T(1,128)S(1)} %bitcast.20, ...), custom_call_target="tpu_custom_call" | custom-call | tf_op jit(solution)/shard_map/finish/pallas_call | solution.py:130
  13.9 0.1 collective-permute-start
  14.1 1.2 %collective-permute-done.other_ref = bf16[3,192,128]{2,1,0:T(8,128)(2,1)S(1)} collective-permute-done((bf16[3,192,128]{2,1,0:T(8,128)(2,1)S(1)}, bf16[3,192,128]{2,1,0:T(8,128)(2,1)S(1)}, u32[]{:S(2)}, u32[]{:S(2)}) %collective-permute-start) | collective-permute-done | bytes 147488 | tf_op jit(solution)/shard_map/ppermute | solution.py:358
  15.3 5.1 %collective-permute-start.5 = (bf16[384,128]{1,0:T(8,128)(2,1)S(1)}, bf16[384,128]{1,0:T(8,128)(2,1)S(1)}, u32[]{:S(2)}, u32[]{:S(2)}) collective-permute-start(bf16[384,128]{1,0:T(8,128)(2,1)S(1)} %pad_maximum_fusion.q_ref), channel_id=1, source_target_pairs={{0,112},{8,120},{16,96},{24,104},{32,80},{40,88},{48,64},{56,72},{... | collective-permute-start | bytes 294920 | tf_op jit(solution)/shard_map/ppermute | solution.py:358
  20.4 1.9 %collective-permute-start.3 = (bf16[384,128]{1,0:T(8,128)(2,1)S(1)}, bf16[384,128]{1,0:T(8,128)(2,1)S(1)}, u32[]{:S(2)}, u32[]{:S(2)}) collective-permute-start(bf16[384,128]{1,0:T(8,128)(2,1)S(1)} %pad_maximum_fusion.q_ref), channel_id=1, source_target_pairs={{0,48},{8,56},{16,32},{24,40},{32,16},{40,24},{48,0},{56,8},{64,11... | collective-permute-start | bytes 294920 | tf_op jit(solution)/shard_map/ppermute | solution.py:358
  22.3 1.0 %collective-permute-start.1 = (bf16[384,128]{1,0:T(8,128)(2,1)S(1)}, bf16[384,128]{1,0:T(8,128)(2,1)S(1)}, u32[]{:S(2)}, u32[]{:S(2)}) collective-permute-start(bf16[384,128]{1,0:T(8,128)(2,1)S(1)} %pad_maximum_fusion.q_ref), channel_id=1, source_target_pairs={{0,80},{8,88},{16,64},{24,72},{32,112},{40,120},{48,96},{56,104},{... | collective-permute-start | bytes 294920 | tf_op jit(solution)/shard_map/ppermute | solution.py:358
  23.3 6.5 %collective-permute-done.5.q_ref = bf16[384,128]{1,0:T(8,128)(2,1)S(1)} collective-permute-done((bf16[384,128]{1,0:T(8,128)(2,1)S(1)}, bf16[384,128]{1,0:T(8,128)(2,1)S(1)}, u32[]{:S(2)}, u32[]{:S(2)}) %collective-permute-start.5) | collective-permute-done | bytes 98336 | tf_op jit(solution)/shard_map/ppermute | solution.py:358
  29.7 0.9 %attend_remote.5 = bf16[400,128]{1,0:T(8,128)(2,1)S(1)} custom-call(bf16[384,128]{1,0:T(8,128)(2,1)S(1)} %collective-permute-done.5.q_ref, bf16[8,2,192,128]{3,2,1,0:T(8,128)(2,1)S(1)} %all-to-all-done.kv_ref), custom_call_target="tpu_custom_call" | custom-call | tf_op jit(solution)/shard_map/attend_remote/pallas_call | solution.py:169
  30.6 0.0 copy-start.1
  30.6 0.1 collective-permute-start.6
  30.8 0.9 %attend_remote.4 = bf16[400,128]{1,0:T(8,128)(2,1)S(1)} custom-call(bf16[384,128]{1,0:T(8,128)(2,1)S(1)} %collective-permute-done.3.q_ref, bf16[8,2,192,128]{3,2,1,0:T(8,128)(2,1)S(1)} %all-to-all-done.kv_ref), custom_call_target="tpu_custom_call" | custom-call | tf_op jit(solution)/shard_map/attend_remote/pallas_call | solution.py:169
  31.7 1.0 %collective-permute-start.4 = (bf16[400,128]{1,0:T(8,128)(2,1)S(1)}, bf16[400,128]{1,0:T(8,128)(2,1)S(1)}, u32[]{:S(2)}, u32[]{:S(2)}) collective-permute-start(bf16[400,128]{1,0:T(8,128)(2,1)S(1)} %attend_remote.4), channel_id=1, source_target_pairs={{0,48},{8,56},{16,32},{24,40},{32,16},{40,24},{48,0},{56,8},{64,11... | collective-permute-start | bytes 307208 | tf_op jit(solution)/shard_map/ppermute | solution.py:358
  32.7 0.9 %attend_remote.3 = bf16[400,128]{1,0:T(8,128)(2,1)S(1)} custom-call(bf16[384,128]{1,0:T(8,128)(2,1)S(1)} %collective-permute-done.1.q_ref, bf16[8,2,192,128]{3,2,1,0:T(8,128)(2,1)S(1)} %all-to-all-done.kv_ref), custom_call_target="tpu_custom_call" | custom-call | tf_op jit(solution)/shard_map/attend_remote/pallas_call | solution.py:169
  33.6 0.0 copy-start.4
  33.6 0.0 copy-start.5
  33.6 3.1 %collective-permute-start.2 = (bf16[400,128]{1,0:T(8,128)(2,1)S(1)}, bf16[400,128]{1,0:T(8,128)(2,1)S(1)}, u32[]{:S(2)}, u32[]{:S(2)}) collective-permute-start(bf16[400,128]{1,0:T(8,128)(2,1)S(1)} %attend_remote.3), channel_id=1, source_target_pairs={{0,80},{8,88},{16,64},{24,72},{32,112},{40,120},{48,96},{56,104},{... | collective-permute-start | bytes 307208 | tf_op jit(solution)/shard_map/ppermute | solution.py:358
  36.7 1.9 %attend_local.1._.local_ref = f32[384,256]{1,0:T(8,128)S(1)} custom-call(s32[2]{0:T(128)S(1)} %pad_add_fusion.c_ref, bf16[384,128]{1,0:T(8,128)(2,1)S(1)} %pad_maximum_fusion.q_ref, bf16[3,192,128]{2,1,0:T(8,128)(2,1)S(1)} %get-tuple-element.15.own_ref, bf16[3,192,128]{2,1,0:T(8,128)(2,1)S(1)} %collective-permute-done.other_ref, ...), custom_call_target="tpu_custom_call" | custom-call | tf_op jit(solution)/shard_map/attend_local/pallas_call | solution.py:197
  38.6 1.5 %edge.1 = (bf16[256,3072]{1,0:T(8,128)(2,1)S(1)}, bf16[192,384]{1,0:T(8,128)(2,1)S(1)}, f32[1,384]{1,0:T(1,128)S(1)}, f32[1,384]{1,0:T(1,128)S(1)}) custom-call(s32[1]{0:T(128)} %bitcast.9.t_ref, bf16[256,3072]{1,0:T(8,128)(2,1)} %w_ref.1, bf16[192,3072]{1,0:T(8,128)(2,1)S(1)} %copy-done, f32[1,3072]{1,0:T(1,128)S(1)} %bitcast.18, f32[1,3072]{1,0:T(1,128)S(1)} %bitcast.19, ...), custom_call_target="tpu_custom_call" | custom-call | tf_op jit(solution)/shard_map/edge/pallas_call | solution.py:275
  40.2 1.8 %collective-permute-done.2.p1_ref = bf16[400,128]{1,0:T(8,128)(2,1)S(1)} collective-permute-done((bf16[400,128]{1,0:T(8,128)(2,1)S(1)}, bf16[400,128]{1,0:T(8,128)(2,1)S(1)}, u32[]{:S(2)}, u32[]{:S(2)}) %collective-permute-start.2) | collective-permute-done | bytes 102432 | tf_op jit(solution)/shard_map/ppermute | solution.py:358
  42.0 0.1 combine.1
  42.1 0.1 collective-permute-start.7
  42.2 1.2 %collective-permute-done.7.swapped_ref = bf16[192,128]{1,0:T(8,128)(2,1)S(1)} collective-permute-done((bf16[192,128]{1,0:T(8,128)(2,1)S(1)}, bf16[192,128]{1,0:T(8,128)(2,1)S(1)}, u32[]{:S(2)}, u32[]{:S(2)}) %collective-permute-start.7) | collective-permute-done | bytes 49184 | tf_op jit(solution)/shard_map/ppermute | solution.py:358
  43.4 1.1 %terms_of.1 = bf16[8,192,384]{2,1,0:T(8,128)(2,1)S(1)} custom-call(s32[2]{0:T(128)S(1)} %pad_add_fusion.c_ref, bf16[192,128]{1,0:T(8,128)(2,1)S(1)} %get-tuple-element.18.kept_ref, bf16[192,128]{1,0:T(8,128)(2,1)S(1)} %collective-permute-done.7.swapped_ref, bf16[256,3072]{1,0:T(8,128)(2,1)S(1)} %get-tuple-element.17._.w_ref), custom_call_target="tpu_custom_call" | custom-call | tf_op jit(solution)/shard_map/terms_of/pallas_call | solution.py:254
  44.5 21.6 %all_to_all.15.terms_ref = bf16[8,192,384]{2,1,0:T(8,128)(2,1)S(1)} all-to-all(bf16[8,192,384]{2,1,0:T(8,128)(2,1)S(1)} %terms_of.1), channel_id=1, replica_groups=mesh['patch'=32,'tp'=8] {'tp'}, dimensions={0} | all-to-all | bytes 2359296 | tf_op jit(solution)/shard_map/all_to_all | solution.py:378
  66.2 0.2 mix.1
  66.4 19.3 %all_to_all.16.pieces_ref = bf16[8,192,384]{2,1,0:T(8,128)(2,1)S(1)} all-to-all(bf16[8,192,384]{2,1,0:T(8,128)(2,1)S(1)} %mix.1), channel_id=1, replica_groups=mesh['patch'=32,'tp'=8] {'tp'}, dimensions={0} | all-to-all | bytes 2359296 | tf_op jit(solution)/shard_map/all_to_all | solution.py:380
  85.7 1.1 %join.1 = bf16[192,3072]{1,0:T(8,128)(2,1)} custom-call(bf16[8,192,384]{2,1,0:T(8,128)(2,1)S(1)} %all_to_all.16.pieces_ref), custom_call_target="tpu_custom_call" | custom-call | tf_op jit(solution)/shard_map/join/pallas_call | solution.py:326
  (23 shorter events, 0.1 us)
Async XLA Ops:
  0.6 7.9 %copy-start = (bf16[192,3072]{1,0:T(8,128)(2,1)S(1)}, bf16[192,3072]{1,0:T(8,128)(2,1)}, u32[]{:S(2)}) copy-start(bf16[192,3072]{1,0:T(8,128)(2,1)} %image_ref.3) | copy-start | bytes 3538948
  0.6 7.9 %copy-start.2 = (f32[3072]{0:T(1024)S(1)}, f32[3072]{0:T(1024)}, u32[]{:S(2)}) copy-start(f32[3072]{0:T(1024)} %shift_ref.1) | copy-start | bytes 36868
  0.7 7.9 %copy-start.3 = (f32[3072]{0:T(1024)S(1)}, f32[3072]{0:T(1024)}, u32[]{:S(2)}) copy-start(f32[3072]{0:T(1024)} %scale_ref.1) | copy-start | bytes 36868
  2.6 27.1 %all-to-all-start = ((bf16[8,2,192,128]{3,2,1,0:T(8,128)(2,1)}), bf16[8,2,192,128]{3,2,1,0:T(8,128)(2,1)S(1)}, u32[]{:S(2)}, u32[]{:S(2)}) async-start(bf16[8,2,192,128]{3,2,1,0:T(8,128)(2,1)} %copies_of.1._), calls=%async_computation | async-start | bytes 1572864 | tf_op jit(solution)/shard_map/all_to_all | solution.py:362
  11.4 1.1 %copy-start.6 = (f32[3,256]{1,0:T(4,128)S(1)}, f32[3,256]{1,0:T(4,128)}, u32[]{:S(2)}) copy-start(f32[3,256]{1,0:T(4,128)} %bias_ref.1) | copy-start | bytes 9220
  11.4 1.1 %copy-start.7 = (f32[128]{0:T(128)S(1)}, f32[128]{0:T(128)}, u32[]{:S(2)}) copy-start(f32[128]{0:T(128)} %param.18) | copy-start | bytes 1540
  11.4 1.1 %copy-start.8 = (f32[128]{0:T(128)S(1)}, f32[128]{0:T(128)}, u32[]{:S(2)}) copy-start(f32[128]{0:T(128)} %param.19) | copy-start | bytes 1540
  13.9 1.4 %collective-permute-start = (bf16[3,192,128]{2,1,0:T(8,128)(2,1)S(1)}, bf16[3,192,128]{2,1,0:T(8,128)(2,1)S(1)}, u32[]{:S(2)}, u32[]{:S(2)}) collective-permute-start(bf16[3,192,128]{2,1,0:T(8,128)(2,1)S(1)} %get-tuple-element.16), channel_id=1, source_target_pairs={{0,8},{8,0},{16,24},{24,16},{32,40},{40,32},{48,56},{56,48},{64,72... | collective-permute-start | bytes 442376 | tf_op jit(solution)/shard_map/ppermute | solution.py:358
  15.3 14.4 %collective-permute-start.5 = (bf16[384,128]{1,0:T(8,128)(2,1)S(1)}, bf16[384,128]{1,0:T(8,128)(2,1)S(1)}, u32[]{:S(2)}, u32[]{:S(2)}) collective-permute-start(bf16[384,128]{1,0:T(8,128)(2,1)S(1)} %pad_maximum_fusion.q_ref), channel_id=1, source_target_pairs={{0,112},{8,120},{16,96},{24,104},{32,80},{40,88},{48,64},{56,72},{... | collective-permute-start | bytes 294920 | tf_op jit(solution)/shard_map/ppermute | solution.py:358
  20.4 10.3 %collective-permute-start.3 = (bf16[384,128]{1,0:T(8,128)(2,1)S(1)}, bf16[384,128]{1,0:T(8,128)(2,1)S(1)}, u32[]{:S(2)}, u32[]{:S(2)}) collective-permute-start(bf16[384,128]{1,0:T(8,128)(2,1)S(1)} %pad_maximum_fusion.q_ref), channel_id=1, source_target_pairs={{0,48},{8,56},{16,32},{24,40},{32,16},{40,24},{48,0},{56,8},{64,11... | collective-permute-start | bytes 294920 | tf_op jit(solution)/shard_map/ppermute | solution.py:358
  22.3 10.4 %collective-permute-start.1 = (bf16[384,128]{1,0:T(8,128)(2,1)S(1)}, bf16[384,128]{1,0:T(8,128)(2,1)S(1)}, u32[]{:S(2)}, u32[]{:S(2)}) collective-permute-start(bf16[384,128]{1,0:T(8,128)(2,1)S(1)} %pad_maximum_fusion.q_ref), channel_id=1, source_target_pairs={{0,80},{8,88},{16,64},{24,72},{32,112},{40,120},{48,96},{56,104},{... | collective-permute-start | bytes 294920 | tf_op jit(solution)/shard_map/ppermute | solution.py:358
  30.6 6.0 %copy-start.1 = (bf16[2,512,256]{2,1,0:T(8,128)(2,1)S(1)}, bf16[2,512,256]{2,1,0:T(8,128)(2,1)}, u32[]{:S(2)}) copy-start(bf16[2,512,256]{2,1,0:T(8,128)(2,1)} %text_ref.1) | copy-start | bytes 1572868
  30.6 9.5 %collective-permute-start.6 = (bf16[400,128]{1,0:T(8,128)(2,1)S(1)}, bf16[400,128]{1,0:T(8,128)(2,1)S(1)}, u32[]{:S(2)}, u32[]{:S(2)}) collective-permute-start(bf16[400,128]{1,0:T(8,128)(2,1)S(1)} %attend_remote.5), channel_id=1, source_target_pairs={{0,112},{8,120},{16,96},{24,104},{32,80},{40,88},{48,64},{56,72},{... | collective-permute-start | bytes 307208 | tf_op jit(solution)/shard_map/ppermute | solution.py:358
  31.7 8.5 %collective-permute-start.4 = (bf16[400,128]{1,0:T(8,128)(2,1)S(1)}, bf16[400,128]{1,0:T(8,128)(2,1)S(1)}, u32[]{:S(2)}, u32[]{:S(2)}) collective-permute-start(bf16[400,128]{1,0:T(8,128)(2,1)S(1)} %attend_remote.4), channel_id=1, source_target_pairs={{0,48},{8,56},{16,32},{24,40},{32,16},{40,24},{48,0},{56,8},{64,11... | collective-permute-start | bytes 307208 | tf_op jit(solution)/shard_map/ppermute | solution.py:358
  33.6 5.1 %copy-start.4 = (f32[3072]{0:T(1024)S(1)}, f32[3072]{0:T(1024)}, u32[]{:S(2)}) copy-start(f32[3072]{0:T(1024)} %param.15) | copy-start | bytes 36868
  33.6 5.1 %copy-start.5 = (f32[3072]{0:T(1024)S(1)}, f32[3072]{0:T(1024)}, u32[]{:S(2)}) copy-start(f32[3072]{0:T(1024)} %param.23) | copy-start | bytes 36868
  33.6 8.4 %collective-permute-start.2 = (bf16[400,128]{1,0:T(8,128)(2,1)S(1)}, bf16[400,128]{1,0:T(8,128)(2,1)S(1)}, u32[]{:S(2)}, u32[]{:S(2)}) collective-permute-start(bf16[400,128]{1,0:T(8,128)(2,1)S(1)} %attend_remote.3), channel_id=1, source_target_pairs={{0,80},{8,88},{16,64},{24,72},{32,112},{40,120},{48,96},{56,104},{... | collective-permute-start | bytes 307208 | tf_op jit(solution)/shard_map/ppermute | solution.py:358
  42.1 1.3 %collective-permute-start.7 = (bf16[192,128]{1,0:T(8,128)(2,1)S(1)}, bf16[192,128]{1,0:T(8,128)(2,1)S(1)}, u32[]{:S(2)}, u32[]{:S(2)}) collective-permute-start(bf16[192,128]{1,0:T(8,128)(2,1)S(1)} %get-tuple-element.19), channel_id=1, source_target_pairs={{0,8},{8,0},{16,24},{24,16},{32,40},{40,32},{48,56},{56,48},{64,72... | collective-permute-start | bytes 147464 | tf_op jit(solution)/shard_map/ppermute | solution.py:358

commit v8 on v7

--- a/solution.py
+++ b/solution.py
@@ -315,8 +315,11 @@
 
 
 def join_kernel(pieces_ref, out_ref, sems):
-    n, _, columns = pieces_ref.shape
-    copies = fetch([(pieces_ref.at[i], out_ref.at[:, pl.ds(i * columns, columns)]) for i in range(n)], sems)
+    n, rows, columns = pieces_ref.shape
+    pairs = []
+    for at in (pl.ds(0, rows // 2), pl.ds(rows // 2, rows // 2)):
+        pairs += [(pieces_ref.at[i, at], out_ref.at[at, pl.ds(i * columns, columns)]) for i in range(n)]
+    copies = fetch(pairs, sems)
     for copy in copies:
         copy.wait()
 
@@ -328,7 +331,7 @@
         in_specs=[ANY],
         out_specs=HBM,
         out_shape=jax.ShapeDtypeStruct((rows, n * columns), BF),
-        scratch_shapes=[pltpu.SemaphoreType.DMA((n,))],
+        scratch_shapes=[pltpu.SemaphoreType.DMA((2 * n,))],
         compiler_params=params(),
         name="join",
     )(pieces)

time: 88.5 us -> 88.6 us (level)
  no operation moved by 1% of the time
where the time goes in v8:
time: 88.6 us; the launch traced here: 86.8 us
  blocking collectives  41 us (46%)
  starting transfers between devices  18.3 us (21%)
  Pallas kernels  14.8 us (17%)
  waiting for transfers between devices  10.7 us (12%)
  matrix products  1.11 us (1%)
    all_to_all x1, blocking collectives, shards(): terms = lax.all_to_all(terms, 'tp', 0, 0)  21.6 us
    all_to_all x1, blocking collectives, shards(): mixed = join(lax.all_to_all(pieces, 'tp', 0, 0))  19.3 us
    ppermute x8, starting transfers between devices, send(): return lax.ppermute(x, 'patch', perm)  12.4 us
    ppermute x8, waiting for transfers between devices, send(): return lax.ppermute(x, 'patch', perm)  10.7 us
    all_to_all x1, starting transfers between devices, shards(): kv = lax.all_to_all(copies, 'patch', 0, 0, axis_index_groups=groups)  5.94 us
    pallas_call x3, Pallas kernels, attend_remote(): pl.pallas_call(remote_kernel, in_specs=[VMEM] * 2, out_specs=VMEM, out_sh...  2.69 us
    pallas_call x1, Pallas kernels, modulate(): pl.pallas_call(modulate_kernel, in_specs=[ANY] * 3 + [HBM, ANY], out_spec...  2.67 us
    pallas_call x1, Pallas kernels, copies_of(): pl.pallas_call(copies_kernel, in_specs=[HBM], out_specs=HBM, out_shape=ja...  1.97 us
  transfers between devices with their start and end apart: 9, of which 4 were waited for; matrix products, arithmetic and copies ran while one was open for 1% of the time, Pallas kernels for 12%

profile of v8, /device:TPU:32, one launch (start us, length us, event | category | flops | bytes accessed | tf_op | source)
XLA Modules:
  0.0 86.8 jit_solution(6779378829067920735)
XLA Ops:
  0.7 2.0 %copies_of.1._ = bf16[8,2,192,128]{3,2,1,0:T(8,128)(2,1)} custom-call(bf16[2,192,256]{2,1,0:T(8,128)(2,1)} %stale_ref.1), custom_call_target="tpu_custom_call" | custom-call | tf_op jit(solution)/shard_map/copies_of/pallas_call | solution.py:45
  2.6 5.9 %all-to-all-start = ((bf16[8,2,192,128]{3,2,1,0:T(8,128)(2,1)}), bf16[8,2,192,128]{3,2,1,0:T(8,128)(2,1)S(1)}, u32[]{:S(2)}, u32[]{:S(2)}) async-start(bf16[8,2,192,128]{3,2,1,0:T(8,128)(2,1)} %copies_of.1._), calls=%async_computation | async-start | bytes 1572864 | tf_op jit(solution)/shard_map/all_to_all | solution.py:365
  8.6 2.7 %modulate.1 = (bf16[192,3072]{1,0:T(8,128)(2,1)S(1)}, bf16[3,3072,256]{2,1,0:T(8,128)(2,1)S(1)}) custom-call(bf16[192,3072]{1,0:T(8,128)(2,1)S(1)} %copy-done, f32[3072]{0:T(1024)S(1)} %copy-done.2, f32[3072]{0:T(1024)S(1)} %copy-done.3, bf16[3,3072,256]{2,1,0:T(8,128)(2,1)} %bitcast.22, bf16[8,2,192,128]{3,2,1,0:T(8,128)(2,1)} %copies_of.1._), custom_call_target="tpu_custom_call" | custom-call | tf_op jit(solution)/shard_map/modulate/pallas_call | solution.py:91
  11.3 0.1 pad_add_fusion.c_ref
  11.4 1.1 %convolution_bitcast_fusion.sums_ref = f32[3,192,256]{2,1,0:T(8,128)S(1)} fusion(bf16[3,3072,256]{2,1,0:T(8,128)(2,1)S(1)} %get-tuple-element.13, bf16[192,3072]{1,0:T(8,128)(2,1)S(1)} %get-tuple-element.14), kind=kOutput, calls=%fused_computation | convolution fusion | flops 905969664 | bytes 6488064 | tf_op jit(solution)/shard_map/tf,jfc->jtc/dot_general | solution.py:128
  12.5 1.4 %finish.1 = (bf16[2,192,256]{2,1,0:T(8,128)(2,1)}, bf16[3,192,128]{2,1,0:T(8,128)(2,1)S(1)}, bf16[3,192,128]{2,1,0:T(8,128)(2,1)S(1)}) custom-call(s32[2]{0:T(128)S(1)} %pad_add_fusion.c_ref, f32[3,192,256]{2,1,0:T(8,128)S(1)} %convolution_bitcast_fusion.sums_ref, f32[3,256]{1,0:T(4,128)S(1)} %copy-done.6, f32[1,128]{1,0:T(1,128)S(1)} %bitcast.20, ...), custom_call_target="tpu_custom_call" | custom-call | tf_op jit(solution)/shard_map/finish/pallas_call | solution.py:130
  13.9 0.1 collective-permute-start
  14.1 1.2 %collective-permute-done.other_ref = bf16[3,192,128]{2,1,0:T(8,128)(2,1)S(1)} collective-permute-done((bf16[3,192,128]{2,1,0:T(8,128)(2,1)S(1)}, bf16[3,192,128]{2,1,0:T(8,128)(2,1)S(1)}, u32[]{:S(2)}, u32[]{:S(2)}) %collective-permute-start) | collective-permute-done | bytes 147488 | tf_op jit(solution)/shard_map/ppermute | solution.py:361
  15.3 5.1 %collective-permute-start.5 = (bf16[384,128]{1,0:T(8,128)(2,1)S(1)}, bf16[384,128]{1,0:T(8,128)(2,1)S(1)}, u32[]{:S(2)}, u32[]{:S(2)}) collective-permute-start(bf16[384,128]{1,0:T(8,128)(2,1)S(1)} %pad_maximum_fusion.q_ref), channel_id=1, source_target_pairs={{0,112},{8,120},{16,96},{24,104},{32,80},{40,88},{48,64},{56,72},{... | collective-permute-start | bytes 294920 | tf_op jit(solution)/shard_map/ppermute | solution.py:361
  20.4 1.9 %collective-permute-start.3 = (bf16[384,128]{1,0:T(8,128)(2,1)S(1)}, bf16[384,128]{1,0:T(8,128)(2,1)S(1)}, u32[]{:S(2)}, u32[]{:S(2)}) collective-permute-start(bf16[384,128]{1,0:T(8,128)(2,1)S(1)} %pad_maximum_fusion.q_ref), channel_id=1, source_target_pairs={{0,48},{8,56},{16,32},{24,40},{32,16},{40,24},{48,0},{56,8},{64,11... | collective-permute-start | bytes 294920 | tf_op jit(solution)/shard_map/ppermute | solution.py:361
  22.3 1.0 %collective-permute-start.1 = (bf16[384,128]{1,0:T(8,128)(2,1)S(1)}, bf16[384,128]{1,0:T(8,128)(2,1)S(1)}, u32[]{:S(2)}, u32[]{:S(2)}) collective-permute-start(bf16[384,128]{1,0:T(8,128)(2,1)S(1)} %pad_maximum_fusion.q_ref), channel_id=1, source_target_pairs={{0,80},{8,88},{16,64},{24,72},{32,112},{40,120},{48,96},{56,104},{... | collective-permute-start | bytes 294920 | tf_op jit(solution)/shard_map/ppermute | solution.py:361
  23.3 6.5 %collective-permute-done.5.q_ref = bf16[384,128]{1,0:T(8,128)(2,1)S(1)} collective-permute-done((bf16[384,128]{1,0:T(8,128)(2,1)S(1)}, bf16[384,128]{1,0:T(8,128)(2,1)S(1)}, u32[]{:S(2)}, u32[]{:S(2)}) %collective-permute-start.5) | collective-permute-done | bytes 98336 | tf_op jit(solution)/shard_map/ppermute | solution.py:361
  29.7 0.9 %attend_remote.5 = bf16[400,128]{1,0:T(8,128)(2,1)S(1)} custom-call(bf16[384,128]{1,0:T(8,128)(2,1)S(1)} %collective-permute-done.5.q_ref, bf16[8,2,192,128]{3,2,1,0:T(8,128)(2,1)S(1)} %all-to-all-done.kv_ref), custom_call_target="tpu_custom_call" | custom-call | tf_op jit(solution)/shard_map/attend_remote/pallas_call | solution.py:169
  30.6 0.0 copy-start.1
  30.6 0.1 collective-permute-start.6
  30.8 0.9 %attend_remote.4 = bf16[400,128]{1,0:T(8,128)(2,1)S(1)} custom-call(bf16[384,128]{1,0:T(8,128)(2,1)S(1)} %collective-permute-done.3.q_ref, bf16[8,2,192,128]{3,2,1,0:T(8,128)(2,1)S(1)} %all-to-all-done.kv_ref), custom_call_target="tpu_custom_call" | custom-call | tf_op jit(solution)/shard_map/attend_remote/pallas_call | solution.py:169
  31.7 1.0 %collective-permute-start.4 = (bf16[400,128]{1,0:T(8,128)(2,1)S(1)}, bf16[400,128]{1,0:T(8,128)(2,1)S(1)}, u32[]{:S(2)}, u32[]{:S(2)}) collective-permute-start(bf16[400,128]{1,0:T(8,128)(2,1)S(1)} %attend_remote.4), channel_id=1, source_target_pairs={{0,48},{8,56},{16,32},{24,40},{32,16},{40,24},{48,0},{56,8},{64,11... | collective-permute-start | bytes 307208 | tf_op jit(solution)/shard_map/ppermute | solution.py:361
  32.7 0.9 %attend_remote.3 = bf16[400,128]{1,0:T(8,128)(2,1)S(1)} custom-call(bf16[384,128]{1,0:T(8,128)(2,1)S(1)} %collective-permute-done.1.q_ref, bf16[8,2,192,128]{3,2,1,0:T(8,128)(2,1)S(1)} %all-to-all-done.kv_ref), custom_call_target="tpu_custom_call" | custom-call | tf_op jit(solution)/shard_map/attend_remote/pallas_call | solution.py:169
  33.6 0.0 copy-start.4
  33.6 0.0 copy-start.5
  33.6 3.1 %collective-permute-start.2 = (bf16[400,128]{1,0:T(8,128)(2,1)S(1)}, bf16[400,128]{1,0:T(8,128)(2,1)S(1)}, u32[]{:S(2)}, u32[]{:S(2)}) collective-permute-start(bf16[400,128]{1,0:T(8,128)(2,1)S(1)} %attend_remote.3), channel_id=1, source_target_pairs={{0,80},{8,88},{16,64},{24,72},{32,112},{40,120},{48,96},{56,104},{... | collective-permute-start | bytes 307208 | tf_op jit(solution)/shard_map/ppermute | solution.py:361
  36.7 1.9 %attend_local.1._.local_ref = f32[384,256]{1,0:T(8,128)S(1)} custom-call(s32[2]{0:T(128)S(1)} %pad_add_fusion.c_ref, bf16[384,128]{1,0:T(8,128)(2,1)S(1)} %pad_maximum_fusion.q_ref, bf16[3,192,128]{2,1,0:T(8,128)(2,1)S(1)} %get-tuple-element.15.own_ref, bf16[3,192,128]{2,1,0:T(8,128)(2,1)S(1)} %collective-permute-done.other_ref, ...), custom_call_target="tpu_custom_call" | custom-call | tf_op jit(solution)/shard_map/attend_local/pallas_call | solution.py:197
  38.6 1.5 %edge.1 = (bf16[256,3072]{1,0:T(8,128)(2,1)S(1)}, bf16[192,384]{1,0:T(8,128)(2,1)S(1)}, f32[1,384]{1,0:T(1,128)S(1)}, f32[1,384]{1,0:T(1,128)S(1)}) custom-call(s32[1]{0:T(128)} %bitcast.9.t_ref, bf16[256,3072]{1,0:T(8,128)(2,1)} %w_ref.1, bf16[192,3072]{1,0:T(8,128)(2,1)S(1)} %copy-done, f32[1,3072]{1,0:T(1,128)S(1)} %bitcast.18, f32[1,3072]{1,0:T(1,128)S(1)} %bitcast.19, ...), custom_call_target="tpu_custom_call" | custom-call | tf_op jit(solution)/shard_map/edge/pallas_call | solution.py:275
  40.2 1.8 %collective-permute-done.2.p1_ref = bf16[400,128]{1,0:T(8,128)(2,1)S(1)} collective-permute-done((bf16[400,128]{1,0:T(8,128)(2,1)S(1)}, bf16[400,128]{1,0:T(8,128)(2,1)S(1)}, u32[]{:S(2)}, u32[]{:S(2)}) %collective-permute-start.2) | collective-permute-done | bytes 102432 | tf_op jit(solution)/shard_map/ppermute | solution.py:361
  42.0 0.1 combine.1
  42.1 0.1 collective-permute-start.7
  42.2 1.2 %collective-permute-done.7.swapped_ref = bf16[192,128]{1,0:T(8,128)(2,1)S(1)} collective-permute-done((bf16[192,128]{1,0:T(8,128)(2,1)S(1)}, bf16[192,128]{1,0:T(8,128)(2,1)S(1)}, u32[]{:S(2)}, u32[]{:S(2)}) %collective-permute-start.7) | collective-permute-done | bytes 49184 | tf_op jit(solution)/shard_map/ppermute | solution.py:361
  43.4 1.1 %terms_of.1 = bf16[8,192,384]{2,1,0:T(8,128)(2,1)S(1)} custom-call(s32[2]{0:T(128)S(1)} %pad_add_fusion.c_ref, bf16[192,128]{1,0:T(8,128)(2,1)S(1)} %get-tuple-element.18.kept_ref, bf16[192,128]{1,0:T(8,128)(2,1)S(1)} %collective-permute-done.7.swapped_ref, bf16[256,3072]{1,0:T(8,128)(2,1)S(1)} %get-tuple-element.17._.w_ref), custom_call_target="tpu_custom_call" | custom-call | tf_op jit(solution)/shard_map/terms_of/pallas_call | solution.py:254
  44.5 21.6 %all_to_all.15.terms_ref = bf16[8,192,384]{2,1,0:T(8,128)(2,1)S(1)} all-to-all(bf16[8,192,384]{2,1,0:T(8,128)(2,1)S(1)} %terms_of.1), channel_id=1, replica_groups=mesh['patch'=32,'tp'=8] {'tp'}, dimensions={0} | all-to-all | bytes 2359296 | tf_op jit(solution)/shard_map/all_to_all | solution.py:381
  66.2 0.2 mix.1
  66.4 19.3 %all_to_all.16.pieces_ref = bf16[8,192,384]{2,1,0:T(8,128)(2,1)S(1)} all-to-all(bf16[8,192,384]{2,1,0:T(8,128)(2,1)S(1)} %mix.1), channel_id=1, replica_groups=mesh['patch'=32,'tp'=8] {'tp'}, dimensions={0} | all-to-all | bytes 2359296 | tf_op jit(solution)/shard_map/all_to_all | solution.py:383
  85.7 1.1 %join.1 = bf16[192,3072]{1,0:T(8,128)(2,1)} custom-call(bf16[8,192,384]{2,1,0:T(8,128)(2,1)S(1)} %all_to_all.16.pieces_ref), custom_call_target="tpu_custom_call" | custom-call | tf_op jit(solution)/shard_map/join/pallas_call | solution.py:329
  (23 shorter events, 0.1 us)
Async XLA Ops:
  0.6 7.9 %copy-start = (bf16[192,3072]{1,0:T(8,128)(2,1)S(1)}, bf16[192,3072]{1,0:T(8,128)(2,1)}, u32[]{:S(2)}) copy-start(bf16[192,3072]{1,0:T(8,128)(2,1)} %image_ref.3) | copy-start | bytes 3538948
  0.6 7.9 %copy-start.2 = (f32[3072]{0:T(1024)S(1)}, f32[3072]{0:T(1024)}, u32[]{:S(2)}) copy-start(f32[3072]{0:T(1024)} %shift_ref.1) | copy-start | bytes 36868
  0.7 7.9 %copy-start.3 = (f32[3072]{0:T(1024)S(1)}, f32[3072]{0:T(1024)}, u32[]{:S(2)}) copy-start(f32[3072]{0:T(1024)} %scale_ref.1) | copy-start | bytes 36868
  2.6 27.1 %all-to-all-start = ((bf16[8,2,192,128]{3,2,1,0:T(8,128)(2,1)}), bf16[8,2,192,128]{3,2,1,0:T(8,128)(2,1)S(1)}, u32[]{:S(2)}, u32[]{:S(2)}) async-start(bf16[8,2,192,128]{3,2,1,0:T(8,128)(2,1)} %copies_of.1._), calls=%async_computation | async-start | bytes 1572864 | tf_op jit(solution)/shard_map/all_to_all | solution.py:365
  11.4 1.1 %copy-start.6 = (f32[3,256]{1,0:T(4,128)S(1)}, f32[3,256]{1,0:T(4,128)}, u32[]{:S(2)}) copy-start(f32[3,256]{1,0:T(4,128)} %bias_ref.1) | copy-start | bytes 9220
  11.4 1.1 %copy-start.7 = (f32[128]{0:T(128)S(1)}, f32[128]{0:T(128)}, u32[]{:S(2)}) copy-start(f32[128]{0:T(128)} %param.18) | copy-start | bytes 1540
  11.4 1.1 %copy-start.8 = (f32[128]{0:T(128)S(1)}, f32[128]{0:T(128)}, u32[]{:S(2)}) copy-start(f32[128]{0:T(128)} %param.19) | copy-start | bytes 1540
  13.9 1.4 %collective-permute-start = (bf16[3,192,128]{2,1,0:T(8,128)(2,1)S(1)}, bf16[3,192,128]{2,1,0:T(8,128)(2,1)S(1)}, u32[]{:S(2)}, u32[]{:S(2)}) collective-permute-start(bf16[3,192,128]{2,1,0:T(8,128)(2,1)S(1)} %get-tuple-element.16), channel_id=1, source_target_pairs={{0,8},{8,0},{16,24},{24,16},{32,40},{40,32},{48,56},{56,48},{64,72... | collective-permute-start | bytes 442376 | tf_op jit(solution)/shard_map/ppermute | solution.py:361
  15.3 14.4 %collective-permute-start.5 = (bf16[384,128]{1,0:T(8,128)(2,1)S(1)}, bf16[384,128]{1,0:T(8,128)(2,1)S(1)}, u32[]{:S(2)}, u32[]{:S(2)}) collective-permute-start(bf16[384,128]{1,0:T(8,128)(2,1)S(1)} %pad_maximum_fusion.q_ref), channel_id=1, source_target_pairs={{0,112},{8,120},{16,96},{24,104},{32,80},{40,88},{48,64},{56,72},{... | collective-permute-start | bytes 294920 | tf_op jit(solution)/shard_map/ppermute | solution.py:361
  20.4 10.3 %collective-permute-start.3 = (bf16[384,128]{1,0:T(8,128)(2,1)S(1)}, bf16[384,128]{1,0:T(8,128)(2,1)S(1)}, u32[]{:S(2)}, u32[]{:S(2)}) collective-permute-start(bf16[384,128]{1,0:T(8,128)(2,1)S(1)} %pad_maximum_fusion.q_ref), channel_id=1, source_target_pairs={{0,48},{8,56},{16,32},{24,40},{32,16},{40,24},{48,0},{56,8},{64,11... | collective-permute-start | bytes 294920 | tf_op jit(solution)/shard_map/ppermute | solution.py:361
  22.3 10.4 %collective-permute-start.1 = (bf16[384,128]{1,0:T(8,128)(2,1)S(1)}, bf16[384,128]{1,0:T(8,128)(2,1)S(1)}, u32[]{:S(2)}, u32[]{:S(2)}) collective-permute-start(bf16[384,128]{1,0:T(8,128)(2,1)S(1)} %pad_maximum_fusion.q_ref), channel_id=1, source_target_pairs={{0,80},{8,88},{16,64},{24,72},{32,112},{40,120},{48,96},{56,104},{... | collective-permute-start | bytes 294920 | tf_op jit(solution)/shard_map/ppermute | solution.py:361
  30.6 6.0 %copy-start.1 = (bf16[2,512,256]{2,1,0:T(8,128)(2,1)S(1)}, bf16[2,512,256]{2,1,0:T(8,128)(2,1)}, u32[]{:S(2)}) copy-start(bf16[2,512,256]{2,1,0:T(8,128)(2,1)} %text_ref.1) | copy-start | bytes 1572868
  30.6 9.5 %collective-permute-start.6 = (bf16[400,128]{1,0:T(8,128)(2,1)S(1)}, bf16[400,128]{1,0:T(8,128)(2,1)S(1)}, u32[]{:S(2)}, u32[]{:S(2)}) collective-permute-start(bf16[400,128]{1,0:T(8,128)(2,1)S(1)} %attend_remote.5), channel_id=1, source_target_pairs={{0,112},{8,120},{16,96},{24,104},{32,80},{40,88},{48,64},{56,72},{... | collective-permute-start | bytes 307208 | tf_op jit(solution)/shard_map/ppermute | solution.py:361
  31.7 8.5 %collective-permute-start.4 = (bf16[400,128]{1,0:T(8,128)(2,1)S(1)}, bf16[400,128]{1,0:T(8,128)(2,1)S(1)}, u32[]{:S(2)}, u32[]{:S(2)}) collective-permute-start(bf16[400,128]{1,0:T(8,128)(2,1)S(1)} %attend_remote.4), channel_id=1, source_target_pairs={{0,48},{8,56},{16,32},{24,40},{32,16},{40,24},{48,0},{56,8},{64,11... | collective-permute-start | bytes 307208 | tf_op jit(solution)/shard_map/ppermute | solution.py:361
  33.6 5.1 %copy-start.4 = (f32[3072]{0:T(1024)S(1)}, f32[3072]{0:T(1024)}, u32[]{:S(2)}) copy-start(f32[3072]{0:T(1024)} %param.15) | copy-start | bytes 36868
  33.6 5.1 %copy-start.5 = (f32[3072]{0:T(1024)S(1)}, f32[3072]{0:T(1024)}, u32[]{:S(2)}) copy-start(f32[3072]{0:T(1024)} %param.23) | copy-start | bytes 36868
  33.6 8.4 %collective-permute-start.2 = (bf16[400,128]{1,0:T(8,128)(2,1)S(1)}, bf16[400,128]{1,0:T(8,128)(2,1)S(1)}, u32[]{:S(2)}, u32[]{:S(2)}) collective-permute-start(bf16[400,128]{1,0:T(8,128)(2,1)S(1)} %attend_remote.3), channel_id=1, source_target_pairs={{0,80},{8,88},{16,64},{24,72},{32,112},{40,120},{48,96},{56,104},{... | collective-permute-start | bytes 307208 | tf_op jit(solution)/shard_map/ppermute | solution.py:361
  42.1 1.3 %collective-permute-start.7 = (bf16[192,128]{1,0:T(8,128)(2,1)S(1)}, bf16[192,128]{1,0:T(8,128)(2,1)S(1)}, u32[]{:S(2)}, u32[]{:S(2)}) collective-permute-start(bf16[192,128]{1,0:T(8,128)(2,1)S(1)} %get-tuple-element.19), channel_id=1, source_target_pairs={{0,8},{8,0},{16,24},{24,16},{32,40},{40,32},{48,56},{56,48},{64,72... | collective-permute-start | bytes 147464 | tf_op jit(solution)/shard_map/ppermute | solution.py:361
